TPU v7x, 32 devices: a whole 2x2x4 slice. The times are simulated.
32 devices in a mesh: die: 2 (over x), ty: 4 (over z), tx: 4 (over y, core).
Axes of the slice: x: 2, y: 2, z: 4, core: 2. Of those that a mesh axis runs over, the one named last changes fastest.
Arguments:
- raster: float32 [2, 1024, 4096], P('die', 'ty', 'tx'), may hold values from -12 to 12
- shift_pick: int32 [2, 4, 4], P('die', 'ty', 'tx'), may hold values from 0 to 7
- offsets: int32 [2, 4, 4, 2], P('die', 'ty', 'tx'), may hold values from -5 to 4
Outputs:
- next_map: float32 [2, 1024, 4096], P('die', 'ty', 'tx')
- prev_map: float32 [2, 1024, 4096], P('die', 'ty', 'tx')
All inputs are finite; a program needn't handle non-finite values.
Results may differ from a plain program's by a relative error of at most 0.0003.
Values sent between devices are 32-bit elements; how exact they have to be, the bound alone decides.
No kernel may reach another device: no remote copies, remote signals or barrier semaphores. Data moves between devices by JAX's collectives and lax.ppermute only.
A program may use at most 64 MiB of HBM per device.

v0:
```python
import jax
import jax.numpy as jnp
from jax import lax
from jax.sharding import PartitionSpec as P

TH = 256
TW = 1024
R = 4
RG = 6
HW = 11


def extended(block, sides, width):
    for axis, dim in sides:
        count = lax.axis_size(axis)
        forward = [(i, i + 1) for i in range(count - 1)]
        backward = [(target, source) for source, target in forward]
        low = lax.ppermute(
            lax.slice_in_dim(block, block.shape[dim] - width, None, axis=dim), axis, forward
        )
        high = lax.ppermute(lax.slice_in_dim(block, 0, width, axis=dim), axis, backward)
        block = jnp.concatenate([low, block, high], axis=dim)
    return block


def shifted(block, axis, distance):
    devices = range(lax.axis_size(axis))
    route = [(i - distance, i) for i in devices if i - distance in devices]
    return lax.ppermute(block, axis, route)


def gauss_taps(sigma):
    spots = jnp.arange(-RG, RG + 1).astype(jnp.float32)
    raw = jnp.exp(-spots * spots / (2.0 * sigma * sigma))
    return raw / jnp.sum(raw)


def blur_tile(image, sigma):
    taps = gauss_taps(sigma)
    column_sum = taps[0] * image[0:TH, :]
    for shift in range(1, 2 * RG + 1):
        column_sum = column_sum + taps[shift] * image[shift : shift + TH, :]
    total = taps[0] * column_sum[:, 0:TW]
    for shift in range(1, 2 * RG + 1):
        total = total + taps[shift] * column_sum[:, shift : shift + TW]
    return total


def tile_dog(block, row_off, col_off, pick):
    row_start = row_off + R + 1
    col_start = col_off + R + 1
    window = lax.dynamic_slice(block, (row_start, col_start), (TH + 2 * RG + 1, TW + 2 * RG + 1))
    frac_y = (pick % 4).astype(jnp.float32) * 0.25 + 0.125
    frac_x = (pick // 4).astype(jnp.float32) * 0.5 + 0.25
    upper = (1.0 - frac_x) * window[:-1, :-1] + frac_x * window[:-1, 1:]
    lower = (1.0 - frac_x) * window[1:, :-1] + frac_x * window[1:, 1:]
    aligned = (1.0 - frac_y) * upper + frac_y * lower
    return blur_tile(aligned, 1.0) - blur_tile(aligned, 2.0)


def body(raster, shift_pick, offsets):
    tile = raster[0]
    block = extended(tile, (("ty", 0), ("tx", 1)), HW)
    dog = tile_dog(block, offsets[0, 0, 0, 0], offsets[0, 0, 0, 1], shift_pick[0, 0, 0])
    position = lax.axis_index("die")
    last_die = lax.axis_size("die") - 1
    following = shifted(dog, "die", -1)
    next_map = jnp.where(position < last_die, following - dog, jnp.zeros_like(dog))
    prev_map = shifted(next_map, "die", 1)
    return (next_map[None], prev_map[None])


def solution(mesh):
    in_specs = (P("die", "ty", "tx"), P("die", "ty", "tx"), P("die", "ty", "tx", None))
    out_specs = (P("die", "ty", "tx"), P("die", "ty", "tx"))
    return jax.shard_map(body, mesh=mesh, in_specs=in_specs, out_specs=out_specs, check_vma=False)
```

profile of v0, /device:TPU:14, one launch (start us, length us, event | category | flops | bytes accessed | tf_op | source)
XLA Modules:
  0.0 116.9 jit_solution(1284173473346068436)
XLA Ops:
  0.6 0.9 slice_bitcast_fusion.1
  1.5 3.5 %collective-permute-start = (f32[11,1024]{1,0:T(8,128)S(1)}, f32[11,1024]{1,0:T(8,128)S(1)}, u32[]{:S(2)}, u32[]{:S(2)}) collective-permute-start(f32[11,1024]{1,0:T(8,128)S(1)} %get-tuple-element.4), channel_id=1, source_target_pairs={{0,4},{4,8},{8,12},{1,5},{5,9},{9,13},{2,6},{6,10},{10,14},{3,7},{... | collective-permute-start | bytes 135176 | tf_op jit(solution)/shard_map/ppermute | solution.py:18
  5.0 2.4 %collective-permute-start.1 = (f32[11,1024]{1,0:T(8,128)S(1)}, f32[11,1024]{1,0:T(8,128)S(1)}, u32[]{:S(2)}, u32[]{:S(2)}) collective-permute-start(f32[11,1024]{1,0:T(8,128)S(1)} %get-tuple-element.5), channel_id=1, source_target_pairs={{4,0},{8,4},{12,8},{5,1},{9,5},{13,9},{6,2},{10,6},{14,10},{7,3},{... | collective-permute-start | bytes 135176 | tf_op jit(solution)/shard_map/ppermute | solution.py:21
  7.4 0.6 fusion.30
  8.0 0.6 fusion.31
  8.6 0.7 broadcast_divide_fusion.1
  9.3 0.7 fusion.33
  10.0 0.7 broadcast_divide_fusion
  10.6 0.7 fusion.34
  11.3 0.0 collective-permute-done
  11.3 0.0 collective-permute-done.1
  11.3 0.0 copy-start.1
  11.4 1.3 %pad_maximum_fusion = f32[278,1024]{1,0:T(8,128)S(1)} fusion(f32[11,1024]{1,0:T(8,128)S(1)} %collective-permute-done.1, f32[256,1024]{1,0:T(8,128)} %bitcast.42, f32[11,1024]{1,0:T(8,128)S(1)} %collective-permute-done), kind=kLoop, calls=%fused_computation.11 | loop fusion | flops 569344 | bytes 2277376 | tf_op jit(solution)/shard_map/concatenate | solution.py:22
  12.7 0.1 fusion.32
  12.8 1.9 %collective-permute-start.2 = (f32[278,11]{1,0:T(8,128)S(1)}, f32[278,11]{1,0:T(8,128)S(1)}, u32[]{:S(2)}, u32[]{:S(2)}) collective-permute-start(f32[278,11]{1,0:T(8,128)S(1)} %get-tuple-element.3), channel_id=1, source_target_pairs={{0,1},{1,2},{2,3},{4,5},{5,6},{6,7},{8,9},{9,10},{10,11},{12,13},{... | collective-permute-start | bytes 36704 | tf_op jit(solution)/shard_map/ppermute | solution.py:18
  14.7 3.6 %collective-permute-start.3 = (f32[278,11]{1,0:T(8,128)S(1)}, f32[278,11]{1,0:T(8,128)S(1)}, u32[]{:S(2)}, u32[]{:S(2)}) collective-permute-start(f32[278,11]{1,0:T(8,128)S(1)} %get-tuple-element.2), channel_id=1, source_target_pairs={{1,0},{2,1},{3,2},{5,4},{6,5},{7,6},{9,8},{10,9},{11,10},{13,12},{... | collective-permute-start | bytes 36704 | tf_op jit(solution)/shard_map/ppermute | solution.py:21
  18.4 0.0 copy-done.1
  18.4 0.6 fusion.35
  22.3 0.0 collective-permute-done.2
  22.3 0.0 collective-permute-done.3
  22.3 1.0 concatenate.7
  23.3 1.4 %fusion.2 = f32[268,1036]{1,0:T(8,128)S(1)} fusion(f32[278,1046]{1,0:T(8,128)S(1)} %concatenate.7, s32[]{:T(128)S(6)} %add.272, s32[]{:T(128)S(6)} %add.271, s32[]{:T(128)S(6)} %select_n.29, s32[]{:T(128)S(6)} %select_n.28, f32[]{:T(128)S(6)} %add.210, f32[]{:T(128)S(6)} %add.211, f32[]{:T(128)S(6)} %sub.19, f32[]{:T(128)S(6)} %sub.17), kind=kLoop, calls=%fused_computation.3 | loop fusion | flops 2498832 | bytes 5552992 | tf_op jit(solution)/shard_map/add | solution.py:57
  24.7 9.7 %multiply_add_fusion.1 = f32[256,1036]{1,0:T(8,128)S(1)} fusion(f32[268,1036]{1,0:T(8,128)S(1)} %fusion.2, f32[]{:T(128)} %bitcast.20, f32[]{:T(128)} %bitcast.19, f32[]{:T(128)} %bitcast.18, f32[]{:T(128)} %bitcast.17, f32[]{:T(128)} %bitcast.16, f32[]{:T(128)} %bitcast.15, f32[]{:T(128)} %bitcast.14, f32[]{:T(128)} %bitcast.13, f32[]{:T(128)} %bitcast.12, ...), kind=kLoop, calls=%fused_computation.10 | loop fusion | flops 6630400 | bytes 14852148 | tf_op jit(solution)/shard_map/add | solution.py:42
  34.4 9.6 %multiply_add_fusion = f32[256,1036]{1,0:T(8,128)S(1)} fusion(f32[268,1036]{1,0:T(8,128)S(1)} %fusion.2, f32[]{:T(128)} %bitcast.33, f32[]{:T(128)} %bitcast.32, f32[]{:T(128)} %bitcast.31, f32[]{:T(128)} %bitcast.30, f32[]{:T(128)} %bitcast.29, f32[]{:T(128)} %bitcast.28, f32[]{:T(128)} %bitcast.27, f32[]{:T(128)} %bitcast.26, f32[]{:T(128)} %bitcast.25, ...), kind=kLoop, calls=%fused_computation.9 | loop fusion | flops 6630400 | bytes 14852148 | tf_op jit(solution)/shard_map/add | solution.py:42
  44.0 22.9 %fusion.6 = f32[256,1024]{1,0:T(8,128)S(1)} fusion(f32[256,1036]{1,0:T(8,128)S(1)} %multiply_add_fusion, f32[256,1036]{1,0:T(8,128)S(1)} %multiply_add_fusion.1, f32[]{:T(128)} %bitcast.33, f32[]{:T(128)} %bitcast.32, f32[]{:T(128)} %bitcast.31, f32[]{:T(128)} %bitcast.30, f32[]{:T(128)} %bitcast.29, f32[]{:T(128)} %bitcast.28, f32[]{:T(128)} %bitcast.27, ...), kind=kLoop, calls=%fused_computation.14 | loop fusion | flops 13369344 | bytes 28311656 | tf_op jit(solution)/shard_map/sub | solution.py:58
  66.9 2.5 %collective-permute-start.4 = (f32[256,1024]{1,0:T(8,128)S(1)}, f32[256,1024]{1,0:T(8,128)S(1)}, u32[]{:S(2)}, u32[]{:S(2)}) collective-permute-start(f32[256,1024]{1,0:T(8,128)S(1)} %fusion.6), channel_id=1, source_target_pairs={{16,0},{17,1},{18,2},{19,3},{20,4},{21,5},{22,6},{23,7},{24,8},{25... | collective-permute-start | bytes 3145736 | tf_op jit(solution)/shard_map/ppermute | solution.py:29
  69.4 21.3 %collective-permute-done.4 = f32[256,1024]{1,0:T(8,128)S(1)} collective-permute-done((f32[256,1024]{1,0:T(8,128)S(1)}, f32[256,1024]{1,0:T(8,128)S(1)}, u32[]{:S(2)}, u32[]{:S(2)}) %collective-permute-start.4) | collective-permute-done | bytes 1048608 | tf_op jit(solution)/shard_map/ppermute | solution.py:29
  90.7 0.2 subtract_select_fusion
  90.9 0.0 copy-start
  91.0 1.3 %collective-permute-start.5 = (f32[256,1024]{1,0:T(8,128)S(1)}, f32[256,1024]{1,0:T(8,128)S(1)}, u32[]{:S(2)}, u32[]{:S(2)}) collective-permute-start(f32[256,1024]{1,0:T(8,128)S(1)} %subtract_select_fusion), channel_id=1, source_target_pairs={{0,16},{1,17},{2,18},{3,19},{4,20},{5,21},{6,22},{7,23},{8,24},{9,... | collective-permute-start | bytes 3145736 | tf_op jit(solution)/shard_map/ppermute | solution.py:29
  92.3 23.7 %collective-permute-done.5 = f32[256,1024]{1,0:T(8,128)S(1)} collective-permute-done((f32[256,1024]{1,0:T(8,128)S(1)}, f32[256,1024]{1,0:T(8,128)S(1)}, u32[]{:S(2)}, u32[]{:S(2)}) %collective-permute-start.5) | collective-permute-done | bytes 1048608 | tf_op jit(solution)/shard_map/ppermute | solution.py:29
  115.9 1.0 copy.7
  116.9 0.0 copy-done
Async XLA Ops:
  1.5 9.8 %collective-permute-start = (f32[11,1024]{1,0:T(8,128)S(1)}, f32[11,1024]{1,0:T(8,128)S(1)}, u32[]{:S(2)}, u32[]{:S(2)}) collective-permute-start(f32[11,1024]{1,0:T(8,128)S(1)} %get-tuple-element.4), channel_id=1, source_target_pairs={{0,4},{4,8},{8,12},{1,5},{5,9},{9,13},{2,6},{6,10},{10,14},{3,7},{... | collective-permute-start | bytes 135176 | tf_op jit(solution)/shard_map/ppermute | solution.py:18
  5.0 6.3 %collective-permute-start.1 = (f32[11,1024]{1,0:T(8,128)S(1)}, f32[11,1024]{1,0:T(8,128)S(1)}, u32[]{:S(2)}, u32[]{:S(2)}) collective-permute-start(f32[11,1024]{1,0:T(8,128)S(1)} %get-tuple-element.5), channel_id=1, source_target_pairs={{4,0},{8,4},{12,8},{5,1},{9,5},{13,9},{6,2},{10,6},{14,10},{7,3},{... | collective-permute-start | bytes 135176 | tf_op jit(solution)/shard_map/ppermute | solution.py:21
  11.3 7.0 %copy-start.1 = (s32[1,1,1,2]{3,2,1,0:T(1,128)S(1)}, s32[1,1,1,2]{3,2,1,0:T(1,128)}, u32[]{:S(2)}) copy-start(s32[1,1,1,2]{3,2,1,0:T(1,128)} %param.5) | copy-start | bytes 28
  12.8 9.5 %collective-permute-start.2 = (f32[278,11]{1,0:T(8,128)S(1)}, f32[278,11]{1,0:T(8,128)S(1)}, u32[]{:S(2)}, u32[]{:S(2)}) collective-permute-start(f32[278,11]{1,0:T(8,128)S(1)} %get-tuple-element.3), channel_id=1, source_target_pairs={{0,1},{1,2},{2,3},{4,5},{5,6},{6,7},{8,9},{9,10},{10,11},{12,13},{... | collective-permute-start | bytes 36704 | tf_op jit(solution)/shard_map/ppermute | solution.py:18
  14.7 7.5 %collective-permute-start.3 = (f32[278,11]{1,0:T(8,128)S(1)}, f32[278,11]{1,0:T(8,128)S(1)}, u32[]{:S(2)}, u32[]{:S(2)}) collective-permute-start(f32[278,11]{1,0:T(8,128)S(1)} %get-tuple-element.2), channel_id=1, source_target_pairs={{1,0},{2,1},{3,2},{5,4},{6,5},{7,6},{9,8},{10,9},{11,10},{13,12},{... | collective-permute-start | bytes 36704 | tf_op jit(solution)/shard_map/ppermute | solution.py:21
  66.9 23.8 %collective-permute-start.4 = (f32[256,1024]{1,0:T(8,128)S(1)}, f32[256,1024]{1,0:T(8,128)S(1)}, u32[]{:S(2)}, u32[]{:S(2)}) collective-permute-start(f32[256,1024]{1,0:T(8,128)S(1)} %fusion.6), channel_id=1, source_target_pairs={{16,0},{17,1},{18,2},{19,3},{20,4},{21,5},{22,6},{23,7},{24,8},{25... | collective-permute-start | bytes 3145736 | tf_op jit(solution)/shard_map/ppermute | solution.py:29
  90.9 26.0 %copy-start = (f32[256,1024]{1,0:T(8,128)}, f32[256,1024]{1,0:T(8,128)S(1)}, u32[]{:S(2)}) copy-start(f32[256,1024]{1,0:T(8,128)S(1)} %subtract_select_fusion) | copy-start | bytes 3145732
  91.0 25.0 %collective-permute-start.5 = (f32[256,1024]{1,0:T(8,128)S(1)}, f32[256,1024]{1,0:T(8,128)S(1)}, u32[]{:S(2)}, u32[]{:S(2)}) collective-permute-start(f32[256,1024]{1,0:T(8,128)S(1)} %subtract_select_fusion), channel_id=1, source_target_pairs={{0,16},{1,17},{2,18},{3,19},{4,20},{5,21},{6,22},{7,23},{8,24},{9,... | collective-permute-start | bytes 3145736 | tf_op jit(solution)/shard_map/ppermute | solution.py:29
where the time goes:
time: 118 us; the launch traced here: 117 us
  other arithmetic  47.7 us (40%)
  waiting for transfers between devices  45 us (38%)
  starting transfers between devices  15.2 us (13%)
  local copies, waits for them, and re-layouts  4.97 us (4%)
  between operations  4.07 us (3%)
    ppermute x2, waiting for transfers between devices, shifted(): return lax.ppermute(block, axis, route)  45 us
    sub x1, other arithmetic, tile_dog(): return blur_tile(aligned, 1.0) - blur_tile(aligned, 2.0)  22.9 us
    add x2, other arithmetic, blur_tile(): column_sum = column_sum + taps[shift] * image[shift:shift + TH, :]  19.3 us
    ppermute x2, starting transfers between devices, extended(): lax.ppermute(lax.slice_in_dim(block, 0, width, axis=dim), axis, backward)  6 us
    ppermute x2, starting transfers between devices, extended(): lax.ppermute(lax.slice_in_dim(block, block.shape[dim] - width, None, axis...  5.41 us
    ppermute x2, starting transfers between devices, shifted(): return lax.ppermute(block, axis, route)  3.8 us
  transfers between devices with their start and end apart: 6, of which 2 were waited for; matrix products, arithmetic and copies ran while one was open for 4% of the time, Pallas kernels for 0%

commit v1 on v0

v1 whole, which is shorter than its diff:
```python
import functools

import jax
import jax.numpy as jnp
import numpy as np
from jax import lax
from jax.experimental import pallas as pl
from jax.experimental.pallas import tpu as pltpu
from jax.sharding import PartitionSpec as P

TH = 256
TW = 1024
RG = 6
HW = 11
LANE = 128
FRAME = 16
STRIP = 2 * FRAME
MID = TH - 2 * FRAME
CORE = TW - 2 * LANE
WIDE = TW + LANE


def gauss_taps(sigma):
    spots = np.arange(-RG, RG + 1).astype(np.float64)
    raw = np.exp(-spots * spots / (2.0 * sigma * sigma))
    return [float(tap) for tap in np.float32(raw / raw.sum())[RG:]]


NARROW = gauss_taps(1.0)
BROAD = gauss_taps(2.0)


def split(values):
    high = values.astype(jnp.bfloat16)
    low = (values - high.astype(jnp.float32)).astype(jnp.bfloat16)
    return high, low


def bands(distance, frac):
    def look(spots):
        away = jnp.abs(spots)
        narrow = jnp.zeros(spots.shape, jnp.float32)
        broad = jnp.zeros(spots.shape, jnp.float32)
        for tap in range(RG + 1):
            here = away == tap
            narrow = jnp.where(here, NARROW[tap], narrow)
            broad = jnp.where(here, BROAD[tap], broad)
        return narrow, broad

    near = look(distance)
    far = look(distance - 1)
    return tuple((1.0 - frac) * a + frac * b for a, b in zip(near, far))


def column_weights(off_ref, pick_ref):
    frac = (pick_ref[0, 0, 0] // 4).astype(jnp.float32) * 0.5 + 0.25
    shape = (2 * LANE, LANE)
    distance = (
        lax.broadcasted_iota(jnp.int32, shape, 0)
        - lax.broadcasted_iota(jnp.int32, shape, 1)
        - (HW + off_ref[0, 0, 0, 1])
    )
    narrow, broad = bands(distance, frac)
    return split(jnp.concatenate([narrow, narrow - broad], axis=1))


def row_weights(off_ref, pick_ref, rows, depth, first):
    frac = (pick_ref[0, 0, 0] % 4).astype(jnp.float32) * 0.25 + 0.125
    shape = (rows, depth)
    distance = (
        lax.broadcasted_iota(jnp.int32, shape, 1)
        - lax.broadcasted_iota(jnp.int32, shape, 0)
        - (first + off_ref[0, 0, 0, 0])
    )
    narrow, broad = bands(distance, frac)
    return split(jnp.concatenate([narrow - broad, broad], axis=1))


def product(left, right):
    dot = functools.partial(jnp.dot, preferred_element_type=jnp.float32)
    return dot(left[0], right[0]) + (dot(left[1], right[0]) + dot(left[0], right[1]))


def core_kernel(off_ref, pick_ref, x_hbm, core_ref, first_ref, last_ref, x, xh, xl, th, tl, sem):
    halves = [pl.ds(0, LANE), pl.ds(LANE, LANE)]
    copies = [
        pltpu.make_async_copy(x_hbm.at[0, rows], x.at[rows], sem.at[k])
        for k, rows in enumerate(halves)
    ]
    for copy in copies:
        copy.start()
    column = column_weights(off_ref, pick_ref)
    row = row_weights(off_ref, pick_ref, MID, TH, FRAME)
    for half, (rows, copy) in enumerate(zip(halves, copies)):
        copy.wait()
        values = x[rows, :]
        first_ref[rows, :] = values[:, :LANE]
        last_ref[rows, :] = values[:, TW - LANE :]
        high, low = split(pltpu.roll(values, HW, 1))
        xh[rows, :] = high
        xl[rows, :] = low
        for block in range(CORE // LANE):
            window = pl.ds((block + 1) * LANE, 2 * LANE)
            summed = product((xh[rows, window], xl[rows, window]), column)
            high, low = split(summed)
            spot = pl.ds(block * LANE, LANE)
            for part in range(2):
                to = pl.ds(part * TH + half * LANE, LANE)
                th[to, spot] = high[:, part * LANE : (part + 1) * LANE]
                tl[to, spot] = low[:, part * LANE : (part + 1) * LANE]
    for block in range(CORE // (2 * LANE)):
        spot = pl.ds(block * 2 * LANE, 2 * LANE)
        core_ref[:, spot] = product(row, (th[:, spot], tl[:, spot]))


def side_kernel(off_ref, pick_ref, xl_ref, xr_ref, x_hbm, left_ref, right_ref, side_ref, head_ref, foot_ref, up_ref, down_ref, sem):
    copies = [
        pltpu.make_async_copy(x_hbm.at[0, pl.ds(0, STRIP)], head_ref.at[:, pl.ds(0, TW)], sem.at[0]),
        pltpu.make_async_copy(x_hbm.at[0, pl.ds(TH - STRIP, STRIP)], foot_ref.at[:, pl.ds(0, TW)], sem.at[1]),
        pltpu.make_async_copy(x_hbm.at[0, pl.ds(0, FRAME)], up_ref.at[:, pl.ds(0, TW)], sem.at[2]),
        pltpu.make_async_copy(x_hbm.at[0, pl.ds(TH - FRAME, FRAME)], down_ref.at[:, pl.ds(0, TW)], sem.at[3]),
    ]
    for copy in copies:
        copy.start()
    left = left_ref[...]
    right = right_ref[...]
    column = column_weights(off_ref, pick_ref)
    row = row_weights(off_ref, pick_ref, MID, TH, FRAME)
    pieces = []
    for strip in (
        jnp.concatenate([left, xl_ref[0]], axis=1),
        jnp.concatenate([xr_ref[0], right], axis=1),
    ):
        window = pltpu.roll(strip, 2 * LANE + HW, 1)[:, : 2 * LANE]
        summed = product(split(window), column)
        pieces.append(jnp.concatenate([summed[:, :LANE], summed[:, LANE:]], axis=0))
    side_ref[...] = product(row, split(jnp.concatenate(pieces, axis=1)))
    lane = lax.broadcasted_iota(jnp.int32, (TH, LANE), 1)
    edge = jnp.where(lane < LANE // 2, right, left)
    spot = pl.ds(TW, LANE)
    head_ref[:, spot] = edge[:STRIP]
    foot_ref[:, spot] = edge[TH - STRIP :]
    up_ref[:, spot] = edge[:FRAME]
    down_ref[:, spot] = edge[TH - FRAME :]
    for copy in copies:
        copy.wait()


def frame_kernel(off_ref, pick_ref, head_ref, foot_ref, top_ref, bottom_ref, frame_ref):
    column = column_weights(off_ref, pick_ref)
    depth = STRIP + FRAME
    row = row_weights(off_ref, pick_ref, FRAME, depth, FRAME)
    values = jnp.concatenate([top_ref[...], head_ref[...], foot_ref[...], bottom_ref[...]], axis=0)
    high, low = split(pltpu.roll(values, HW, 1))
    for pair in range(TW // (2 * LANE)):
        sums = []
        for block in (2 * pair, 2 * pair + 1):
            window = slice(block * LANE, (block + 2) * LANE)
            sums.append(product((high[:, window], low[:, window]), column))
        spot = pl.ds(pair * 2 * LANE, 2 * LANE)
        for end in range(2):
            rows = slice(end * depth, (end + 1) * depth)
            stacked = jnp.concatenate(
                [
                    jnp.concatenate([s[rows, :LANE] for s in sums], axis=1),
                    jnp.concatenate([s[rows, LANE:] for s in sums], axis=1),
                ],
                axis=0,
            )
            frame_ref[pl.ds(end * FRAME, FRAME), spot] = product(row, split(stacked))


SMALL = pl.BlockSpec(memory_space=pltpu.SMEM)
FAST = pl.BlockSpec(memory_space=pltpu.VMEM)
ANY = pl.BlockSpec(memory_space=pl.ANY)
LIMIT = pltpu.CompilerParams(vmem_limit_bytes=16 * 2**20)


def f32(*shape):
    return jax.ShapeDtypeStruct(shape, jnp.float32)


def core_call(offsets, pick, raster):
    wide = pltpu.VMEM((TH, TW), jnp.bfloat16)
    tall = pltpu.VMEM((2 * TH, CORE), jnp.bfloat16)
    return pl.pallas_call(
        core_kernel,
        out_shape=(f32(MID, CORE), f32(TH, LANE), f32(TH, LANE)),
        in_specs=[SMALL, SMALL, ANY],
        out_specs=(FAST, FAST, FAST),
        scratch_shapes=[
            pltpu.VMEM((TH, TW), jnp.float32), wide, wide, tall, tall, pltpu.SemaphoreType.DMA((2,)),
        ],
        compiler_params=LIMIT,
        cost_estimate=pl.CostEstimate(flops=2 * 10**9, bytes_accessed=3 * 2**20, transcendentals=0),
        name="core",
    )(offsets, pick, raster)


def side_call(offsets, pick, raster, left, right):
    ends = [
        pl.BlockSpec((1, TH, 2 * LANE), lambda step: (0, 0, 0)),
        pl.BlockSpec((1, TH, 2 * LANE), lambda step: (0, 0, TW // (2 * LANE) - 1)),
    ]
    return pl.pallas_call(
        side_kernel,
        grid=(1,),
        out_shape=(f32(MID, 2 * LANE), f32(STRIP, WIDE), f32(STRIP, WIDE), f32(FRAME, WIDE), f32(FRAME, WIDE)),
        in_specs=[SMALL, SMALL, *ends, ANY, FAST, FAST],
        out_specs=(FAST,) * 5,
        scratch_shapes=[pltpu.SemaphoreType.DMA((4,))],
        compiler_params=LIMIT,
        cost_estimate=pl.CostEstimate(flops=10**9, bytes_accessed=2**20, transcendentals=0),
        name="side",
    )(offsets, pick, raster, raster, raster, left, right)


def frame_call(offsets, pick, head, foot, top, bottom):
    return pl.pallas_call(
        frame_kernel,
        out_shape=f32(2 * FRAME, TW),
        in_specs=[SMALL, SMALL, FAST, FAST, FAST, FAST],
        out_specs=FAST,
        compiler_params=LIMIT,
        cost_estimate=pl.CostEstimate(flops=10**9, bytes_accessed=2**20, transcendentals=0),
        name="frame",
    )(offsets, pick, head, foot, top, bottom)


def change_kernel(places, count, own_ref, *refs):
    next_out, prev_out, later, earlier, sem = refs[-5:]
    others = refs[: 1 if count == 2 else 2]
    position = lax.axis_index("die")
    own = own_ref[...]
    later[...] = jnp.where(position < count - 1, others[0][...] - own, 0.0)
    earlier[...] = jnp.where(position > 0, own - others[-1][...], 0.0)
    copies = []
    for source, target in places:
        for values, out in ((later, next_out), (earlier, prev_out)):
            spot = sem.at[len(copies)]
            copies.append(pltpu.make_async_copy(values.at[source], out.at[(0, *target)], spot))
    for copy in copies:
        copy.start()
    for copy in copies:
        copy.wait()


def change_call(count, places, own, others, maps):
    out = f32(1, TH, TW)
    first = 1 + len(others)
    return pl.pallas_call(
        functools.partial(change_kernel, places, count),
        out_shape=(out, out),
        in_specs=[FAST] * first + [ANY] * len(maps),
        out_specs=(ANY, ANY),
        scratch_shapes=[
            pltpu.VMEM(own.shape, jnp.float32),
            pltpu.VMEM(own.shape, jnp.float32),
            pltpu.SemaphoreType.DMA((2 * len(places),)),
        ],
        input_output_aliases={first + k: k for k in range(len(maps))},
        compiler_params=LIMIT,
        cost_estimate=pl.CostEstimate(flops=2 * own.size, bytes_accessed=20 * own.size, transcendentals=0),
        name="change",
    )(own, *others, *maps)


ALL = pl.ds(0, MID)
ROWS = pl.ds(FRAME, MID)
CORE_PLACES = (((ALL, pl.ds(0, CORE)), (ROWS, pl.ds(LANE, CORE))),)
SIDE_PLACES = (
    ((ALL, pl.ds(0, LANE)), (ROWS, pl.ds(0, LANE))),
    ((ALL, pl.ds(LANE, LANE)), (ROWS, pl.ds(TW - LANE, LANE))),
)
FRAME_PLACES = (
    ((pl.ds(0, FRAME), pl.ds(0, TW)), (pl.ds(0, FRAME), pl.ds(0, TW))),
    ((pl.ds(FRAME, FRAME), pl.ds(0, TW)), (pl.ds(TH - FRAME, FRAME), pl.ds(0, TW))),
)


def from_before(block, axis):
    return lax.ppermute(block, axis, [(i, i + 1) for i in range(lax.axis_size(axis) - 1)])


def from_after(block, axis):
    return lax.ppermute(block, axis, [(i + 1, i) for i in range(lax.axis_size(axis) - 1)])


def other_dies(block):
    if lax.axis_size("die") == 2:
        return (lax.ppermute(block, "die", [(0, 1), (1, 0)]),)
    return (from_after(block, "die"), from_before(block, "die"))


def body(raster, shift_pick, offsets):
    count = lax.axis_size("die")
    core, first, last = core_call(offsets, shift_pick, raster)
    core_others = other_dies(core)
    left = from_before(last, "tx")
    right = from_after(first, "tx")
    side, head, foot, up, down = side_call(offsets, shift_pick, raster, left, right)
    side_others = other_dies(side)
    top = from_before(down, "ty")
    bottom = from_after(up, "ty")
    frame = frame_call(offsets, shift_pick, head, foot, top, bottom)
    frame_others = other_dies(frame)
    maps = change_call(count, CORE_PLACES, core, core_others, ())
    maps = change_call(count, SIDE_PLACES, side, side_others, maps)
    return tuple(change_call(count, FRAME_PLACES, frame, frame_others, maps))


def solution(mesh):
    in_specs = (P("die", "ty", "tx"), P("die", "ty", "tx"), P("die", "ty", "tx", None))
    out_specs = (P("die", "ty", "tx"), P("die", "ty", "tx"))
    return jax.shard_map(body, mesh=mesh, in_specs=in_specs, out_specs=out_specs, check_vma=False)
```

time: 118 us -> 36.4 us (0.31)
  the two profiles are of different devices: /device:TPU:14 before, /device:TPU:1 now
where the time goes in v1:
time: 36.4 us; the launch traced here: 36.2 us
  starting transfers between devices  13.1 us (36%)
  Pallas kernels  10.8 us (30%)
  waiting for transfers between devices  9.61 us (26%)
  between operations  1.4 us (4%)
  local copies, waits for them, and re-layouts  1.22 us (3%)
    ppermute x2, waiting for transfers between devices, from_after(): lax.ppermute(block, axis, [(i + 1, i) for i in range(lax.axis_size(axis)...  8.11 us
    ppermute x2, starting transfers between devices, from_before(): lax.ppermute(block, axis, [(i, i + 1) for i in range(lax.axis_size(axis)...  7.18 us
    pallas_call x1, Pallas kernels, core_call(): pl.pallas_call(core_kernel, out_shape=(f32(MID, CORE), f32(TH, LANE), f32...  3.65 us
    ppermute x2, starting transfers between devices, from_after(): lax.ppermute(block, axis, [(i + 1, i) for i in range(lax.axis_size(axis)...  3.21 us
    pallas_call x3, Pallas kernels, change_call(): pl.pallas_call(functools.partial(change_kernel, places, count), out_shape...  2.8 us
    ppermute x3, starting transfers between devices, other_dies(): return (lax.ppermute(block, 'die', [(0, 1), (1, 0)]),)  2.7 us
    pallas_call x1, Pallas kernels, side_call(): pl.pallas_call(side_kernel, grid=(1,), out_shape=(f32(MID, 2 * LANE), f32...  2.33 us
    pallas_call x1, Pallas kernels, frame_call(): pl.pallas_call(frame_kernel, out_shape=f32(2 * FRAME, TW), in_specs=[SMAL...  2.07 us
  transfers between devices with their start and end apart: 7, of which 3 were waited for; matrix products, arithmetic and copies ran while one was open for 0% of the time, Pallas kernels for 18%

profile of v1, /device:TPU:1, one launch (start us, length us, event | category | flops | bytes accessed | tf_op | source)
XLA Modules:
  0.0 36.2 jit_solution(16318065899280827963)
XLA Ops:
  0.6 0.0 copy-start.1
  1.3 0.0 copy-done.1
  1.3 0.0 copy-start
  1.3 1.2 %copy-done = f32[1,256,1024]{2,1,0:T(8,128)S(1)} copy-done((f32[1,256,1024]{2,1,0:T(8,128)S(1)}, f32[1,256,1024]{2,1,0:T(8,128)}, u32[]{:S(2)}) %copy-start) | copy-done | bytes 1048600
  2.5 3.7 %core.1 = (f32[224,768]{1,0:T(8,128)S(1)}, f32[256,128]{1,0:T(8,128)S(1)}, f32[256,128]{1,0:T(8,128)S(1)}) custom-call(s32[1,1,1,2]{3,2,1,0:T(1,128)S(1)} %copy-done.1, s32[1,1,1]{2,1,0:T(1,128)S(6)} %copy.13.pick_ref, f32[1,256,1024]{2,1,0:T(8,128)S(1)} %copy-done), custom_call_target="tpu_custom_call" | custom-call | flops 2000000000 | bytes 3145728 | tf_op jit(solution)/shard_map/core/pallas_call | solution.py:186
  6.2 2.1 %collective-permute-start.6 = (f32[224,768]{1,0:T(8,128)S(1)}, f32[224,768]{1,0:T(8,128)S(1)}, u32[]{:S(2)}, u32[]{:S(2)}) collective-permute-start(f32[224,768]{1,0:T(8,128)S(1)} %get-tuple-element.21.own_ref), channel_id=1, source_target_pairs={{0,16},{16,0},{1,17},{17,1},{2,18},{18,2},{3,19},{19,3},{4,20},{20... | collective-permute-start | bytes 2064392 | tf_op jit(solution)/shard_map/ppermute | solution.py:291
  8.3 4.0 %collective-permute-start = (f32[256,128]{1,0:T(8,128)S(1)}, f32[256,128]{1,0:T(8,128)S(1)}, u32[]{:S(2)}, u32[]{:S(2)}) collective-permute-start(f32[256,128]{1,0:T(8,128)S(1)} %get-tuple-element.14), channel_id=1, source_target_pairs={{0,1},{1,2},{2,3},{4,5},{5,6},{6,7},{8,9},{9,10},{10,11},{12,13},{... | collective-permute-start | bytes 393224 | tf_op jit(solution)/shard_map/ppermute | solution.py:282
  12.3 1.9 %collective-permute-start.1 = (f32[256,128]{1,0:T(8,128)S(1)}, f32[256,128]{1,0:T(8,128)S(1)}, u32[]{:S(2)}, u32[]{:S(2)}) collective-permute-start(f32[256,128]{1,0:T(8,128)S(1)} %get-tuple-element.15), channel_id=1, source_target_pairs={{1,0},{2,1},{3,2},{5,4},{6,5},{7,6},{9,8},{10,9},{11,10},{13,12},{... | collective-permute-start | bytes 393224 | tf_op jit(solution)/shard_map/ppermute | solution.py:286
  14.2 0.0 collective-permute-done.left_ref
  14.2 4.6 %collective-permute-done.1.right_ref = f32[256,128]{1,0:T(8,128)S(1)} collective-permute-done((f32[256,128]{1,0:T(8,128)S(1)}, f32[256,128]{1,0:T(8,128)S(1)}, u32[]{:S(2)}, u32[]{:S(2)}) %collective-permute-start.1) | collective-permute-done | bytes 131104 | tf_op jit(solution)/shard_map/ppermute | solution.py:286
  18.9 2.3 %side.1 = (f32[224,256]{1,0:T(8,128)S(1)}, f32[32,1152]{1,0:T(8,128)S(1)}, f32[32,1152]{1,0:T(8,128)S(1)}, f32[16,1152]{1,0:T(8,128)S(1)}, f32[16,1152]{1,0:T(8,128)S(1)}) custom-call(s32[1,1,1,2]{3,2,1,0:T(1,128)S(1)} %copy-done.1, s32[1,1,1]{2,1,0:T(1,128)S(6)} %copy.13.pick_ref, f32[1,256,1024]{2,1,0:T(8,128)S(1)} %copy-done, ...), custom_call_target="tpu_custom_call" | custom-call | flops 1000000000 | bytes 1048576 | tf_op jit(solution)/shard_map/side/pallas_call | solution.py:205
  21.2 3.2 %collective-permute-start.2 = (f32[16,1152]{1,0:T(8,128)S(1)}, f32[16,1152]{1,0:T(8,128)S(1)}, u32[]{:S(2)}, u32[]{:S(2)}) collective-permute-start(f32[16,1152]{1,0:T(8,128)S(1)} %get-tuple-element.18), channel_id=1, source_target_pairs={{0,4},{4,8},{8,12},{1,5},{5,9},{9,13},{2,6},{6,10},{10,14},{3,7},{... | collective-permute-start | bytes 221192 | tf_op jit(solution)/shard_map/ppermute | solution.py:282
  24.4 1.3 %collective-permute-start.3 = (f32[16,1152]{1,0:T(8,128)S(1)}, f32[16,1152]{1,0:T(8,128)S(1)}, u32[]{:S(2)}, u32[]{:S(2)}) collective-permute-start(f32[16,1152]{1,0:T(8,128)S(1)} %get-tuple-element.19), channel_id=1, source_target_pairs={{4,0},{8,4},{12,8},{5,1},{9,5},{13,9},{6,2},{10,6},{14,10},{7,3},{... | collective-permute-start | bytes 221192 | tf_op jit(solution)/shard_map/ppermute | solution.py:286
  25.7 0.3 collective-permute-start.5
  26.0 0.0 collective-permute-done.2.top_ref
  26.0 3.5 %collective-permute-done.3.bottom_ref = f32[16,1152]{1,0:T(8,128)S(1)} collective-permute-done((f32[16,1152]{1,0:T(8,128)S(1)}, f32[16,1152]{1,0:T(8,128)S(1)}, u32[]{:S(2)}, u32[]{:S(2)}) %collective-permute-start.3) | collective-permute-done | bytes 73760 | tf_op jit(solution)/shard_map/ppermute | solution.py:286
  29.5 2.1 %frame.1.own_ref = f32[32,1024]{1,0:T(8,128)S(1)} custom-call(s32[1,1,1,2]{3,2,1,0:T(1,128)S(1)} %copy-done.1, s32[1,1,1]{2,1,0:T(1,128)S(6)} %copy.13.pick_ref, f32[32,1152]{1,0:T(8,128)S(1)} %get-tuple-element.16.head_ref, f32[32,1152]{1,0:T(8,128)S(1)} %get-tuple-element.17.foot_ref, f32[16,1152]{1,0:T(8,128)S(1)} %collective-permute-done.2.top_ref, ...), custom_call_target="tpu_custom_call" | custom-call | flops 1000000000 | bytes 1048576 | tf_op jit(solution)/shard_map/frame/pallas_call | solution.py:219
  31.6 0.3 collective-permute-start.4
  31.9 0.0 collective-permute-done.6.refs_0_
  31.9 1.2 %change.3 = (f32[1,256,1024]{2,1,0:T(8,128)}, f32[1,256,1024]{2,1,0:T(8,128)}) custom-call(f32[224,768]{1,0:T(8,128)S(1)} %get-tuple-element.21.own_ref, f32[224,768]{1,0:T(8,128)S(1)} %collective-permute-done.6.refs_0_), custom_call_target="tpu_custom_call" | custom-call | flops 344064 | bytes 3440640 | tf_op jit(solution)/shard_map/change/pallas_call | solution.py:251
  33.1 0.0 collective-permute-done.5.refs_0_
  33.1 0.8 %change.4 = (f32[1,256,1024]{2,1,0:T(8,128)}, f32[1,256,1024]{2,1,0:T(8,128)}) custom-call(f32[224,256]{1,0:T(8,128)S(1)} %get-tuple-element.20.own_ref, f32[224,256]{1,0:T(8,128)S(1)} %collective-permute-done.5.refs_0_, f32[1,256,1024]{2,1,0:T(8,128)} %get-tuple-element.22.refs_1_, ...), custom_call_target="tpu_custom_call", output_to_operand_aliasing={{0}: (2, {}), {1}: (3, {})} | custom-call | flops 114688 | bytes 1146880 | tf_op jit(solution)/shard_map/change/pallas_call | solution.py:251
  33.9 1.5 %collective-permute-done.4.refs_0_ = f32[32,1024]{1,0:T(8,128)S(1)} collective-permute-done((f32[32,1024]{1,0:T(8,128)S(1)}, f32[32,1024]{1,0:T(8,128)S(1)}, u32[]{:S(2)}, u32[]{:S(2)}) %collective-permute-start.4) | collective-permute-done | bytes 131104 | tf_op jit(solution)/shard_map/ppermute | solution.py:291
  35.4 0.7 %change.5 = (f32[1,256,1024]{2,1,0:T(8,128)}, f32[1,256,1024]{2,1,0:T(8,128)}) custom-call(f32[32,1024]{1,0:T(8,128)S(1)} %frame.1.own_ref, f32[32,1024]{1,0:T(8,128)S(1)} %collective-permute-done.4.refs_0_, f32[1,256,1024]{2,1,0:T(8,128)} %get-tuple-element.24.refs_1_, ...), custom_call_target="tpu_custom_call", output_to_operand_aliasing={{0}: (2, {}), {1}: (3, {})} | custom-call | flops 65536 | bytes 655360 | tf_op jit(solution)/shard_map/change/pallas_call | solution.py:251
Async XLA Ops:
  0.6 0.7 %copy-start.1 = (s32[1,1,1,2]{3,2,1,0:T(1,128)S(1)}, s32[1,1,1,2]{3,2,1,0:T(1,128)}, u32[]{:S(2)}) copy-start(s32[1,1,1,2]{3,2,1,0:T(1,128)} %off_ref.5) | copy-start | bytes 28
  1.3 1.2 %copy-start = (f32[1,256,1024]{2,1,0:T(8,128)S(1)}, f32[1,256,1024]{2,1,0:T(8,128)}, u32[]{:S(2)}) copy-start(f32[1,256,1024]{2,1,0:T(8,128)} %x_hbm.3) | copy-start | bytes 3145732
  6.2 25.7 %collective-permute-start.6 = (f32[224,768]{1,0:T(8,128)S(1)}, f32[224,768]{1,0:T(8,128)S(1)}, u32[]{:S(2)}, u32[]{:S(2)}) collective-permute-start(f32[224,768]{1,0:T(8,128)S(1)} %get-tuple-element.21.own_ref), channel_id=1, source_target_pairs={{0,16},{16,0},{1,17},{17,1},{2,18},{18,2},{3,19},{19,3},{4,20},{20... | collective-permute-start | bytes 2064392 | tf_op jit(solution)/shard_map/ppermute | solution.py:291
  8.3 5.9 %collective-permute-start = (f32[256,128]{1,0:T(8,128)S(1)}, f32[256,128]{1,0:T(8,128)S(1)}, u32[]{:S(2)}, u32[]{:S(2)}) collective-permute-start(f32[256,128]{1,0:T(8,128)S(1)} %get-tuple-element.14), channel_id=1, source_target_pairs={{0,1},{1,2},{2,3},{4,5},{5,6},{6,7},{8,9},{9,10},{10,11},{12,13},{... | collective-permute-start | bytes 393224 | tf_op jit(solution)/shard_map/ppermute | solution.py:282
  12.3 6.6 %collective-permute-start.1 = (f32[256,128]{1,0:T(8,128)S(1)}, f32[256,128]{1,0:T(8,128)S(1)}, u32[]{:S(2)}, u32[]{:S(2)}) collective-permute-start(f32[256,128]{1,0:T(8,128)S(1)} %get-tuple-element.15), channel_id=1, source_target_pairs={{1,0},{2,1},{3,2},{5,4},{6,5},{7,6},{9,8},{10,9},{11,10},{13,12},{... | collective-permute-start | bytes 393224 | tf_op jit(solution)/shard_map/ppermute | solution.py:286
  21.2 4.8 %collective-permute-start.2 = (f32[16,1152]{1,0:T(8,128)S(1)}, f32[16,1152]{1,0:T(8,128)S(1)}, u32[]{:S(2)}, u32[]{:S(2)}) collective-permute-start(f32[16,1152]{1,0:T(8,128)S(1)} %get-tuple-element.18), channel_id=1, source_target_pairs={{0,4},{4,8},{8,12},{1,5},{5,9},{9,13},{2,6},{6,10},{10,14},{3,7},{... | collective-permute-start | bytes 221192 | tf_op jit(solution)/shard_map/ppermute | solution.py:282
  24.4 5.1 %collective-permute-start.3 = (f32[16,1152]{1,0:T(8,128)S(1)}, f32[16,1152]{1,0:T(8,128)S(1)}, u32[]{:S(2)}, u32[]{:S(2)}) collective-permute-start(f32[16,1152]{1,0:T(8,128)S(1)} %get-tuple-element.19), channel_id=1, source_target_pairs={{4,0},{8,4},{12,8},{5,1},{9,5},{13,9},{6,2},{10,6},{14,10},{7,3},{... | collective-permute-start | bytes 221192 | tf_op jit(solution)/shard_map/ppermute | solution.py:286
  25.7 7.4 %collective-permute-start.5 = (f32[224,256]{1,0:T(8,128)S(1)}, f32[224,256]{1,0:T(8,128)S(1)}, u32[]{:S(2)}, u32[]{:S(2)}) collective-permute-start(f32[224,256]{1,0:T(8,128)S(1)} %get-tuple-element.20.own_ref), channel_id=1, source_target_pairs={{0,16},{16,0},{1,17},{17,1},{2,18},{18,2},{3,19},{19,3},{4,20},{20... | collective-permute-start | bytes 688136 | tf_op jit(solution)/shard_map/ppermute | solution.py:291
  31.6 3.8 %collective-permute-start.4 = (f32[32,1024]{1,0:T(8,128)S(1)}, f32[32,1024]{1,0:T(8,128)S(1)}, u32[]{:S(2)}, u32[]{:S(2)}) collective-permute-start(f32[32,1024]{1,0:T(8,128)S(1)} %frame.1.own_ref), channel_id=1, source_target_pairs={{0,16},{16,0},{1,17},{17,1},{2,18},{18,2},{3,19},{19,3},{4,20},{20... | collective-permute-start | bytes 393224 | tf_op jit(solution)/shard_map/ppermute | solution.py:291

commit v2 on v0

v2 whole, which is shorter than its diff:
```python
import functools

import jax
import jax.numpy as jnp
import numpy as np
from jax import lax
from jax.experimental import pallas as pl
from jax.experimental.pallas import tpu as pltpu
from jax.sharding import PartitionSpec as P

TH = 256
TW = 1024
RG = 6
HW = 11
LANE = 128
FRAME = 16
STRIP = 2 * FRAME
CORE = TW - 2 * LANE
LEAD = 96
DEPTH = LEAD + 2 * FRAME
MID = TH - 2 * FRAME
REST = MID - LEAD
BF16 = jnp.bfloat16


def gauss_taps(sigma):
    spots = np.arange(-RG, RG + 1).astype(np.float64)
    raw = np.exp(-spots * spots / (2.0 * sigma * sigma))
    return [float(tap) for tap in np.float32(raw / raw.sum())[RG:]]


NARROW = gauss_taps(1.0)
BROAD = gauss_taps(2.0)


def split(values):
    high = values.astype(BF16)
    low = (values - high.astype(jnp.float32)).astype(BF16)
    return high, low


def bands(distance, frac):
    def look(spots):
        away = jnp.abs(spots)
        narrow = jnp.zeros(spots.shape, jnp.float32)
        broad = jnp.zeros(spots.shape, jnp.float32)
        for tap in range(RG + 1):
            here = away == tap
            narrow = jnp.where(here, NARROW[tap], narrow)
            broad = jnp.where(here, BROAD[tap], broad)
        return narrow, broad

    near = look(distance)
    far = look(distance - 1)
    return tuple((1.0 - frac) * a + frac * b for a, b in zip(near, far))


def column_weights(offset, pick):
    frac = (pick // 4).astype(jnp.float32) * 0.5 + 0.25
    shape = (2 * LANE, LANE)
    window = lax.broadcasted_iota(jnp.int32, shape, 0)
    result = lax.broadcasted_iota(jnp.int32, shape, 1)
    narrow, broad = bands(window - result - (HW + offset), frac)
    return split(jnp.concatenate([narrow, narrow - broad], axis=1))


def row_weights(offset, pick):
    frac = (pick % 4).astype(jnp.float32) * 0.25 + 0.125
    shape = (LEAD, DEPTH)
    source = lax.broadcasted_iota(jnp.int32, shape, 1)
    result = lax.broadcasted_iota(jnp.int32, shape, 0)
    narrow, broad = bands(source - result - (FRAME + offset), frac)
    return split(jnp.concatenate([narrow - broad, broad], axis=1))


def product(left, right):
    dot = functools.partial(jnp.dot, preferred_element_type=jnp.float32)
    return dot(left[0], right[0]) + (dot(left[1], right[0]) + dot(left[0], right[1]))


def column_sums(windows, column):
    rows = windows[0].shape[0]
    sums = split(product(split(jnp.concatenate(windows, axis=0)), column))
    blocks = [slice(k * rows, (k + 1) * rows) for k in range(len(windows))]
    return [
        [jnp.concatenate([half[block, part] for block in blocks], axis=1) for half in sums]
        for part in (slice(0, LANE), slice(LANE, 2 * LANE))
    ]


def row_sums(row, sums, rows):
    narrow, change = sums
    stacked = [jnp.concatenate([a[rows], b[rows]], axis=0) for a, b in zip(narrow, change)]
    return product(row, stacked)


def core_windows(values):
    rolled = pltpu.roll(values, HW, 1)
    return [rolled[:, block * LANE : (block + 2) * LANE] for block in range(1, TW // LANE - 1)]


def lead_kernel(off_hbm, pick_hbm, x_hbm, lead, first, second, wh, wl, vh, vl, x, off, pick, sem):
    odd = lax.axis_index("tx") % 2
    spots = [pl.multiple_of(LANE * (TW // LANE - 1) * side, LANE) for side in (1 - odd, odd)]
    copies = [
        pltpu.make_async_copy(off_hbm, off, sem.at[0]),
        pltpu.make_async_copy(pick_hbm, pick, sem.at[1]),
        pltpu.make_async_copy(x_hbm.at[0, pl.ds(0, DEPTH)], x, sem.at[2]),
        pltpu.make_async_copy(x_hbm.at[0, :, pl.ds(spots[0], LANE)], first, sem.at[3]),
        pltpu.make_async_copy(x_hbm.at[0, :, pl.ds(spots[1], LANE)], second, sem.at[4]),
    ]
    for copy in copies:
        copy.start()
    copies[0].wait()
    copies[1].wait()
    column = column_weights(off[0, 0, 0, 1], pick[0, 0, 0])
    row = row_weights(off[0, 0, 0, 0], pick[0, 0, 0])
    wh[...], wl[...] = column
    vh[...], vl[...] = row
    copies[2].wait()
    sums = column_sums(core_windows(x[...]), column)
    lead[...] = row_sums(row, sums, slice(0, DEPTH))
    copies[3].wait()
    copies[4].wait()


def rest_kernel(x, wh, wl, vh, vl, rest):
    column = (wh[...], wl[...])
    row = (vh[...], vl[...])
    sums = column_sums(core_windows(x[0, LEAD:, :]), column)
    rest[:LEAD, :] = row_sums(row, sums, slice(0, DEPTH))
    last = REST - LEAD
    lower = [v[LEAD - last :] for v in row]
    rest[LEAD:, :] = row_sums(lower, sums, slice(TH - LEAD - DEPTH, TH - LEAD))


def halos(axis, first, second):
    place = lax.axis_index(axis)
    inner = (place > 0) & (place < lax.axis_size(axis) - 1)
    even = place % 2 == 0
    second = jnp.where(inner, second, 0.0)
    return jnp.where(even, second, first), jnp.where(even, first, second)


def edge_block(before, after):
    lane = lax.broadcasted_iota(jnp.int32, before.shape, 1)
    return jnp.where(lane < LANE // 2, after, before)


def side_kernel(x, first, second, wh, wl, vh, vl, side, send_first, send_second):
    column = (wh[...], wl[...])
    row = (vh[...], vl[...])
    before, after = halos("tx", first[...], second[...])
    windows = [
        pltpu.roll(jnp.concatenate(strip, axis=1), 2 * LANE + HW, 1)[:, : 2 * LANE]
        for strip in ((before, x[0, :, : 2 * LANE]), (x[0, :, TW - 2 * LANE :], after))
    ]
    sums = column_sums(windows, column)
    side[:LEAD, :] = row_sums(row, sums, slice(0, DEPTH))
    side[LEAD : 2 * LEAD, :] = row_sums(row, sums, slice(LEAD, LEAD + DEPTH))
    last = MID - 2 * LEAD
    lower = [v[LEAD - last :] for v in row]
    side[2 * LEAD :, :] = row_sums(lower, sums, slice(TH - DEPTH, TH))
    edge = edge_block(before, after)
    top = jnp.concatenate([x[0, :FRAME, :], edge[:FRAME]], axis=1)
    bottom = jnp.concatenate([x[0, TH - FRAME :, :], edge[TH - FRAME :]], axis=1)
    even = lax.axis_index("ty") % 2 == 0
    send_first[...] = jnp.where(even, bottom, top)
    send_second[...] = jnp.where(even, top, bottom)


def frame_kernel(x, first, second, row_first, row_second, wh, wl, vh, vl, frame):
    column = (wh[...], wl[...])
    top, bottom = halos("ty", row_first[...], row_second[...])
    own = []
    for rows in (slice(0, STRIP), slice(TH - STRIP, TH)):
        edge = edge_block(*halos("tx", first[rows, :], second[rows, :]))
        own.append(jnp.concatenate([x[0, rows, :], edge], axis=1))
    values = jnp.concatenate([top, own[0], own[1], bottom], axis=0)
    rolled = pltpu.roll(values, HW, 1)
    windows = [rolled[:, block * LANE : (block + 2) * LANE] for block in range(TW // LANE)]
    sums = column_sums(windows, column)
    tall = values.shape[0]
    filler = jnp.zeros((DEPTH - tall, TW), BF16)
    padded = [[jnp.concatenate([half, filler], axis=0) for half in part] for part in sums]
    row = [jnp.concatenate([v[:FRAME, :], v[tall // 2 : tall // 2 + FRAME, :]], axis=0) for v in (vh, vl)]
    frame[...] = row_sums(row, padded, slice(0, DEPTH))


FAST = pl.BlockSpec(memory_space=pltpu.VMEM)
SLOW = pl.BlockSpec(memory_space=pltpu.HBM)
ANY = pl.BlockSpec(memory_space=pl.ANY)
LIMIT = pltpu.CompilerParams(vmem_limit_bytes=16 * 2**20)


def f32(*shape):
    return jax.ShapeDtypeStruct(shape, jnp.float32)


def bf16(*shape):
    return jax.ShapeDtypeStruct(shape, BF16)


def cost(flops):
    return pl.CostEstimate(flops=flops, bytes_accessed=2**12, transcendentals=0)


def lead_call(offsets, pick, raster):
    column = bf16(2 * LANE, 2 * LANE)
    row = bf16(LEAD, 2 * DEPTH)
    return pl.pallas_call(
        lead_kernel,
        out_shape=(f32(LEAD, CORE), f32(TH, LANE), f32(TH, LANE), column, column, row, row),
        in_specs=[SLOW] * 3,
        out_specs=(FAST,) * 7,
        scratch_shapes=[
            pltpu.VMEM((DEPTH, TW), jnp.float32),
            pltpu.SMEM(offsets.shape, jnp.int32),
            pltpu.SMEM(pick.shape, jnp.int32),
            pltpu.SemaphoreType.DMA((5,)),
        ],
        compiler_params=LIMIT,
        cost_estimate=cost(10**6),
        name="lead",
    )(offsets, pick, pltpu.with_memory_space_constraint(raster, pltpu.HBM))


def fast_call(kernel, name, out_shape, *operands):
    many = isinstance(out_shape, tuple)
    return pl.pallas_call(
        kernel,
        out_shape=out_shape,
        in_specs=[FAST] * len(operands),
        out_specs=(FAST,) * len(out_shape) if many else FAST,
        compiler_params=LIMIT,
        cost_estimate=cost(10**6),
        name=name,
    )(*operands)


def change_kernel(blocks, count, fill, *refs):
    width = 2 if count == 2 else 3
    pieces = [refs[k * width : (k + 1) * width] for k in range(len(blocks))]
    scratch = len(blocks) + 1 + bool(fill)
    outs = refs[-scratch - 2 : -scratch]
    values = refs[-scratch:][: len(blocks)]
    sem = refs[-1]
    position = lax.axis_index("die")
    for out, there, forward in (
        (outs[0], position < count - 1, True),
        (outs[1], position > 0, False),
    ):

        @pl.when(there)
        def _():
            copies = []
            for piece, value, places in zip(pieces, values, blocks):
                own = piece[0][...]
                value[...] = piece[1][...] - own if forward else own - piece[-1][...]
                for (row, column), (out_row, out_column), (tall, wide) in places:
                    copies.append(
                        pltpu.make_async_copy(
                            value.at[pl.ds(row, tall), pl.ds(column, wide)],
                            out.at[0, pl.ds(out_row, tall), pl.ds(out_column, wide)],
                            sem.at[len(copies)],
                        )
                    )
                    copies[-1].start()
            for copy in copies:
                copy.wait()

        if fill:

            @pl.when(jnp.logical_not(there))
            def _():
                zeros = refs[-2]
                zeros[...] = jnp.zeros_like(zeros)
                copy = pltpu.make_async_copy(zeros, out.at[0], sem.at[0])
                copy.start()
                copy.wait()


def change_call(count, blocks, pieces, maps):
    operands = [array for own, others in pieces for array in (own, *others)]
    fill = not maps
    out = f32(1, TH, TW)
    return pl.pallas_call(
        functools.partial(change_kernel, blocks, count, fill),
        out_shape=(out, out),
        in_specs=[FAST] * len(operands) + [SLOW] * len(maps),
        out_specs=(SLOW, SLOW),
        scratch_shapes=[
            *(pltpu.VMEM(own.shape, jnp.float32) for own, _ in pieces),
            *([pltpu.VMEM((TH, TW), jnp.float32)] if fill else []),
            pltpu.SemaphoreType.DMA((sum(map(len, blocks)),)),
        ],
        input_output_aliases={len(operands) + k: k for k in range(len(maps))},
        compiler_params=LIMIT,
        cost_estimate=cost(10**6),
        name="change",
    )(*operands, *maps)


CORE_PLACES = (
    (((0, 0), (FRAME, LANE), (LEAD, CORE)),),
    (((0, 0), (FRAME + LEAD, LANE), (REST, CORE)),),
)
SIDE_PLACES = ((((0, 0), (FRAME, 0), (MID, LANE)), ((0, LANE), (FRAME, TW - LANE), (MID, LANE))),)
FRAME_PLACES = ((((0, 0), (0, 0), (FRAME, TW)), ((FRAME, 0), (TH - FRAME, 0), (FRAME, TW))),)


def swap_rounds(axis, first, second):
    count = lax.axis_size(axis)
    assert count % 2 == 0
    pairs = [(i, i ^ 1) for i in range(count)]
    others = [(i, min(max((i ^ 1) + 2 * (i % 2 * 2 - 1), 0), count - 1)) for i in range(count)]
    return lax.ppermute(first, axis, pairs), lax.ppermute(second, axis, others)


def other_dies(block):
    count = lax.axis_size("die")
    forward = [(i, i + 1) for i in range(count - 1)]
    backward = [(i + 1, i) for i in range(count - 1)]
    if count == 2:
        return (lax.ppermute(block, "die", forward + backward),)
    return (lax.ppermute(block, "die", backward), lax.ppermute(block, "die", forward))


def body(raster, shift_pick, offsets):
    count = lax.axis_size("die")
    lead, first, second, *weights = lead_call(offsets, shift_pick, raster)
    lead_others = other_dies(lead)
    first, second = swap_rounds("tx", first, second)
    rest = fast_call(rest_kernel, "rest", f32(REST, CORE), raster, *weights)
    rest_others = other_dies(rest)
    halo = f32(FRAME, TW + LANE)
    side, send_first, send_second = fast_call(
        side_kernel, "side", (f32(MID, 2 * LANE), halo, halo), raster, first, second, *weights
    )
    side_others = other_dies(side)
    row_first, row_second = swap_rounds("ty", send_first, send_second)
    frame = fast_call(
        frame_kernel, "frame", f32(STRIP, TW), raster, first, second, row_first, row_second, *weights
    )
    frame_others = other_dies(frame)
    maps = change_call(count, CORE_PLACES, [(lead, lead_others), (rest, rest_others)], ())
    maps = change_call(count, SIDE_PLACES, [(side, side_others)], maps)
    return tuple(change_call(count, FRAME_PLACES, [(frame, frame_others)], maps))


def solution(mesh):
    in_specs = (P("die", "ty", "tx"), P("die", "ty", "tx"), P("die", "ty", "tx", None))
    out_specs = (P("die", "ty", "tx"), P("die", "ty", "tx"))
    return jax.shard_map(body, mesh=mesh, in_specs=in_specs, out_specs=out_specs, check_vma=False)
```

time: 118 us -> 32.7 us (0.28)
  the two profiles are of different devices: /device:TPU:14 before, /device:TPU:0 now
where the time goes in v2:
time: 32.7 us; the launch traced here: 32.5 us
  waiting for transfers between devices  13.3 us (41%)
  Pallas kernels  9.02 us (28%)
  starting transfers between devices  8.14 us (25%)
  between operations  1.44 us (4%)
  local copies, waits for them, and re-layouts  0.65 us (2%)
    ppermute x4, waiting for transfers between devices, other_dies(): return (lax.ppermute(block, 'die', forward + backward),)  10.7 us
    ppermute x4, starting transfers between devices, other_dies(): return (lax.ppermute(block, 'die', forward + backward),)  5.25 us
    pallas_call x3, Pallas kernels, fast_call(): pl.pallas_call(kernel, out_shape=out_shape, in_specs=[FAST] * len(operand...  3.55 us
    pallas_call x3, Pallas kernels, change_call(): pl.pallas_call(functools.partial(change_kernel, blocks, count, fill), out...  3.33 us
    ppermute x2, waiting for transfers between devices, swap_rounds(): lax.ppermute(first, axis, pairs)  2.63 us
    pallas_call x1, Pallas kernels, lead_call(): pl.pallas_call(lead_kernel, out_shape=(f32(LEAD, CORE), f32(TH, LANE), f3...  2.14 us
    ppermute x2, starting transfers between devices, swap_rounds(): lax.ppermute(first, axis, pairs)  1.58 us
    ppermute x2, starting transfers between devices, swap_rounds(): lax.ppermute(second, axis, others)  1.31 us
  transfers between devices with their start and end apart: 8, of which 5 were waited for; matrix products, arithmetic and copies ran while one was open for 0% of the time, Pallas kernels for 14%

profile of v2, /device:TPU:0, one launch (start us, length us, event | category | flops | bytes accessed | tf_op | source)
XLA Modules:
  0.0 32.5 jit_solution(3786568799250896818)
XLA Ops:
  0.6 0.0 copy-start
  1.4 0.0 copy-start.1
  1.4 0.6 %copy-done.1 = s32[1,1,1,2]{3,2,1,0:T(1,128)S(1)} copy-done((s32[1,1,1,2]{3,2,1,0:T(1,128)S(1)}, s32[1,1,1,2]{3,2,1,0:T(1,128)}, u32[]{:S(2)}) %copy-start.1) | copy-done | bytes 32
  2.0 2.1 %lead.1 = (f32[96,768]{1,0:T(8,128)S(1)}, f32[256,128]{1,0:T(8,128)S(1)}, f32[256,128]{1,0:T(8,128)S(1)}, bf16[256,256]{1,0:T(8,128)(2,1)S(1)}, bf16[256,256]{1,...) custom-call(s32[1,1,1,2]{3,2,1,0:T(1,128)S(1)} %copy-done.1, ...), custom_call_target="tpu_custom_call" | custom-call | flops 1000000 | bytes 4096 | tf_op jit(solution)/shard_map/lead/pallas_call | solution.py:211
  4.2 0.0 copy-done
  4.2 1.5 %rest.1.refs_2_ = f32[128,768]{1,0:T(8,128)S(1)} custom-call(f32[1,256,1024]{2,1,0:T(8,128)S(1)} %copy-done, bf16[256,256]{1,0:T(8,128)(2,1)S(1)} %get-tuple-element.18.wh, bf16[256,256]{1,0:T(8,128)(2,1)S(1)} %get-tuple-element.19.wl, bf16[96,256]{1,0:T(8,128)(2,1)S(1)} %get-tuple-element.20.vh, bf16[96,256]{1,0:T(8,128)(2,1)S(1)} %get-tuple-element.21.vl), custom_call_target="tpu_custom_call" | custom-call | flops 1000000 | bytes 4096 | tf_op jit(solution)/shard_map/rest/pallas_call | solution.py:230
  5.7 3.0 %collective-permute-start.7 = (f32[128,768]{1,0:T(8,128)S(1)}, f32[128,768]{1,0:T(8,128)S(1)}, u32[]{:S(2)}, u32[]{:S(2)}) collective-permute-start(f32[128,768]{1,0:T(8,128)S(1)} %rest.1.refs_2_), channel_id=1, source_target_pairs={{0,16},{16,0},{1,17},{17,1},{2,18},{18,2},{3,19},{19,3},{4,20},{20... | collective-permute-start | bytes 1179656 | tf_op jit(solution)/shard_map/ppermute | solution.py:325
  8.7 0.0 collective-permute-start
  8.7 0.7 %collective-permute-start.1 = (f32[256,128]{1,0:T(8,128)S(1)}, f32[256,128]{1,0:T(8,128)S(1)}, u32[]{:S(2)}, u32[]{:S(2)}) collective-permute-start(f32[256,128]{1,0:T(8,128)S(1)} %get-tuple-element.17), channel_id=1, source_target_pairs={{0,0},{1,2},{2,1},{3,3},{4,4},{5,6},{6,5},{7,7},{8,8},{9,10},{10,9... | collective-permute-start | bytes 393224 | tf_op jit(solution)/shard_map/ppermute | solution.py:317
  9.4 0.2 collective-permute-start.6
  9.5 0.5 %collective-permute-done.first = f32[256,128]{1,0:T(8,128)S(1)} collective-permute-done((f32[256,128]{1,0:T(8,128)S(1)}, f32[256,128]{1,0:T(8,128)S(1)}, u32[]{:S(2)}, u32[]{:S(2)}) %collective-permute-start) | collective-permute-done | bytes 131104 | tf_op jit(solution)/shard_map/ppermute | solution.py:317
  10.1 0.0 collective-permute-done.1.second
  10.1 1.0 %side.1 = (f32[224,256]{1,0:T(8,128)S(1)}, f32[16,1152]{1,0:T(8,128)S(1)}, f32[16,1152]{1,0:T(8,128)S(1)}) custom-call(f32[1,256,1024]{2,1,0:T(8,128)S(1)} %copy-done, f32[256,128]{1,0:T(8,128)S(1)} %collective-permute-done.first, f32[256,128]{1,0:T(8,128)S(1)} %collective-permute-done.1.second, bf16[256,256]{1,0:T(8,128)(2,1)S(1)} %get-tuple-element.18.wh, ...), custom_call_target="tpu_custom_call" | custom-call | flops 1000000 | bytes 4096 | tf_op jit(solution)/shard_map/side/pallas_call | solution.py:230
  11.0 1.4 %collective-permute-start.5 = (f32[224,256]{1,0:T(8,128)S(1)}, f32[224,256]{1,0:T(8,128)S(1)}, u32[]{:S(2)}, u32[]{:S(2)}) collective-permute-start(f32[224,256]{1,0:T(8,128)S(1)} %get-tuple-element.24.refs_0_), channel_id=1, source_target_pairs={{0,16},{16,0},{1,17},{17,1},{2,18},{18,2},{3,19},{19,3},{4,20},{20... | collective-permute-start | bytes 688136 | tf_op jit(solution)/shard_map/ppermute | solution.py:325
  12.4 1.6 %collective-permute-start.2 = (f32[16,1152]{1,0:T(8,128)S(1)}, f32[16,1152]{1,0:T(8,128)S(1)}, u32[]{:S(2)}, u32[]{:S(2)}) collective-permute-start(f32[16,1152]{1,0:T(8,128)S(1)} %get-tuple-element.22), channel_id=1, source_target_pairs={{0,4},{4,0},{8,12},{12,8},{1,5},{5,1},{9,13},{13,9},{2,6},{6,2},{1... | collective-permute-start | bytes 221192 | tf_op jit(solution)/shard_map/ppermute | solution.py:317
  14.0 0.7 %collective-permute-start.3 = (f32[16,1152]{1,0:T(8,128)S(1)}, f32[16,1152]{1,0:T(8,128)S(1)}, u32[]{:S(2)}, u32[]{:S(2)}) collective-permute-start(f32[16,1152]{1,0:T(8,128)S(1)} %get-tuple-element.23), channel_id=1, source_target_pairs={{0,0},{4,8},{8,4},{12,12},{1,1},{5,9},{9,5},{13,13},{2,2},{6,10},{... | collective-permute-start | bytes 221192 | tf_op jit(solution)/shard_map/ppermute | solution.py:317
  14.7 2.1 %collective-permute-done.2.row_first = f32[16,1152]{1,0:T(8,128)S(1)} collective-permute-done((f32[16,1152]{1,0:T(8,128)S(1)}, f32[16,1152]{1,0:T(8,128)S(1)}, u32[]{:S(2)}, u32[]{:S(2)}) %collective-permute-start.2) | collective-permute-done | bytes 73760 | tf_op jit(solution)/shard_map/ppermute | solution.py:317
  16.8 0.0 collective-permute-done.3.row_second
  16.8 1.1 %frame.1.refs_0_ = f32[32,1024]{1,0:T(8,128)S(1)} custom-call(f32[1,256,1024]{2,1,0:T(8,128)S(1)} %copy-done, f32[256,128]{1,0:T(8,128)S(1)} %collective-permute-done.first, f32[256,128]{1,0:T(8,128)S(1)} %collective-permute-done.1.second, f32[16,1152]{1,0:T(8,128)S(1)} %collective-permute-done.2.row_first, ...), custom_call_target="tpu_custom_call" | custom-call | flops 1000000 | bytes 4096 | tf_op jit(solution)/shard_map/frame/pallas_call | solution.py:230
  17.9 0.7 %collective-permute-start.4 = (f32[32,1024]{1,0:T(8,128)S(1)}, f32[32,1024]{1,0:T(8,128)S(1)}, u32[]{:S(2)}, u32[]{:S(2)}) collective-permute-start(f32[32,1024]{1,0:T(8,128)S(1)} %frame.1.refs_0_), channel_id=1, source_target_pairs={{0,16},{16,0},{1,17},{17,1},{2,18},{18,2},{3,19},{19,3},{4,20},{20... | collective-permute-start | bytes 393224 | tf_op jit(solution)/shard_map/ppermute | solution.py:325
  18.5 6.4 %collective-permute-done.6.refs_1_ = f32[96,768]{1,0:T(8,128)S(1)} collective-permute-done((f32[96,768]{1,0:T(8,128)S(1)}, f32[96,768]{1,0:T(8,128)S(1)}, u32[]{:S(2)}, u32[]{:S(2)}) %collective-permute-start.6) | collective-permute-done | bytes 294944 | tf_op jit(solution)/shard_map/ppermute | solution.py:325
  25.0 0.0 collective-permute-done.7.refs_3_
  25.0 1.9 %change.3 = (f32[1,256,1024]{2,1,0:T(8,128)}, f32[1,256,1024]{2,1,0:T(8,128)}) custom-call(f32[96,768]{1,0:T(8,128)S(1)} %get-tuple-element.25.refs_0_, f32[96,768]{1,0:T(8,128)S(1)} %collective-permute-done.6.refs_1_, f32[128,768]{1,0:T(8,128)S(1)} %rest.1.refs_2_, f32[128,768]{1,0:T(8,128)S(1)} %collective-permute-done.7.refs_3_), custom_call_target="tpu_custom_call" | custom-call | flops 1000000 | bytes 4096 | tf_op jit(solution)/shard_map/change/pallas_call | solution.py:287
  26.9 3.0 %collective-permute-done.5.refs_1_ = f32[224,256]{1,0:T(8,128)S(1)} collective-permute-done((f32[224,256]{1,0:T(8,128)S(1)}, f32[224,256]{1,0:T(8,128)S(1)}, u32[]{:S(2)}, u32[]{:S(2)}) %collective-permute-start.5) | collective-permute-done | bytes 229408 | tf_op jit(solution)/shard_map/ppermute | solution.py:325
  29.9 0.7 %change.4 = (f32[1,256,1024]{2,1,0:T(8,128)}, f32[1,256,1024]{2,1,0:T(8,128)}) custom-call(f32[224,256]{1,0:T(8,128)S(1)} %get-tuple-element.24.refs_0_, f32[224,256]{1,0:T(8,128)S(1)} %collective-permute-done.5.refs_1_, f32[1,256,1024]{2,1,0:T(8,128)} %get-tuple-element.26.refs_2_, ...), custom_call_target="tpu_custom_call", output_to_operand_aliasing={{0}: (2, {}), {1}: (3, {})} | custom-call | flops 1000000 | bytes 4096 | tf_op jit(solution)/shard_map/change/pallas_call | solution.py:287
  30.6 1.2 %collective-permute-done.4.refs_1_ = f32[32,1024]{1,0:T(8,128)S(1)} collective-permute-done((f32[32,1024]{1,0:T(8,128)S(1)}, f32[32,1024]{1,0:T(8,128)S(1)}, u32[]{:S(2)}, u32[]{:S(2)}) %collective-permute-start.4) | collective-permute-done | bytes 131104 | tf_op jit(solution)/shard_map/ppermute | solution.py:325
  31.9 0.7 %change.5 = (f32[1,256,1024]{2,1,0:T(8,128)}, f32[1,256,1024]{2,1,0:T(8,128)}) custom-call(f32[32,1024]{1,0:T(8,128)S(1)} %frame.1.refs_0_, f32[32,1024]{1,0:T(8,128)S(1)} %collective-permute-done.4.refs_1_, f32[1,256,1024]{2,1,0:T(8,128)} %get-tuple-element.28.refs_2_, ...), custom_call_target="tpu_custom_call", output_to_operand_aliasing={{0}: (2, {}), {1}: (3, {})} | custom-call | flops 1000000 | bytes 4096 | tf_op jit(solution)/shard_map/change/pallas_call | solution.py:287
Async XLA Ops:
  0.6 3.5 %copy-start = (f32[1,256,1024]{2,1,0:T(8,128)S(1)}, f32[1,256,1024]{2,1,0:T(8,128)}, u32[]{:S(2)}) copy-start(f32[1,256,1024]{2,1,0:T(8,128)} %x.5) | copy-start | bytes 3145732
  1.4 0.7 %copy-start.1 = (s32[1,1,1,2]{3,2,1,0:T(1,128)S(1)}, s32[1,1,1,2]{3,2,1,0:T(1,128)}, u32[]{:S(2)}) copy-start(s32[1,1,1,2]{3,2,1,0:T(1,128)} %off_hbm.1) | copy-start | bytes 28
  5.7 19.3 %collective-permute-start.7 = (f32[128,768]{1,0:T(8,128)S(1)}, f32[128,768]{1,0:T(8,128)S(1)}, u32[]{:S(2)}, u32[]{:S(2)}) collective-permute-start(f32[128,768]{1,0:T(8,128)S(1)} %rest.1.refs_2_), channel_id=1, source_target_pairs={{0,16},{16,0},{1,17},{17,1},{2,18},{18,2},{3,19},{19,3},{4,20},{20... | collective-permute-start | bytes 1179656 | tf_op jit(solution)/shard_map/ppermute | solution.py:325
  8.7 1.3 %collective-permute-start = (f32[256,128]{1,0:T(8,128)S(1)}, f32[256,128]{1,0:T(8,128)S(1)}, u32[]{:S(2)}, u32[]{:S(2)}) collective-permute-start(f32[256,128]{1,0:T(8,128)S(1)} %get-tuple-element.16), channel_id=1, source_target_pairs={{0,1},{1,0},{2,3},{3,2},{4,5},{5,4},{6,7},{7,6},{8,9},{9,8},{10,11... | collective-permute-start | bytes 393224 | tf_op jit(solution)/shard_map/ppermute | solution.py:317
  8.7 1.3 %collective-permute-start.1 = (f32[256,128]{1,0:T(8,128)S(1)}, f32[256,128]{1,0:T(8,128)S(1)}, u32[]{:S(2)}, u32[]{:S(2)}) collective-permute-start(f32[256,128]{1,0:T(8,128)S(1)} %get-tuple-element.17), channel_id=1, source_target_pairs={{0,0},{1,2},{2,1},{3,3},{4,4},{5,6},{6,5},{7,7},{8,8},{9,10},{10,9... | collective-permute-start | bytes 393224 | tf_op jit(solution)/shard_map/ppermute | solution.py:317
  9.4 15.6 %collective-permute-start.6 = (f32[96,768]{1,0:T(8,128)S(1)}, f32[96,768]{1,0:T(8,128)S(1)}, u32[]{:S(2)}, u32[]{:S(2)}) collective-permute-start(f32[96,768]{1,0:T(8,128)S(1)} %get-tuple-element.25.refs_0_), channel_id=1, source_target_pairs={{0,16},{16,0},{1,17},{17,1},{2,18},{18,2},{3,19},{19,3},{4,20},{20... | collective-permute-start | bytes 884744 | tf_op jit(solution)/shard_map/ppermute | solution.py:325
  11.0 18.9 %collective-permute-start.5 = (f32[224,256]{1,0:T(8,128)S(1)}, f32[224,256]{1,0:T(8,128)S(1)}, u32[]{:S(2)}, u32[]{:S(2)}) collective-permute-start(f32[224,256]{1,0:T(8,128)S(1)} %get-tuple-element.24.refs_0_), channel_id=1, source_target_pairs={{0,16},{16,0},{1,17},{17,1},{2,18},{18,2},{3,19},{19,3},{4,20},{20... | collective-permute-start | bytes 688136 | tf_op jit(solution)/shard_map/ppermute | solution.py:325
  12.4 4.4 %collective-permute-start.2 = (f32[16,1152]{1,0:T(8,128)S(1)}, f32[16,1152]{1,0:T(8,128)S(1)}, u32[]{:S(2)}, u32[]{:S(2)}) collective-permute-start(f32[16,1152]{1,0:T(8,128)S(1)} %get-tuple-element.22), channel_id=1, source_target_pairs={{0,4},{4,0},{8,12},{12,8},{1,5},{5,1},{9,13},{13,9},{2,6},{6,2},{1... | collective-permute-start | bytes 221192 | tf_op jit(solution)/shard_map/ppermute | solution.py:317
  14.0 2.8 %collective-permute-start.3 = (f32[16,1152]{1,0:T(8,128)S(1)}, f32[16,1152]{1,0:T(8,128)S(1)}, u32[]{:S(2)}, u32[]{:S(2)}) collective-permute-start(f32[16,1152]{1,0:T(8,128)S(1)} %get-tuple-element.23), channel_id=1, source_target_pairs={{0,0},{4,8},{8,4},{12,12},{1,1},{5,9},{9,5},{13,13},{2,2},{6,10},{... | collective-permute-start | bytes 221192 | tf_op jit(solution)/shard_map/ppermute | solution.py:317
  17.9 14.0 %collective-permute-start.4 = (f32[32,1024]{1,0:T(8,128)S(1)}, f32[32,1024]{1,0:T(8,128)S(1)}, u32[]{:S(2)}, u32[]{:S(2)}) collective-permute-start(f32[32,1024]{1,0:T(8,128)S(1)} %frame.1.refs_0_), channel_id=1, source_target_pairs={{0,16},{16,0},{1,17},{17,1},{2,18},{18,2},{3,19},{19,3},{4,20},{20... | collective-permute-start | bytes 393224 | tf_op jit(solution)/shard_map/ppermute | solution.py:325

commit v3 on v2

--- a/solution.py
+++ b/solution.py
@@ -16,10 +16,12 @@
 FRAME = 16
 STRIP = 2 * FRAME
 CORE = TW - 2 * LANE
-LEAD = 96
-DEPTH = LEAD + 2 * FRAME
+SPAN = 96
+DEPTH = SPAN + 2 * FRAME
 MID = TH - 2 * FRAME
+LEAD = 80
 REST = MID - LEAD
+REACH = LANE + 2 * FRAME
 BF16 = jnp.bfloat16
 
 
@@ -57,16 +59,18 @@
 
 def column_weights(offset, pick):
     frac = (pick // 4).astype(jnp.float32) * 0.5 + 0.25
-    shape = (2 * LANE, LANE)
+    shape = (REACH, LANE)
     window = lax.broadcasted_iota(jnp.int32, shape, 0)
     result = lax.broadcasted_iota(jnp.int32, shape, 1)
     narrow, broad = bands(window - result - (HW + offset), frac)
-    return split(jnp.concatenate([narrow, narrow - broad], axis=1))
+    weights = split(jnp.concatenate([narrow, narrow - broad], axis=1))
+    zeros = jnp.zeros((2 * LANE - REACH, 2 * LANE), BF16)
+    return tuple(jnp.concatenate([half, zeros], axis=0) for half in weights)
 
 
 def row_weights(offset, pick):
     frac = (pick % 4).astype(jnp.float32) * 0.25 + 0.125
-    shape = (LEAD, DEPTH)
+    shape = (SPAN, DEPTH)
     source = lax.broadcasted_iota(jnp.int32, shape, 1)
     result = lax.broadcasted_iota(jnp.int32, shape, 0)
     narrow, broad = bands(source - result - (FRAME + offset), frac)
@@ -88,9 +92,12 @@
     ]
 
 
-def row_sums(row, sums, rows):
+def row_sums(row, sums, first=0):
     narrow, change = sums
-    stacked = [jnp.concatenate([a[rows], b[rows]], axis=0) for a, b in zip(narrow, change)]
+    short = DEPTH - (narrow[0].shape[0] - first)
+    filler = [jnp.zeros((short, narrow[0].shape[1]), BF16)] if short > 0 else []
+    rows = slice(first, first + DEPTH)
+    stacked = [jnp.concatenate([a[rows], *filler, b[rows], *filler], axis=0) for a, b in zip(narrow, change)]
     return product(row, stacked)
 
 
@@ -105,7 +112,7 @@
     copies = [
         pltpu.make_async_copy(off_hbm, off, sem.at[0]),
         pltpu.make_async_copy(pick_hbm, pick, sem.at[1]),
-        pltpu.make_async_copy(x_hbm.at[0, pl.ds(0, DEPTH)], x, sem.at[2]),
+        pltpu.make_async_copy(x_hbm.at[0, pl.ds(0, LEAD + 2 * FRAME)], x, sem.at[2]),
         pltpu.make_async_copy(x_hbm.at[0, :, pl.ds(spots[0], LANE)], first, sem.at[3]),
         pltpu.make_async_copy(x_hbm.at[0, :, pl.ds(spots[1], LANE)], second, sem.at[4]),
     ]
@@ -119,7 +126,7 @@
     vh[...], vl[...] = row
     copies[2].wait()
     sums = column_sums(core_windows(x[...]), column)
-    lead[...] = row_sums(row, sums, slice(0, DEPTH))
+    lead[...] = row_sums([half[:LEAD] for half in row], sums)
     copies[3].wait()
     copies[4].wait()
 
@@ -128,10 +135,10 @@
     column = (wh[...], wl[...])
     row = (vh[...], vl[...])
     sums = column_sums(core_windows(x[0, LEAD:, :]), column)
-    rest[:LEAD, :] = row_sums(row, sums, slice(0, DEPTH))
-    last = REST - LEAD
-    lower = [v[LEAD - last :] for v in row]
-    rest[LEAD:, :] = row_sums(lower, sums, slice(TH - LEAD - DEPTH, TH - LEAD))
+    rest[:SPAN, :] = row_sums(row, sums)
+    last = REST - SPAN
+    lower = [half[SPAN - last :] for half in row]
+    rest[SPAN:, :] = row_sums(lower, sums, TH - DEPTH - LEAD)
 
 
 def halos(axis, first, second):
@@ -156,11 +163,11 @@
         for strip in ((before, x[0, :, : 2 * LANE]), (x[0, :, TW - 2 * LANE :], after))
     ]
     sums = column_sums(windows, column)
-    side[:LEAD, :] = row_sums(row, sums, slice(0, DEPTH))
-    side[LEAD : 2 * LEAD, :] = row_sums(row, sums, slice(LEAD, LEAD + DEPTH))
-    last = MID - 2 * LEAD
-    lower = [v[LEAD - last :] for v in row]
-    side[2 * LEAD :, :] = row_sums(lower, sums, slice(TH - DEPTH, TH))
+    side[:SPAN, :] = row_sums(row, sums)
+    side[SPAN : 2 * SPAN, :] = row_sums(row, sums, SPAN)
+    last = MID - 2 * SPAN
+    lower = [half[SPAN - last :] for half in row]
+    side[2 * SPAN :, :] = row_sums(lower, sums, TH - DEPTH)
     edge = edge_block(before, after)
     top = jnp.concatenate([x[0, :FRAME, :], edge[:FRAME]], axis=1)
     bottom = jnp.concatenate([x[0, TH - FRAME :, :], edge[TH - FRAME :]], axis=1)
@@ -180,16 +187,14 @@
     rolled = pltpu.roll(values, HW, 1)
     windows = [rolled[:, block * LANE : (block + 2) * LANE] for block in range(TW // LANE)]
     sums = column_sums(windows, column)
-    tall = values.shape[0]
-    filler = jnp.zeros((DEPTH - tall, TW), BF16)
-    padded = [[jnp.concatenate([half, filler], axis=0) for half in part] for part in sums]
-    row = [jnp.concatenate([v[:FRAME, :], v[tall // 2 : tall // 2 + FRAME, :]], axis=0) for v in (vh, vl)]
-    frame[...] = row_sums(row, padded, slice(0, DEPTH))
-
-
+    below = values.shape[0] // 2
+    row = [jnp.concatenate([half[:FRAME, :], half[below : below + FRAME, :]], axis=0) for half in (vh, vl)]
+    frame[...] = row_sums(row, sums)
+
+
+CHANGE_COST = 10**10
 FAST = pl.BlockSpec(memory_space=pltpu.VMEM)
 SLOW = pl.BlockSpec(memory_space=pltpu.HBM)
-ANY = pl.BlockSpec(memory_space=pl.ANY)
 LIMIT = pltpu.CompilerParams(vmem_limit_bytes=16 * 2**20)
 
 
@@ -205,16 +210,20 @@
     return pl.CostEstimate(flops=flops, bytes_accessed=2**12, transcendentals=0)
 
 
+def keep(array):
+    return pltpu.with_memory_space_constraint(array, pltpu.HBM)
+
+
 def lead_call(offsets, pick, raster):
     column = bf16(2 * LANE, 2 * LANE)
-    row = bf16(LEAD, 2 * DEPTH)
+    row = bf16(SPAN, 2 * DEPTH)
     return pl.pallas_call(
         lead_kernel,
         out_shape=(f32(LEAD, CORE), f32(TH, LANE), f32(TH, LANE), column, column, row, row),
         in_specs=[SLOW] * 3,
         out_specs=(FAST,) * 7,
         scratch_shapes=[
-            pltpu.VMEM((DEPTH, TW), jnp.float32),
+            pltpu.VMEM((LEAD + 2 * FRAME, TW), jnp.float32),
             pltpu.SMEM(offsets.shape, jnp.int32),
             pltpu.SMEM(pick.shape, jnp.int32),
             pltpu.SemaphoreType.DMA((5,)),
@@ -222,7 +231,7 @@
         compiler_params=LIMIT,
         cost_estimate=cost(10**6),
         name="lead",
-    )(offsets, pick, pltpu.with_memory_space_constraint(raster, pltpu.HBM))
+    )(keep(offsets), pick, keep(raster))
 
 
 def fast_call(kernel, name, out_shape, *operands):
@@ -238,34 +247,30 @@
     )(*operands)
 
 
-def change_kernel(blocks, count, fill, *refs):
-    width = 2 if count == 2 else 3
-    pieces = [refs[k * width : (k + 1) * width] for k in range(len(blocks))]
-    scratch = len(blocks) + 1 + bool(fill)
-    outs = refs[-scratch - 2 : -scratch]
-    values = refs[-scratch:][: len(blocks)]
+def change_kernel(places, count, fill, own_ref, *refs):
+    others = refs[: 1 if count == 2 else 2]
+    next_out, prev_out, value = refs[-4 - fill :][:3]
     sem = refs[-1]
     position = lax.axis_index("die")
     for out, there, forward in (
-        (outs[0], position < count - 1, True),
-        (outs[1], position > 0, False),
+        (next_out, position < count - 1, True),
+        (prev_out, position > 0, False),
     ):
 
         @pl.when(there)
         def _():
-            copies = []
-            for piece, value, places in zip(pieces, values, blocks):
-                own = piece[0][...]
-                value[...] = piece[1][...] - own if forward else own - piece[-1][...]
-                for (row, column), (out_row, out_column), (tall, wide) in places:
-                    copies.append(
-                        pltpu.make_async_copy(
-                            value.at[pl.ds(row, tall), pl.ds(column, wide)],
-                            out.at[0, pl.ds(out_row, tall), pl.ds(out_column, wide)],
-                            sem.at[len(copies)],
-                        )
-                    )
-                    copies[-1].start()
+            own = own_ref[...]
+            value[...] = others[0][...] - own if forward else own - others[-1][...]
+            copies = [
+                pltpu.make_async_copy(
+                    value.at[pl.ds(row, tall), pl.ds(column, wide)],
+                    out.at[0, pl.ds(out_row, tall), pl.ds(out_column, wide)],
+                    sem.at[k],
+                )
+                for k, ((row, column), (out_row, out_column), (tall, wide)) in enumerate(places)
+            ]
+            for copy in copies:
+                copy.start()
             for copy in copies:
                 copy.wait()
 
@@ -280,33 +285,31 @@
                 copy.wait()
 
 
-def change_call(count, blocks, pieces, maps):
-    operands = [array for own, others in pieces for array in (own, *others)]
+def change_call(count, places, own, others, maps):
+    operands = (own, *others)
     fill = not maps
     out = f32(1, TH, TW)
     return pl.pallas_call(
-        functools.partial(change_kernel, blocks, count, fill),
+        functools.partial(change_kernel, places, count, fill),
         out_shape=(out, out),
         in_specs=[FAST] * len(operands) + [SLOW] * len(maps),
         out_specs=(SLOW, SLOW),
         scratch_shapes=[
-            *(pltpu.VMEM(own.shape, jnp.float32) for own, _ in pieces),
+            pltpu.VMEM(own.shape, jnp.float32),
             *([pltpu.VMEM((TH, TW), jnp.float32)] if fill else []),
-            pltpu.SemaphoreType.DMA((sum(map(len, blocks)),)),
+            pltpu.SemaphoreType.DMA((len(places),)),
         ],
         input_output_aliases={len(operands) + k: k for k in range(len(maps))},
         compiler_params=LIMIT,
-        cost_estimate=cost(10**6),
+        cost_estimate=cost(CHANGE_COST),
         name="change",
     )(*operands, *maps)
 
 
-CORE_PLACES = (
-    (((0, 0), (FRAME, LANE), (LEAD, CORE)),),
-    (((0, 0), (FRAME + LEAD, LANE), (REST, CORE)),),
-)
-SIDE_PLACES = ((((0, 0), (FRAME, 0), (MID, LANE)), ((0, LANE), (FRAME, TW - LANE), (MID, LANE))),)
-FRAME_PLACES = ((((0, 0), (0, 0), (FRAME, TW)), ((FRAME, 0), (TH - FRAME, 0), (FRAME, TW))),)
+LEAD_PLACES = (((0, 0), (FRAME, LANE), (LEAD, CORE)),)
+REST_PLACES = (((0, 0), (FRAME + LEAD, LANE), (REST, CORE)),)
+SIDE_PLACES = (((0, 0), (FRAME, 0), (MID, LANE)), ((0, LANE), (FRAME, TW - LANE), (MID, LANE)))
+FRAME_PLACES = (((0, 0), (0, 0), (FRAME, TW)), ((FRAME, 0), (TH - FRAME, 0), (FRAME, TW)))
 
 
 def swap_rounds(axis, first, second):
@@ -343,9 +346,10 @@
         frame_kernel, "frame", f32(STRIP, TW), raster, first, second, row_first, row_second, *weights
     )
     frame_others = other_dies(frame)
-    maps = change_call(count, CORE_PLACES, [(lead, lead_others), (rest, rest_others)], ())
-    maps = change_call(count, SIDE_PLACES, [(side, side_others)], maps)
-    return tuple(change_call(count, FRAME_PLACES, [(frame, frame_others)], maps))
+    maps = change_call(count, LEAD_PLACES, lead, lead_others, ())
+    maps = change_call(count, REST_PLACES, rest, rest_others, maps)
+    maps = change_call(count, SIDE_PLACES, side, side_others, maps)
+    return tuple(change_call(count, FRAME_PLACES, frame, frame_others, maps))
 
 
 def solution(mesh):

time: 32.7 us -> 35.6 us (1.089)
  the two profiles are of different devices: /device:TPU:0 before, /device:TPU:9 now
where the time goes in v3:
time: 35.6 us; the launch traced here: 35.4 us
  waiting for transfers between devices  12.5 us (35%)
  starting transfers between devices  11.9 us (33%)
  Pallas kernels  9.6 us (27%)
  between operations  1.44 us (4%)
    ppermute x4, waiting for transfers between devices, other_dies(): return (lax.ppermute(block, 'die', forward + backward),)  9.25 us
    ppermute x2, starting transfers between devices, swap_rounds(): lax.ppermute(second, axis, others)  7.34 us
    pallas_call x4, Pallas kernels, change_call(): pl.pallas_call(functools.partial(change_kernel, places, count, fill), out...  3.98 us
    pallas_call x3, Pallas kernels, fast_call(): pl.pallas_call(kernel, out_shape=out_shape, in_specs=[FAST] * len(operand...  3.57 us
    ppermute x4, starting transfers between devices, other_dies(): return (lax.ppermute(block, 'die', forward + backward),)  3.41 us
    ppermute x2, waiting for transfers between devices, swap_rounds(): lax.ppermute(second, axis, others)  3.24 us
    pallas_call x1, Pallas kernels, lead_call(): pl.pallas_call(lead_kernel, out_shape=(f32(LEAD, CORE), f32(TH, LANE), f3...  2.04 us
    ppermute x2, starting transfers between devices, swap_rounds(): lax.ppermute(first, axis, pairs)  1.14 us
  transfers between devices with their start and end apart: 8, of which 4 were waited for; matrix products, arithmetic and copies ran while one was open for 0% of the time, Pallas kernels for 19%

profile of v3, /device:TPU:9, one launch (start us, length us, event | category | flops | bytes accessed | tf_op | source)
XLA Modules:
  0.0 35.4 jit_solution(8899809346861155336)
XLA Ops:
  0.6 0.0 copy-start
  1.4 2.0 %lead.1 = (f32[80,768]{1,0:T(8,128)S(1)}, f32[256,128]{1,0:T(8,128)S(1)}, f32[256,128]{1,0:T(8,128)S(1)}, bf16[256,256]{1,0:T(8,128)(2,1)S(1)}, bf16[256,256]{1,...) custom-call(s32[1,1,1,2]{3,2,1,0:T(1,128)} %off_hbm.1, s32[1,1,1]{2,1,0:T(1,128)S(6)} %copy.17.pick_hbm, ...), custom_call_target="tpu_custom_call" | custom-call | flops 1000000 | bytes 4096 | tf_op jit(solution)/shard_map/lead/pallas_call | solution.py:220
  3.4 1.3 %collective-permute-start.7 = (f32[80,768]{1,0:T(8,128)S(1)}, f32[80,768]{1,0:T(8,128)S(1)}, u32[]{:S(2)}, u32[]{:S(2)}) collective-permute-start(f32[80,768]{1,0:T(8,128)S(1)} %get-tuple-element.27.own_ref), channel_id=1, source_target_pairs={{0,16},{16,0},{1,17},{17,1},{2,18},{18,2},{3,19},{19,3},{4,20},{20... | collective-permute-start | bytes 737288 | tf_op jit(solution)/shard_map/ppermute | solution.py:328
  4.7 1.0 %collective-permute-start = (f32[256,128]{1,0:T(8,128)S(1)}, f32[256,128]{1,0:T(8,128)S(1)}, u32[]{:S(2)}, u32[]{:S(2)}) collective-permute-start(f32[256,128]{1,0:T(8,128)S(1)} %get-tuple-element.18), channel_id=1, source_target_pairs={{0,1},{1,0},{2,3},{3,2},{4,5},{5,4},{6,7},{7,6},{8,9},{9,8},{10,11... | collective-permute-start | bytes 393224 | tf_op jit(solution)/shard_map/ppermute | solution.py:320
  5.7 3.0 %collective-permute-start.1 = (f32[256,128]{1,0:T(8,128)S(1)}, f32[256,128]{1,0:T(8,128)S(1)}, u32[]{:S(2)}, u32[]{:S(2)}) collective-permute-start(f32[256,128]{1,0:T(8,128)S(1)} %get-tuple-element.19), channel_id=1, source_target_pairs={{0,0},{1,2},{2,1},{3,3},{4,4},{5,6},{6,5},{7,7},{8,8},{9,10},{10,9... | collective-permute-start | bytes 393224 | tf_op jit(solution)/shard_map/ppermute | solution.py:320
  8.7 0.0 collective-permute-done.first
  8.7 3.2 %collective-permute-done.1.second = f32[256,128]{1,0:T(8,128)S(1)} collective-permute-done((f32[256,128]{1,0:T(8,128)S(1)}, f32[256,128]{1,0:T(8,128)S(1)}, u32[]{:S(2)}, u32[]{:S(2)}) %collective-permute-start.1) | collective-permute-done | bytes 131104 | tf_op jit(solution)/shard_map/ppermute | solution.py:320
  11.9 0.0 copy-done
  11.9 1.0 %side.1 = (f32[224,256]{1,0:T(8,128)S(1)}, f32[16,1152]{1,0:T(8,128)S(1)}, f32[16,1152]{1,0:T(8,128)S(1)}) custom-call(f32[1,256,1024]{2,1,0:T(8,128)S(1)} %copy-done, f32[256,128]{1,0:T(8,128)S(1)} %collective-permute-done.first, f32[256,128]{1,0:T(8,128)S(1)} %collective-permute-done.1.second, bf16[256,256]{1,0:T(8,128)(2,1)S(1)} %get-tuple-element.20.wh, ...), custom_call_target="tpu_custom_call" | custom-call | flops 1000000 | bytes 4096 | tf_op jit(solution)/shard_map/side/pallas_call | solution.py:239
  12.9 0.2 collective-permute-start.2
  13.1 4.3 %collective-permute-start.3 = (f32[16,1152]{1,0:T(8,128)S(1)}, f32[16,1152]{1,0:T(8,128)S(1)}, u32[]{:S(2)}, u32[]{:S(2)}) collective-permute-start(f32[16,1152]{1,0:T(8,128)S(1)} %get-tuple-element.25), channel_id=1, source_target_pairs={{0,0},{4,8},{8,4},{12,12},{1,1},{5,9},{9,5},{13,13},{2,2},{6,10},{... | collective-permute-start | bytes 221192 | tf_op jit(solution)/shard_map/ppermute | solution.py:320
  17.4 1.6 %rest.1.own_ref = f32[144,768]{1,0:T(8,128)S(1)} custom-call(f32[1,256,1024]{2,1,0:T(8,128)S(1)} %copy-done, bf16[256,256]{1,0:T(8,128)(2,1)S(1)} %get-tuple-element.20.wh, bf16[256,256]{1,0:T(8,128)(2,1)S(1)} %get-tuple-element.21.wl, bf16[96,256]{1,0:T(8,128)(2,1)S(1)} %get-tuple-element.22.vh, bf16[96,256]{1,0:T(8,128)(2,1)S(1)} %get-tuple-element.23.vl), custom_call_target="tpu_custom_call" | custom-call | flops 1000000 | bytes 4096 | tf_op jit(solution)/shard_map/rest/pallas_call | solution.py:239
  19.0 0.6 %collective-permute-start.6 = (f32[144,768]{1,0:T(8,128)S(1)}, f32[144,768]{1,0:T(8,128)S(1)}, u32[]{:S(2)}, u32[]{:S(2)}) collective-permute-start(f32[144,768]{1,0:T(8,128)S(1)} %rest.1.own_ref), channel_id=1, source_target_pairs={{0,16},{16,0},{1,17},{17,1},{2,18},{18,2},{3,19},{19,3},{4,20},{20... | collective-permute-start | bytes 1327112 | tf_op jit(solution)/shard_map/ppermute | solution.py:328
  19.6 0.9 %collective-permute-start.5 = (f32[224,256]{1,0:T(8,128)S(1)}, f32[224,256]{1,0:T(8,128)S(1)}, u32[]{:S(2)}, u32[]{:S(2)}) collective-permute-start(f32[224,256]{1,0:T(8,128)S(1)} %get-tuple-element.26.own_ref), channel_id=1, source_target_pairs={{0,16},{16,0},{1,17},{17,1},{2,18},{18,2},{3,19},{19,3},{4,20},{20... | collective-permute-start | bytes 688136 | tf_op jit(solution)/shard_map/ppermute | solution.py:328
  20.5 0.0 collective-permute-done.2.row_first
  20.5 0.0 collective-permute-done.3.row_second
  20.5 1.1 %frame.1.own_ref = f32[32,1024]{1,0:T(8,128)S(1)} custom-call(f32[1,256,1024]{2,1,0:T(8,128)S(1)} %copy-done, f32[256,128]{1,0:T(8,128)S(1)} %collective-permute-done.first, f32[256,128]{1,0:T(8,128)S(1)} %collective-permute-done.1.second, f32[16,1152]{1,0:T(8,128)S(1)} %collective-permute-done.2.row_first, ...), custom_call_target="tpu_custom_call" | custom-call | flops 1000000 | bytes 4096 | tf_op jit(solution)/shard_map/frame/pallas_call | solution.py:239
  21.6 0.6 %collective-permute-start.4 = (f32[32,1024]{1,0:T(8,128)S(1)}, f32[32,1024]{1,0:T(8,128)S(1)}, u32[]{:S(2)}, u32[]{:S(2)}) collective-permute-start(f32[32,1024]{1,0:T(8,128)S(1)} %frame.1.own_ref), channel_id=1, source_target_pairs={{0,16},{16,0},{1,17},{17,1},{2,18},{18,2},{3,19},{19,3},{4,20},{20... | collective-permute-start | bytes 393224 | tf_op jit(solution)/shard_map/ppermute | solution.py:328
  22.2 0.0 collective-permute-done.7.refs_0_
  22.2 1.8 %change.4 = (f32[1,256,1024]{2,1,0:T(8,128)}, f32[1,256,1024]{2,1,0:T(8,128)}) custom-call(f32[80,768]{1,0:T(8,128)S(1)} %get-tuple-element.27.own_ref, f32[80,768]{1,0:T(8,128)S(1)} %collective-permute-done.7.refs_0_), custom_call_target="tpu_custom_call" | custom-call | flops 10000000000 | bytes 4096 | tf_op jit(solution)/shard_map/change/pallas_call | solution.py:292
  23.9 7.1 %collective-permute-done.6.refs_0_ = f32[144,768]{1,0:T(8,128)S(1)} collective-permute-done((f32[144,768]{1,0:T(8,128)S(1)}, f32[144,768]{1,0:T(8,128)S(1)}, u32[]{:S(2)}, u32[]{:S(2)}) %collective-permute-start.6) | collective-permute-done | bytes 442400 | tf_op jit(solution)/shard_map/ppermute | solution.py:328
  31.1 0.8 %change.5 = (f32[1,256,1024]{2,1,0:T(8,128)}, f32[1,256,1024]{2,1,0:T(8,128)}) custom-call(f32[144,768]{1,0:T(8,128)S(1)} %rest.1.own_ref, f32[144,768]{1,0:T(8,128)S(1)} %collective-permute-done.6.refs_0_, f32[1,256,1024]{2,1,0:T(8,128)} %get-tuple-element.28.refs_1_, ...), custom_call_target="tpu_custom_call", output_to_operand_aliasing={{0}: (2, {}), {1}: (3, {})} | custom-call | flops 10000000000 | bytes 4096 | tf_op jit(solution)/shard_map/change/pallas_call | solution.py:292
  31.9 1.4 %collective-permute-done.5.refs_0_ = f32[224,256]{1,0:T(8,128)S(1)} collective-permute-done((f32[224,256]{1,0:T(8,128)S(1)}, f32[224,256]{1,0:T(8,128)S(1)}, u32[]{:S(2)}, u32[]{:S(2)}) %collective-permute-start.5) | collective-permute-done | bytes 229408 | tf_op jit(solution)/shard_map/ppermute | solution.py:328
  33.3 0.7 %change.6 = (f32[1,256,1024]{2,1,0:T(8,128)}, f32[1,256,1024]{2,1,0:T(8,128)}) custom-call(f32[224,256]{1,0:T(8,128)S(1)} %get-tuple-element.26.own_ref, f32[224,256]{1,0:T(8,128)S(1)} %collective-permute-done.5.refs_0_, f32[1,256,1024]{2,1,0:T(8,128)} %get-tuple-element.30.refs_1_, ...), custom_call_target="tpu_custom_call", output_to_operand_aliasing={{0}: (2, {}), {1}: (3, {})} | custom-call | flops 10000000000 | bytes 4096 | tf_op jit(solution)/shard_map/change/pallas_call | solution.py:292
  34.1 0.7 %collective-permute-done.4.refs_0_ = f32[32,1024]{1,0:T(8,128)S(1)} collective-permute-done((f32[32,1024]{1,0:T(8,128)S(1)}, f32[32,1024]{1,0:T(8,128)S(1)}, u32[]{:S(2)}, u32[]{:S(2)}) %collective-permute-start.4) | collective-permute-done | bytes 131104 | tf_op jit(solution)/shard_map/ppermute | solution.py:328
  34.7 0.7 %change.7 = (f32[1,256,1024]{2,1,0:T(8,128)}, f32[1,256,1024]{2,1,0:T(8,128)}) custom-call(f32[32,1024]{1,0:T(8,128)S(1)} %frame.1.own_ref, f32[32,1024]{1,0:T(8,128)S(1)} %collective-permute-done.4.refs_0_, f32[1,256,1024]{2,1,0:T(8,128)} %get-tuple-element.32.refs_1_, ...), custom_call_target="tpu_custom_call", output_to_operand_aliasing={{0}: (2, {}), {1}: (3, {})} | custom-call | flops 10000000000 | bytes 4096 | tf_op jit(solution)/shard_map/change/pallas_call | solution.py:292
Async XLA Ops:
  0.6 11.3 %copy-start = (f32[1,256,1024]{2,1,0:T(8,128)S(1)}, f32[1,256,1024]{2,1,0:T(8,128)}, u32[]{:S(2)}) copy-start(f32[1,256,1024]{2,1,0:T(8,128)} %x.5) | copy-start | bytes 3145732
  3.4 18.7 %collective-permute-start.7 = (f32[80,768]{1,0:T(8,128)S(1)}, f32[80,768]{1,0:T(8,128)S(1)}, u32[]{:S(2)}, u32[]{:S(2)}) collective-permute-start(f32[80,768]{1,0:T(8,128)S(1)} %get-tuple-element.27.own_ref), channel_id=1, source_target_pairs={{0,16},{16,0},{1,17},{17,1},{2,18},{18,2},{3,19},{19,3},{4,20},{20... | collective-permute-start | bytes 737288 | tf_op jit(solution)/shard_map/ppermute | solution.py:328
  4.7 4.0 %collective-permute-start = (f32[256,128]{1,0:T(8,128)S(1)}, f32[256,128]{1,0:T(8,128)S(1)}, u32[]{:S(2)}, u32[]{:S(2)}) collective-permute-start(f32[256,128]{1,0:T(8,128)S(1)} %get-tuple-element.18), channel_id=1, source_target_pairs={{0,1},{1,0},{2,3},{3,2},{4,5},{5,4},{6,7},{7,6},{8,9},{9,8},{10,11... | collective-permute-start | bytes 393224 | tf_op jit(solution)/shard_map/ppermute | solution.py:320
  5.7 6.3 %collective-permute-start.1 = (f32[256,128]{1,0:T(8,128)S(1)}, f32[256,128]{1,0:T(8,128)S(1)}, u32[]{:S(2)}, u32[]{:S(2)}) collective-permute-start(f32[256,128]{1,0:T(8,128)S(1)} %get-tuple-element.19), channel_id=1, source_target_pairs={{0,0},{1,2},{2,1},{3,3},{4,4},{5,6},{6,5},{7,7},{8,8},{9,10},{10,9... | collective-permute-start | bytes 393224 | tf_op jit(solution)/shard_map/ppermute | solution.py:320
  12.9 7.6 %collective-permute-start.2 = (f32[16,1152]{1,0:T(8,128)S(1)}, f32[16,1152]{1,0:T(8,128)S(1)}, u32[]{:S(2)}, u32[]{:S(2)}) collective-permute-start(f32[16,1152]{1,0:T(8,128)S(1)} %get-tuple-element.24), channel_id=1, source_target_pairs={{0,4},{4,0},{8,12},{12,8},{1,5},{5,1},{9,13},{13,9},{2,6},{6,2},{1... | collective-permute-start | bytes 221192 | tf_op jit(solution)/shard_map/ppermute | solution.py:320
  13.1 7.4 %collective-permute-start.3 = (f32[16,1152]{1,0:T(8,128)S(1)}, f32[16,1152]{1,0:T(8,128)S(1)}, u32[]{:S(2)}, u32[]{:S(2)}) collective-permute-start(f32[16,1152]{1,0:T(8,128)S(1)} %get-tuple-element.25), channel_id=1, source_target_pairs={{0,0},{4,8},{8,4},{12,12},{1,1},{5,9},{9,5},{13,13},{2,2},{6,10},{... | collective-permute-start | bytes 221192 | tf_op jit(solution)/shard_map/ppermute | solution.py:320
  19.0 12.1 %collective-permute-start.6 = (f32[144,768]{1,0:T(8,128)S(1)}, f32[144,768]{1,0:T(8,128)S(1)}, u32[]{:S(2)}, u32[]{:S(2)}) collective-permute-start(f32[144,768]{1,0:T(8,128)S(1)} %rest.1.own_ref), channel_id=1, source_target_pairs={{0,16},{16,0},{1,17},{17,1},{2,18},{18,2},{3,19},{19,3},{4,20},{20... | collective-permute-start | bytes 1327112 | tf_op jit(solution)/shard_map/ppermute | solution.py:328
  19.6 13.8 %collective-permute-start.5 = (f32[224,256]{1,0:T(8,128)S(1)}, f32[224,256]{1,0:T(8,128)S(1)}, u32[]{:S(2)}, u32[]{:S(2)}) collective-permute-start(f32[224,256]{1,0:T(8,128)S(1)} %get-tuple-element.26.own_ref), channel_id=1, source_target_pairs={{0,16},{16,0},{1,17},{17,1},{2,18},{18,2},{3,19},{19,3},{4,20},{20... | collective-permute-start | bytes 688136 | tf_op jit(solution)/shard_map/ppermute | solution.py:328
  21.6 13.2 %collective-permute-start.4 = (f32[32,1024]{1,0:T(8,128)S(1)}, f32[32,1024]{1,0:T(8,128)S(1)}, u32[]{:S(2)}, u32[]{:S(2)}) collective-permute-start(f32[32,1024]{1,0:T(8,128)S(1)} %frame.1.own_ref), channel_id=1, source_target_pairs={{0,16},{16,0},{1,17},{17,1},{2,18},{18,2},{3,19},{19,3},{4,20},{20... | collective-permute-start | bytes 393224 | tf_op jit(solution)/shard_map/ppermute | solution.py:328

commit v4 on v3

--- a/solution.py
+++ b/solution.py
@@ -19,7 +19,7 @@
 SPAN = 96
 DEPTH = SPAN + 2 * FRAME
 MID = TH - 2 * FRAME
-LEAD = 80
+LEAD = 64
 REST = MID - LEAD
 REACH = LANE + 2 * FRAME
 BF16 = jnp.bfloat16
@@ -106,15 +106,11 @@
     return [rolled[:, block * LANE : (block + 2) * LANE] for block in range(1, TW // LANE - 1)]
 
 
-def lead_kernel(off_hbm, pick_hbm, x_hbm, lead, first, second, wh, wl, vh, vl, x, off, pick, sem):
-    odd = lax.axis_index("tx") % 2
-    spots = [pl.multiple_of(LANE * (TW // LANE - 1) * side, LANE) for side in (1 - odd, odd)]
+def lead_kernel(off_hbm, pick_hbm, x_hbm, lead, wh, wl, vh, vl, x, off, pick, sem):
     copies = [
         pltpu.make_async_copy(off_hbm, off, sem.at[0]),
         pltpu.make_async_copy(pick_hbm, pick, sem.at[1]),
         pltpu.make_async_copy(x_hbm.at[0, pl.ds(0, LEAD + 2 * FRAME)], x, sem.at[2]),
-        pltpu.make_async_copy(x_hbm.at[0, :, pl.ds(spots[0], LANE)], first, sem.at[3]),
-        pltpu.make_async_copy(x_hbm.at[0, :, pl.ds(spots[1], LANE)], second, sem.at[4]),
     ]
     for copy in copies:
         copy.start()
@@ -127,11 +123,13 @@
     copies[2].wait()
     sums = column_sums(core_windows(x[...]), column)
     lead[...] = row_sums([half[:LEAD] for half in row], sums)
-    copies[3].wait()
-    copies[4].wait()
-
-
-def rest_kernel(x, wh, wl, vh, vl, rest):
+
+
+def rest_kernel(x, wh, wl, vh, vl, rest, first, second):
+    even = lax.axis_index("tx") % 2 == 0
+    start, end = x[0, :, :LANE], x[0, :, TW - LANE :]
+    first[...] = jnp.where(even, end, start)
+    second[...] = jnp.where(even, start, end)
     column = (wh[...], wl[...])
     row = (vh[...], vl[...])
     sums = column_sums(core_windows(x[0, LEAD:, :]), column)
@@ -219,14 +217,14 @@
     row = bf16(SPAN, 2 * DEPTH)
     return pl.pallas_call(
         lead_kernel,
-        out_shape=(f32(LEAD, CORE), f32(TH, LANE), f32(TH, LANE), column, column, row, row),
+        out_shape=(f32(LEAD, CORE), column, column, row, row),
         in_specs=[SLOW] * 3,
-        out_specs=(FAST,) * 7,
+        out_specs=(FAST,) * 5,
         scratch_shapes=[
             pltpu.VMEM((LEAD + 2 * FRAME, TW), jnp.float32),
             pltpu.SMEM(offsets.shape, jnp.int32),
             pltpu.SMEM(pick.shape, jnp.int32),
-            pltpu.SemaphoreType.DMA((5,)),
+            pltpu.SemaphoreType.DMA((3,)),
         ],
         compiler_params=LIMIT,
         cost_estimate=cost(10**6),
@@ -331,11 +329,12 @@
 
 def body(raster, shift_pick, offsets):
     count = lax.axis_size("die")
-    lead, first, second, *weights = lead_call(offsets, shift_pick, raster)
+    lead, *weights = lead_call(offsets, shift_pick, raster)
     lead_others = other_dies(lead)
+    strip = f32(TH, LANE)
+    rest, first, second = fast_call(rest_kernel, "rest", (f32(REST, CORE), strip, strip), raster, *weights)
+    rest_others = other_dies(rest)
     first, second = swap_rounds("tx", first, second)
-    rest = fast_call(rest_kernel, "rest", f32(REST, CORE), raster, *weights)
-    rest_others = other_dies(rest)
     halo = f32(FRAME, TW + LANE)
     side, send_first, send_second = fast_call(
         side_kernel, "side", (f32(MID, 2 * LANE), halo, halo), raster, first, second, *weights

time: 35.6 us -> 30.8 us (0.87)
  the two profiles are of different devices: /device:TPU:9 before, /device:TPU:1 now
where the time goes in v4:
time: 30.8 us; the launch traced here: 30.7 us
  starting transfers between devices  9.99 us (32%)
  waiting for transfers between devices  9.63 us (31%)
  Pallas kernels  9.57 us (31%)
  between operations  1.47 us (5%)
    ppermute x4, waiting for transfers between devices, other_dies(): return (lax.ppermute(block, 'die', forward + backward),)  6.44 us
    pallas_call x4, Pallas kernels, change_call(): pl.pallas_call(functools.partial(change_kernel, places, count, fill), out...  3.99 us
    ppermute x4, starting transfers between devices, other_dies(): return (lax.ppermute(block, 'die', forward + backward),)  3.71 us
    ppermute x2, starting transfers between devices, swap_rounds(): lax.ppermute(second, axis, others)  3.7 us
    pallas_call x3, Pallas kernels, fast_call(): pl.pallas_call(kernel, out_shape=out_shape, in_specs=[FAST] * len(operand...  3.65 us
    ppermute x2, waiting for transfers between devices, swap_rounds(): lax.ppermute(second, axis, others)  3.18 us
    ppermute x2, starting transfers between devices, swap_rounds(): lax.ppermute(first, axis, pairs)  2.59 us
    pallas_call x1, Pallas kernels, lead_call(): pl.pallas_call(lead_kernel, out_shape=(f32(LEAD, CORE), column, column, r...  1.93 us
  transfers between devices with their start and end apart: 8, of which 4 were waited for; matrix products, arithmetic and copies ran while one was open for 0% of the time, Pallas kernels for 23%

profile of v4, /device:TPU:1, one launch (start us, length us, event | category | flops | bytes accessed | tf_op | source)
XLA Modules:
  0.0 30.7 jit_solution(14769499246811596589)
XLA Ops:
  0.6 0.0 copy-start
  1.4 1.9 %lead.1 = (f32[64,768]{1,0:T(8,128)S(1)}, bf16[256,256]{1,0:T(8,128)(2,1)S(1)}, bf16[256,256]{1,0:T(8,128)(2,1)S(1)}, bf16[96,256]{1,0:T(8,128)(2,1)S(1)}, bf16[96,256]{1,0:T(8,128)(2,1)S(1)}) custom-call(s32[1,1,1,2]{3,2,1,0:T(1,128)} %off_hbm.1, s32[1,1,1]{2,1,0:T(1,128)S(6)} %copy.17.pick_hbm, f32[1,256,1024]{2,1,0:T(8,128)} %x.5), custom_call_target="tpu_custom_call" | custom-call | flops 1000000 | bytes 4096 | tf_op jit(solution)/shard_map/lead/pallas_call | solution.py:218
  3.3 2.1 %collective-permute-start.7 = (f32[64,768]{1,0:T(8,128)S(1)}, f32[64,768]{1,0:T(8,128)S(1)}, u32[]{:S(2)}, u32[]{:S(2)}) collective-permute-start(f32[64,768]{1,0:T(8,128)S(1)} %get-tuple-element.29.own_ref), channel_id=1, source_target_pairs={{0,16},{16,0},{1,17},{17,1},{2,18},{18,2},{3,19},{19,3},{4,20},{20... | collective-permute-start | bytes 589832 | tf_op jit(solution)/shard_map/ppermute | solution.py:326
  5.4 0.0 copy-done
  5.4 1.6 %rest.1 = (f32[160,768]{1,0:T(8,128)S(1)}, f32[256,128]{1,0:T(8,128)S(1)}, f32[256,128]{1,0:T(8,128)S(1)}) custom-call(f32[1,256,1024]{2,1,0:T(8,128)S(1)} %copy-done, bf16[256,256]{1,0:T(8,128)(2,1)S(1)} %get-tuple-element.19.wh, bf16[256,256]{1,0:T(8,128)(2,1)S(1)} %get-tuple-element.20.wl, bf16[96,256]{1,0:T(8,128)(2,1)S(1)} %get-tuple-element.21.vh, ...), custom_call_target="tpu_custom_call" | custom-call | flops 1000000 | bytes 4096 | tf_op jit(solution)/shard_map/rest/pallas_call | solution.py:237
  7.1 1.0 %collective-permute-start = (f32[256,128]{1,0:T(8,128)S(1)}, f32[256,128]{1,0:T(8,128)S(1)}, u32[]{:S(2)}, u32[]{:S(2)}) collective-permute-start(f32[256,128]{1,0:T(8,128)S(1)} %get-tuple-element.23), channel_id=1, source_target_pairs={{0,1},{1,0},{2,3},{3,2},{4,5},{5,4},{6,7},{7,6},{8,9},{9,8},{10,11... | collective-permute-start | bytes 393224 | tf_op jit(solution)/shard_map/ppermute | solution.py:318
  8.1 3.0 %collective-permute-start.1 = (f32[256,128]{1,0:T(8,128)S(1)}, f32[256,128]{1,0:T(8,128)S(1)}, u32[]{:S(2)}, u32[]{:S(2)}) collective-permute-start(f32[256,128]{1,0:T(8,128)S(1)} %get-tuple-element.24), channel_id=1, source_target_pairs={{0,0},{1,2},{2,1},{3,3},{4,4},{5,6},{6,5},{7,7},{8,8},{9,10},{10,9... | collective-permute-start | bytes 393224 | tf_op jit(solution)/shard_map/ppermute | solution.py:318
  11.1 0.3 %collective-permute-start.6 = (f32[160,768]{1,0:T(8,128)S(1)}, f32[160,768]{1,0:T(8,128)S(1)}, u32[]{:S(2)}, u32[]{:S(2)}) collective-permute-start(f32[160,768]{1,0:T(8,128)S(1)} %get-tuple-element.28.own_ref), channel_id=1, source_target_pairs={{0,16},{16,0},{1,17},{17,1},{2,18},{18,2},{3,19},{19,3},{4,20},{20... | collective-permute-start | bytes 1474568 | tf_op jit(solution)/shard_map/ppermute | solution.py:326
  11.5 0.0 collective-permute-done.first
  11.5 3.2 %collective-permute-done.1.second = f32[256,128]{1,0:T(8,128)S(1)} collective-permute-done((f32[256,128]{1,0:T(8,128)S(1)}, f32[256,128]{1,0:T(8,128)S(1)}, u32[]{:S(2)}, u32[]{:S(2)}) %collective-permute-start.1) | collective-permute-done | bytes 131104 | tf_op jit(solution)/shard_map/ppermute | solution.py:318
  14.7 1.0 %side.1 = (f32[224,256]{1,0:T(8,128)S(1)}, f32[16,1152]{1,0:T(8,128)S(1)}, f32[16,1152]{1,0:T(8,128)S(1)}) custom-call(f32[1,256,1024]{2,1,0:T(8,128)S(1)} %copy-done, f32[256,128]{1,0:T(8,128)S(1)} %collective-permute-done.first, f32[256,128]{1,0:T(8,128)S(1)} %collective-permute-done.1.second, bf16[256,256]{1,0:T(8,128)(2,1)S(1)} %get-tuple-element.19.wh, ...), custom_call_target="tpu_custom_call" | custom-call | flops 1000000 | bytes 4096 | tf_op jit(solution)/shard_map/side/pallas_call | solution.py:237
  15.6 0.0 collective-permute-start.5
  15.6 1.6 %collective-permute-start.2 = (f32[16,1152]{1,0:T(8,128)S(1)}, f32[16,1152]{1,0:T(8,128)S(1)}, u32[]{:S(2)}, u32[]{:S(2)}) collective-permute-start(f32[16,1152]{1,0:T(8,128)S(1)} %get-tuple-element.25), channel_id=1, source_target_pairs={{0,4},{4,0},{8,12},{12,8},{1,5},{5,1},{9,13},{13,9},{2,6},{6,2},{1... | collective-permute-start | bytes 221192 | tf_op jit(solution)/shard_map/ppermute | solution.py:318
  17.2 0.7 %collective-permute-start.3 = (f32[16,1152]{1,0:T(8,128)S(1)}, f32[16,1152]{1,0:T(8,128)S(1)}, u32[]{:S(2)}, u32[]{:S(2)}) collective-permute-start(f32[16,1152]{1,0:T(8,128)S(1)} %get-tuple-element.26), channel_id=1, source_target_pairs={{0,0},{4,8},{8,4},{12,12},{1,1},{5,9},{9,5},{13,13},{2,2},{6,10},{... | collective-permute-start | bytes 221192 | tf_op jit(solution)/shard_map/ppermute | solution.py:318
  17.8 0.0 collective-permute-done.7.refs_0_
  17.9 1.8 %change.4 = (f32[1,256,1024]{2,1,0:T(8,128)}, f32[1,256,1024]{2,1,0:T(8,128)}) custom-call(f32[64,768]{1,0:T(8,128)S(1)} %get-tuple-element.29.own_ref, f32[64,768]{1,0:T(8,128)S(1)} %collective-permute-done.7.refs_0_), custom_call_target="tpu_custom_call" | custom-call | flops 10000000000 | bytes 4096 | tf_op jit(solution)/shard_map/change/pallas_call | solution.py:290
  19.6 0.0 collective-permute-done.2.row_first
  19.6 0.0 collective-permute-done.3.row_second
  19.6 1.1 %frame.1.own_ref = f32[32,1024]{1,0:T(8,128)S(1)} custom-call(f32[1,256,1024]{2,1,0:T(8,128)S(1)} %copy-done, f32[256,128]{1,0:T(8,128)S(1)} %collective-permute-done.first, f32[256,128]{1,0:T(8,128)S(1)} %collective-permute-done.1.second, f32[16,1152]{1,0:T(8,128)S(1)} %collective-permute-done.2.row_first, ...), custom_call_target="tpu_custom_call" | custom-call | flops 1000000 | bytes 4096 | tf_op jit(solution)/shard_map/frame/pallas_call | solution.py:237
  20.7 1.3 %collective-permute-start.4 = (f32[32,1024]{1,0:T(8,128)S(1)}, f32[32,1024]{1,0:T(8,128)S(1)}, u32[]{:S(2)}, u32[]{:S(2)}) collective-permute-start(f32[32,1024]{1,0:T(8,128)S(1)} %frame.1.own_ref), channel_id=1, source_target_pairs={{0,16},{16,0},{1,17},{17,1},{2,18},{18,2},{3,19},{19,3},{4,20},{20... | collective-permute-start | bytes 393224 | tf_op jit(solution)/shard_map/ppermute | solution.py:326
  22.0 2.6 %collective-permute-done.6.refs_0_ = f32[160,768]{1,0:T(8,128)S(1)} collective-permute-done((f32[160,768]{1,0:T(8,128)S(1)}, f32[160,768]{1,0:T(8,128)S(1)}, u32[]{:S(2)}, u32[]{:S(2)}) %collective-permute-start.6) | collective-permute-done | bytes 491552 | tf_op jit(solution)/shard_map/ppermute | solution.py:326
  24.5 0.8 %change.5 = (f32[1,256,1024]{2,1,0:T(8,128)}, f32[1,256,1024]{2,1,0:T(8,128)}) custom-call(f32[160,768]{1,0:T(8,128)S(1)} %get-tuple-element.28.own_ref, f32[160,768]{1,0:T(8,128)S(1)} %collective-permute-done.6.refs_0_, f32[1,256,1024]{2,1,0:T(8,128)} %get-tuple-element.30.refs_1_, ...), custom_call_target="tpu_custom_call", output_to_operand_aliasing={{0}: (2, {}), {1}: (3, {})} | custom-call | flops 10000000000 | bytes 4096 | tf_op jit(solution)/shard_map/change/pallas_call | solution.py:290
  25.4 3.2 %collective-permute-done.5.refs_0_ = f32[224,256]{1,0:T(8,128)S(1)} collective-permute-done((f32[224,256]{1,0:T(8,128)S(1)}, f32[224,256]{1,0:T(8,128)S(1)}, u32[]{:S(2)}, u32[]{:S(2)}) %collective-permute-start.5) | collective-permute-done | bytes 229408 | tf_op jit(solution)/shard_map/ppermute | solution.py:326
  28.6 0.7 %change.6 = (f32[1,256,1024]{2,1,0:T(8,128)}, f32[1,256,1024]{2,1,0:T(8,128)}) custom-call(f32[224,256]{1,0:T(8,128)S(1)} %get-tuple-element.27.own_ref, f32[224,256]{1,0:T(8,128)S(1)} %collective-permute-done.5.refs_0_, f32[1,256,1024]{2,1,0:T(8,128)} %get-tuple-element.32.refs_1_, ...), custom_call_target="tpu_custom_call", output_to_operand_aliasing={{0}: (2, {}), {1}: (3, {})} | custom-call | flops 10000000000 | bytes 4096 | tf_op jit(solution)/shard_map/change/pallas_call | solution.py:290
  29.3 0.7 %collective-permute-done.4.refs_0_ = f32[32,1024]{1,0:T(8,128)S(1)} collective-permute-done((f32[32,1024]{1,0:T(8,128)S(1)}, f32[32,1024]{1,0:T(8,128)S(1)}, u32[]{:S(2)}, u32[]{:S(2)}) %collective-permute-start.4) | collective-permute-done | bytes 131104 | tf_op jit(solution)/shard_map/ppermute | solution.py:326
  30.0 0.7 %change.7 = (f32[1,256,1024]{2,1,0:T(8,128)}, f32[1,256,1024]{2,1,0:T(8,128)}) custom-call(f32[32,1024]{1,0:T(8,128)S(1)} %frame.1.own_ref, f32[32,1024]{1,0:T(8,128)S(1)} %collective-permute-done.4.refs_0_, f32[1,256,1024]{2,1,0:T(8,128)} %get-tuple-element.34.refs_1_, ...), custom_call_target="tpu_custom_call", output_to_operand_aliasing={{0}: (2, {}), {1}: (3, {})} | custom-call | flops 10000000000 | bytes 4096 | tf_op jit(solution)/shard_map/change/pallas_call | solution.py:290
Async XLA Ops:
  0.6 4.8 %copy-start = (f32[1,256,1024]{2,1,0:T(8,128)S(1)}, f32[1,256,1024]{2,1,0:T(8,128)}, u32[]{:S(2)}) copy-start(f32[1,256,1024]{2,1,0:T(8,128)} %x.5) | copy-start | bytes 3145732
  3.3 14.5 %collective-permute-start.7 = (f32[64,768]{1,0:T(8,128)S(1)}, f32[64,768]{1,0:T(8,128)S(1)}, u32[]{:S(2)}, u32[]{:S(2)}) collective-permute-start(f32[64,768]{1,0:T(8,128)S(1)} %get-tuple-element.29.own_ref), channel_id=1, source_target_pairs={{0,16},{16,0},{1,17},{17,1},{2,18},{18,2},{3,19},{19,3},{4,20},{20... | collective-permute-start | bytes 589832 | tf_op jit(solution)/shard_map/ppermute | solution.py:326
  7.1 4.4 %collective-permute-start = (f32[256,128]{1,0:T(8,128)S(1)}, f32[256,128]{1,0:T(8,128)S(1)}, u32[]{:S(2)}, u32[]{:S(2)}) collective-permute-start(f32[256,128]{1,0:T(8,128)S(1)} %get-tuple-element.23), channel_id=1, source_target_pairs={{0,1},{1,0},{2,3},{3,2},{4,5},{5,4},{6,7},{7,6},{8,9},{9,8},{10,11... | collective-permute-start | bytes 393224 | tf_op jit(solution)/shard_map/ppermute | solution.py:318
  8.1 6.6 %collective-permute-start.1 = (f32[256,128]{1,0:T(8,128)S(1)}, f32[256,128]{1,0:T(8,128)S(1)}, u32[]{:S(2)}, u32[]{:S(2)}) collective-permute-start(f32[256,128]{1,0:T(8,128)S(1)} %get-tuple-element.24), channel_id=1, source_target_pairs={{0,0},{1,2},{2,1},{3,3},{4,4},{5,6},{6,5},{7,7},{8,8},{9,10},{10,9... | collective-permute-start | bytes 393224 | tf_op jit(solution)/shard_map/ppermute | solution.py:318
  11.1 13.4 %collective-permute-start.6 = (f32[160,768]{1,0:T(8,128)S(1)}, f32[160,768]{1,0:T(8,128)S(1)}, u32[]{:S(2)}, u32[]{:S(2)}) collective-permute-start(f32[160,768]{1,0:T(8,128)S(1)} %get-tuple-element.28.own_ref), channel_id=1, source_target_pairs={{0,16},{16,0},{1,17},{17,1},{2,18},{18,2},{3,19},{19,3},{4,20},{20... | collective-permute-start | bytes 1474568 | tf_op jit(solution)/shard_map/ppermute | solution.py:326
  15.6 13.0 %collective-permute-start.5 = (f32[224,256]{1,0:T(8,128)S(1)}, f32[224,256]{1,0:T(8,128)S(1)}, u32[]{:S(2)}, u32[]{:S(2)}) collective-permute-start(f32[224,256]{1,0:T(8,128)S(1)} %get-tuple-element.27.own_ref), channel_id=1, source_target_pairs={{0,16},{16,0},{1,17},{17,1},{2,18},{18,2},{3,19},{19,3},{4,20},{20... | collective-permute-start | bytes 688136 | tf_op jit(solution)/shard_map/ppermute | solution.py:326
  15.6 4.0 %collective-permute-start.2 = (f32[16,1152]{1,0:T(8,128)S(1)}, f32[16,1152]{1,0:T(8,128)S(1)}, u32[]{:S(2)}, u32[]{:S(2)}) collective-permute-start(f32[16,1152]{1,0:T(8,128)S(1)} %get-tuple-element.25), channel_id=1, source_target_pairs={{0,4},{4,0},{8,12},{12,8},{1,5},{5,1},{9,13},{13,9},{2,6},{6,2},{1... | collective-permute-start | bytes 221192 | tf_op jit(solution)/shard_map/ppermute | solution.py:318
  17.2 2.4 %collective-permute-start.3 = (f32[16,1152]{1,0:T(8,128)S(1)}, f32[16,1152]{1,0:T(8,128)S(1)}, u32[]{:S(2)}, u32[]{:S(2)}) collective-permute-start(f32[16,1152]{1,0:T(8,128)S(1)} %get-tuple-element.26), channel_id=1, source_target_pairs={{0,0},{4,8},{8,4},{12,12},{1,1},{5,9},{9,5},{13,13},{2,2},{6,10},{... | collective-permute-start | bytes 221192 | tf_op jit(solution)/shard_map/ppermute | solution.py:318
  20.7 9.3 %collective-permute-start.4 = (f32[32,1024]{1,0:T(8,128)S(1)}, f32[32,1024]{1,0:T(8,128)S(1)}, u32[]{:S(2)}, u32[]{:S(2)}) collective-permute-start(f32[32,1024]{1,0:T(8,128)S(1)} %frame.1.own_ref), channel_id=1, source_target_pairs={{0,16},{16,0},{1,17},{17,1},{2,18},{18,2},{3,19},{19,3},{4,20},{20... | collective-permute-start | bytes 393224 | tf_op jit(solution)/shard_map/ppermute | solution.py:326

commit v5 on v4

--- a/solution.py
+++ b/solution.py
@@ -106,33 +106,35 @@
     return [rolled[:, block * LANE : (block + 2) * LANE] for block in range(1, TW // LANE - 1)]
 
 
-def lead_kernel(off_hbm, pick_hbm, x_hbm, lead, wh, wl, vh, vl, x, off, pick, sem):
+def lead_kernel(off_ref, pick_ref, x_hbm, lead, x, wh, wl, vh, vl, sem):
+    need = LEAD + 2 * FRAME
+    parts = [pl.ds(0, need), pl.ds(need, TH - need)]
     copies = [
-        pltpu.make_async_copy(off_hbm, off, sem.at[0]),
-        pltpu.make_async_copy(pick_hbm, pick, sem.at[1]),
-        pltpu.make_async_copy(x_hbm.at[0, pl.ds(0, LEAD + 2 * FRAME)], x, sem.at[2]),
+        pltpu.make_async_copy(x_hbm.at[0, rows], x.at[rows], sem.at[k]) for k, rows in enumerate(parts)
     ]
     for copy in copies:
         copy.start()
-    copies[0].wait()
-    copies[1].wait()
-    column = column_weights(off[0, 0, 0, 1], pick[0, 0, 0])
-    row = row_weights(off[0, 0, 0, 0], pick[0, 0, 0])
+    offsets = off_ref[0, 0]
+    pick = pick_ref[0, 0, 0]
+    column = column_weights(offsets[:, 1:], pick)
+    row = row_weights(offsets[:, :1], pick)
     wh[...], wl[...] = column
     vh[...], vl[...] = row
-    copies[2].wait()
-    sums = column_sums(core_windows(x[...]), column)
+    copies[0].wait()
+    sums = column_sums(core_windows(x[:need, :]), column)
     lead[...] = row_sums([half[:LEAD] for half in row], sums)
+    copies[1].wait()
 
 
 def rest_kernel(x, wh, wl, vh, vl, rest, first, second):
     even = lax.axis_index("tx") % 2 == 0
-    start, end = x[0, :, :LANE], x[0, :, TW - LANE :]
+    start = x[:, :LANE].T[:FRAME]
+    end = x[:, TW - LANE :].T[LANE - FRAME :]
     first[...] = jnp.where(even, end, start)
     second[...] = jnp.where(even, start, end)
     column = (wh[...], wl[...])
     row = (vh[...], vl[...])
-    sums = column_sums(core_windows(x[0, LEAD:, :]), column)
+    sums = column_sums(core_windows(x[LEAD:, :]), column)
     rest[:SPAN, :] = row_sums(row, sums)
     last = REST - SPAN
     lower = [half[SPAN - last :] for half in row]
@@ -147,18 +149,16 @@
     return jnp.where(even, second, first), jnp.where(even, first, second)
 
 
-def edge_block(before, after):
-    lane = lax.broadcasted_iota(jnp.int32, before.shape, 1)
-    return jnp.where(lane < LANE // 2, after, before)
-
-
-def side_kernel(x, first, second, wh, wl, vh, vl, side, send_first, send_second):
+def side_kernel(x, first, second, wh, wl, vh, vl, side, send_first, send_second, edge_ref):
     column = (wh[...], wl[...])
     row = (vh[...], vl[...])
     before, after = halos("tx", first[...], second[...])
+    filler = jnp.zeros((LANE - 2 * FRAME, TH), jnp.float32)
+    edge = jnp.concatenate([after, filler, before], axis=0).T
+    edge_ref[...] = edge
     windows = [
         pltpu.roll(jnp.concatenate(strip, axis=1), 2 * LANE + HW, 1)[:, : 2 * LANE]
-        for strip in ((before, x[0, :, : 2 * LANE]), (x[0, :, TW - 2 * LANE :], after))
+        for strip in ((edge, x[:, : 2 * LANE]), (x[:, TW - 2 * LANE :], edge))
     ]
     sums = column_sums(windows, column)
     side[:SPAN, :] = row_sums(row, sums)
@@ -166,21 +166,20 @@
     last = MID - 2 * SPAN
     lower = [half[SPAN - last :] for half in row]
     side[2 * SPAN :, :] = row_sums(lower, sums, TH - DEPTH)
-    edge = edge_block(before, after)
-    top = jnp.concatenate([x[0, :FRAME, :], edge[:FRAME]], axis=1)
-    bottom = jnp.concatenate([x[0, TH - FRAME :, :], edge[TH - FRAME :]], axis=1)
+    top = jnp.concatenate([x[:FRAME, :], edge[:FRAME]], axis=1)
+    bottom = jnp.concatenate([x[TH - FRAME :, :], edge[TH - FRAME :]], axis=1)
     even = lax.axis_index("ty") % 2 == 0
     send_first[...] = jnp.where(even, bottom, top)
     send_second[...] = jnp.where(even, top, bottom)
 
 
-def frame_kernel(x, first, second, row_first, row_second, wh, wl, vh, vl, frame):
+def frame_kernel(x, edge, row_first, row_second, wh, wl, vh, vl, frame):
     column = (wh[...], wl[...])
     top, bottom = halos("ty", row_first[...], row_second[...])
-    own = []
-    for rows in (slice(0, STRIP), slice(TH - STRIP, TH)):
-        edge = edge_block(*halos("tx", first[rows, :], second[rows, :]))
-        own.append(jnp.concatenate([x[0, rows, :], edge], axis=1))
+    own = [
+        jnp.concatenate([x[rows, :], edge[rows, :]], axis=1)
+        for rows in (slice(0, STRIP), slice(TH - STRIP, TH))
+    ]
     values = jnp.concatenate([top, own[0], own[1], bottom], axis=0)
     rolled = pltpu.roll(values, HW, 1)
     windows = [rolled[:, block * LANE : (block + 2) * LANE] for block in range(TW // LANE)]
@@ -190,7 +189,7 @@
     frame[...] = row_sums(row, sums)
 
 
-CHANGE_COST = 10**10
+COSTS = (4 * 10**9, 10**10, 10**10, 10**10)
 FAST = pl.BlockSpec(memory_space=pltpu.VMEM)
 SLOW = pl.BlockSpec(memory_space=pltpu.HBM)
 LIMIT = pltpu.CompilerParams(vmem_limit_bytes=16 * 2**20)
@@ -217,19 +216,14 @@
     row = bf16(SPAN, 2 * DEPTH)
     return pl.pallas_call(
         lead_kernel,
-        out_shape=(f32(LEAD, CORE), column, column, row, row),
-        in_specs=[SLOW] * 3,
-        out_specs=(FAST,) * 5,
-        scratch_shapes=[
-            pltpu.VMEM((LEAD + 2 * FRAME, TW), jnp.float32),
-            pltpu.SMEM(offsets.shape, jnp.int32),
-            pltpu.SMEM(pick.shape, jnp.int32),
-            pltpu.SemaphoreType.DMA((3,)),
-        ],
+        out_shape=(f32(LEAD, CORE), f32(TH, TW), column, column, row, row),
+        in_specs=[FAST, pl.BlockSpec(memory_space=pltpu.SMEM), SLOW],
+        out_specs=(FAST,) * 6,
+        scratch_shapes=[pltpu.SemaphoreType.DMA((2,))],
         compiler_params=LIMIT,
         cost_estimate=cost(10**6),
         name="lead",
-    )(keep(offsets), pick, keep(raster))
+    )(offsets, pick, keep(raster))
 
 
 def fast_call(kernel, name, out_shape, *operands):
@@ -283,7 +277,7 @@
                 copy.wait()
 
 
-def change_call(count, places, own, others, maps):
+def change_call(count, places, flops, own, others, maps):
     operands = (own, *others)
     fill = not maps
     out = f32(1, TH, TW)
@@ -299,7 +293,7 @@
         ],
         input_output_aliases={len(operands) + k: k for k in range(len(maps))},
         compiler_params=LIMIT,
-        cost_estimate=cost(CHANGE_COST),
+        cost_estimate=cost(flops),
         name="change",
     )(*operands, *maps)
 
@@ -329,26 +323,26 @@
 
 def body(raster, shift_pick, offsets):
     count = lax.axis_size("die")
-    lead, *weights = lead_call(offsets, shift_pick, raster)
+    lead, tile, *weights = lead_call(offsets, shift_pick, raster)
     lead_others = other_dies(lead)
-    strip = f32(TH, LANE)
-    rest, first, second = fast_call(rest_kernel, "rest", (f32(REST, CORE), strip, strip), raster, *weights)
+    strip = f32(FRAME, TH)
+    rest, first, second = fast_call(rest_kernel, "rest", (f32(REST, CORE), strip, strip), tile, *weights)
     rest_others = other_dies(rest)
     first, second = swap_rounds("tx", first, second)
     halo = f32(FRAME, TW + LANE)
-    side, send_first, send_second = fast_call(
-        side_kernel, "side", (f32(MID, 2 * LANE), halo, halo), raster, first, second, *weights
+    side, send_first, send_second, edge = fast_call(
+        side_kernel, "side", (f32(MID, 2 * LANE), halo, halo, f32(TH, LANE)), tile, first, second, *weights
     )
     side_others = other_dies(side)
     row_first, row_second = swap_rounds("ty", send_first, send_second)
     frame = fast_call(
-        frame_kernel, "frame", f32(STRIP, TW), raster, first, second, row_first, row_second, *weights
+        frame_kernel, "frame", f32(STRIP, TW), tile, edge, row_first, row_second, *weights
     )
     frame_others = other_dies(frame)
-    maps = change_call(count, LEAD_PLACES, lead, lead_others, ())
-    maps = change_call(count, REST_PLACES, rest, rest_others, maps)
-    maps = change_call(count, SIDE_PLACES, side, side_others, maps)
-    return tuple(change_call(count, FRAME_PLACES, frame, frame_others, maps))
+    maps = change_call(count, LEAD_PLACES, COSTS[0], lead, lead_others, ())
+    maps = change_call(count, REST_PLACES, COSTS[1], rest, rest_others, maps)
+    maps = change_call(count, SIDE_PLACES, COSTS[2], side, side_others, maps)
+    return tuple(change_call(count, FRAME_PLACES, COSTS[3], frame, frame_others, maps))
 
 
 def solution(mesh):

time: 30.8 us -> 30.3 us (0.984)
  the two profiles are of different devices: /device:TPU:1 before, /device:TPU:0 now
where the time goes in v5:
time: 30.3 us; the launch traced here: 30.1 us
  starting transfers between devices  10.1 us (33%)
  Pallas kernels  9.72 us (32%)
  waiting for transfers between devices  8.92 us (29%)
  between operations  1.37 us (5%)
    ppermute x4, waiting for transfers between devices, other_dies(): return (lax.ppermute(block, 'die', forward + backward),)  8.3 us
    ppermute x4, starting transfers between devices, other_dies(): return (lax.ppermute(block, 'die', forward + backward),)  6.62 us
    pallas_call x4, Pallas kernels, change_call(): pl.pallas_call(functools.partial(change_kernel, places, count, fill), out...  3.98 us
    pallas_call x3, Pallas kernels, fast_call(): pl.pallas_call(kernel, out_shape=out_shape, in_specs=[FAST] * len(operand...  3.82 us
    ppermute x2, starting transfers between devices, swap_rounds(): lax.ppermute(first, axis, pairs)  2.12 us
    pallas_call x1, Pallas kernels, lead_call(): pl.pallas_call(lead_kernel, out_shape=(f32(LEAD, CORE), f32(TH, TW), colu...  1.92 us
    ppermute x2, starting transfers between devices, swap_rounds(): lax.ppermute(second, axis, others)  1.32 us
    ppermute x2, waiting for transfers between devices, swap_rounds(): lax.ppermute(first, axis, pairs)  0.61 us
  transfers between devices with their start and end apart: 8, of which 5 were waited for; matrix products, arithmetic and copies ran while one was open for 0% of the time, Pallas kernels for 24%

profile of v5, /device:TPU:0, one launch (start us, length us, event | category | flops | bytes accessed | tf_op | source)
XLA Modules:
  0.0 30.1 jit_solution(17161619304769408955)
XLA Ops:
  0.6 0.0 copy-start
  1.3 0.0 copy-done
  1.3 1.9 %lead.1 = (f32[64,768]{1,0:T(8,128)S(1)}, f32[256,1024]{1,0:T(8,128)S(1)}, bf16[256,256]{1,0:T(8,128)(2,1)S(1)}, bf16[256,256]{1,0:T(8,128)(2,1)S(1)}, bf16[96,2...) custom-call(s32[1,1,1,2]{3,2,1,0:T(1,128)S(1)} %copy-done, s32[1,1,1]{2,1,0:T(1,128)S(6)} %copy.17.pick_ref, ...), custom_call_target="tpu_custom_call" | custom-call | flops 1000000 | bytes 4096 | tf_op jit(solution)/shard_map/lead/pallas_call | solution.py:217
  3.2 3.0 %collective-permute-start.7 = (f32[64,768]{1,0:T(8,128)S(1)}, f32[64,768]{1,0:T(8,128)S(1)}, u32[]{:S(2)}, u32[]{:S(2)}) collective-permute-start(f32[64,768]{1,0:T(8,128)S(1)} %get-tuple-element.33.own_ref), channel_id=1, source_target_pairs={{0,16},{16,0},{1,17},{17,1},{2,18},{18,2},{3,19},{19,3},{4,20},{20... | collective-permute-start | bytes 589832 | tf_op jit(solution)/shard_map/ppermute | solution.py:320
  6.2 1.6 %rest.1 = (f32[160,768]{1,0:T(8,128)S(1)}, f32[16,256]{1,0:T(8,128)S(1)}, f32[16,256]{1,0:T(8,128)S(1)}) custom-call(f32[256,1024]{1,0:T(8,128)S(1)} %get-tuple-element.21.x, bf16[256,256]{1,0:T(8,128)(2,1)S(1)} %get-tuple-element.22.wh, bf16[256,256]{1,0:T(8,128)(2,1)S(1)} %get-tuple-element.23.wl, bf16[96,256]{1,0:T(8,128)(2,1)S(1)} %get-tuple-element.24.vh, ...), custom_call_target="tpu_custom_call" | custom-call | flops 1000000 | bytes 4096 | tf_op jit(solution)/shard_map/rest/pallas_call | solution.py:231
  7.9 0.1 collective-permute-start.6
  8.0 0.1 collective-permute-start
  8.0 0.7 %collective-permute-start.1 = (f32[16,256]{1,0:T(8,128)S(1)}, f32[16,256]{1,0:T(8,128)S(1)}, u32[]{:S(2)}, u32[]{:S(2)}) collective-permute-start(f32[16,256]{1,0:T(8,128)S(1)} %get-tuple-element.27), channel_id=1, source_target_pairs={{0,0},{1,2},{2,1},{3,3},{4,4},{5,6},{6,5},{7,7},{8,8},{9,10},{10,9... | collective-permute-start | bytes 49160 | tf_op jit(solution)/shard_map/ppermute | solution.py:312
  8.7 0.5 %collective-permute-done.first = f32[16,256]{1,0:T(8,128)S(1)} collective-permute-done((f32[16,256]{1,0:T(8,128)S(1)}, f32[16,256]{1,0:T(8,128)S(1)}, u32[]{:S(2)}, u32[]{:S(2)}) %collective-permute-start) | collective-permute-done | bytes 16416 | tf_op jit(solution)/shard_map/ppermute | solution.py:312
  9.2 0.0 collective-permute-done.1.second
  9.2 1.1 %side.1 = (f32[224,256]{1,0:T(8,128)S(1)}, f32[16,1152]{1,0:T(8,128)S(1)}, f32[16,1152]{1,0:T(8,128)S(1)}, f32[256,128]{1,0:T(8,128)S(1)}) custom-call(f32[256,1024]{1,0:T(8,128)S(1)} %get-tuple-element.21.x, f32[16,256]{1,0:T(8,128)S(1)} %collective-permute-done.first, f32[16,256]{1,0:T(8,128)S(1)} %collective-permute-done.1.second, ...), custom_call_target="tpu_custom_call" | custom-call | flops 1000000 | bytes 4096 | tf_op jit(solution)/shard_map/side/pallas_call | solution.py:231
  10.3 2.1 %collective-permute-start.2 = (f32[16,1152]{1,0:T(8,128)S(1)}, f32[16,1152]{1,0:T(8,128)S(1)}, u32[]{:S(2)}, u32[]{:S(2)}) collective-permute-start(f32[16,1152]{1,0:T(8,128)S(1)} %get-tuple-element.29), channel_id=1, source_target_pairs={{0,4},{4,0},{8,12},{12,8},{1,5},{5,1},{9,13},{13,9},{2,6},{6,2},{1... | collective-permute-start | bytes 221192 | tf_op jit(solution)/shard_map/ppermute | solution.py:312
  12.4 0.7 %collective-permute-start.3 = (f32[16,1152]{1,0:T(8,128)S(1)}, f32[16,1152]{1,0:T(8,128)S(1)}, u32[]{:S(2)}, u32[]{:S(2)}) collective-permute-start(f32[16,1152]{1,0:T(8,128)S(1)} %get-tuple-element.30), channel_id=1, source_target_pairs={{0,0},{4,8},{8,4},{12,12},{1,1},{5,9},{9,5},{13,13},{2,2},{6,10},{... | collective-permute-start | bytes 221192 | tf_op jit(solution)/shard_map/ppermute | solution.py:312
  13.1 1.6 %collective-permute-start.5 = (f32[224,256]{1,0:T(8,128)S(1)}, f32[224,256]{1,0:T(8,128)S(1)}, u32[]{:S(2)}, u32[]{:S(2)}) collective-permute-start(f32[224,256]{1,0:T(8,128)S(1)} %get-tuple-element.31.own_ref), channel_id=1, source_target_pairs={{0,16},{16,0},{1,17},{17,1},{2,18},{18,2},{3,19},{19,3},{4,20},{20... | collective-permute-start | bytes 688136 | tf_op jit(solution)/shard_map/ppermute | solution.py:320
  14.6 0.1 collective-permute-done.2.row_first
  14.7 0.0 collective-permute-done.3.row_second
  14.7 1.1 %frame.1.own_ref = f32[32,1024]{1,0:T(8,128)S(1)} custom-call(f32[256,1024]{1,0:T(8,128)S(1)} %get-tuple-element.21.x, f32[256,128]{1,0:T(8,128)S(1)} %get-tuple-element.28.edge, f32[16,1152]{1,0:T(8,128)S(1)} %collective-permute-done.2.row_first, f32[16,1152]{1,0:T(8,128)S(1)} %collective-permute-done.3.row_second, ...), custom_call_target="tpu_custom_call" | custom-call | flops 1000000 | bytes 4096 | tf_op jit(solution)/shard_map/frame/pallas_call | solution.py:231
  15.8 2.0 %collective-permute-start.4 = (f32[32,1024]{1,0:T(8,128)S(1)}, f32[32,1024]{1,0:T(8,128)S(1)}, u32[]{:S(2)}, u32[]{:S(2)}) collective-permute-start(f32[32,1024]{1,0:T(8,128)S(1)} %frame.1.own_ref), channel_id=1, source_target_pairs={{0,16},{16,0},{1,17},{17,1},{2,18},{18,2},{3,19},{19,3},{4,20},{20... | collective-permute-start | bytes 393224 | tf_op jit(solution)/shard_map/ppermute | solution.py:320
  17.8 0.0 collective-permute-done.7.refs_0_
  17.8 1.7 %change.4 = (f32[1,256,1024]{2,1,0:T(8,128)}, f32[1,256,1024]{2,1,0:T(8,128)}) custom-call(f32[64,768]{1,0:T(8,128)S(1)} %get-tuple-element.33.own_ref, f32[64,768]{1,0:T(8,128)S(1)} %collective-permute-done.7.refs_0_), custom_call_target="tpu_custom_call" | custom-call | flops 4000000000 | bytes 4096 | tf_op jit(solution)/shard_map/change/pallas_call | solution.py:284
  19.5 3.0 %collective-permute-done.6.refs_0_ = f32[160,768]{1,0:T(8,128)S(1)} collective-permute-done((f32[160,768]{1,0:T(8,128)S(1)}, f32[160,768]{1,0:T(8,128)S(1)}, u32[]{:S(2)}, u32[]{:S(2)}) %collective-permute-start.6) | collective-permute-done | bytes 491552 | tf_op jit(solution)/shard_map/ppermute | solution.py:320
  22.5 0.8 %change.5 = (f32[1,256,1024]{2,1,0:T(8,128)}, f32[1,256,1024]{2,1,0:T(8,128)}) custom-call(f32[160,768]{1,0:T(8,128)S(1)} %get-tuple-element.32.own_ref, f32[160,768]{1,0:T(8,128)S(1)} %collective-permute-done.6.refs_0_, f32[1,256,1024]{2,1,0:T(8,128)} %get-tuple-element.34.refs_1_, ...), custom_call_target="tpu_custom_call", output_to_operand_aliasing={{0}: (2, {}), {1}: (3, {})} | custom-call | flops 10000000000 | bytes 4096 | tf_op jit(solution)/shard_map/change/pallas_call | solution.py:284
  23.3 4.1 %collective-permute-done.5.refs_0_ = f32[224,256]{1,0:T(8,128)S(1)} collective-permute-done((f32[224,256]{1,0:T(8,128)S(1)}, f32[224,256]{1,0:T(8,128)S(1)}, u32[]{:S(2)}, u32[]{:S(2)}) %collective-permute-start.5) | collective-permute-done | bytes 229408 | tf_op jit(solution)/shard_map/ppermute | solution.py:320
  27.4 0.7 %change.6 = (f32[1,256,1024]{2,1,0:T(8,128)}, f32[1,256,1024]{2,1,0:T(8,128)}) custom-call(f32[224,256]{1,0:T(8,128)S(1)} %get-tuple-element.31.own_ref, f32[224,256]{1,0:T(8,128)S(1)} %collective-permute-done.5.refs_0_, f32[1,256,1024]{2,1,0:T(8,128)} %get-tuple-element.36.refs_1_, ...), custom_call_target="tpu_custom_call", output_to_operand_aliasing={{0}: (2, {}), {1}: (3, {})} | custom-call | flops 10000000000 | bytes 4096 | tf_op jit(solution)/shard_map/change/pallas_call | solution.py:284
  28.1 1.3 %collective-permute-done.4.refs_0_ = f32[32,1024]{1,0:T(8,128)S(1)} collective-permute-done((f32[32,1024]{1,0:T(8,128)S(1)}, f32[32,1024]{1,0:T(8,128)S(1)}, u32[]{:S(2)}, u32[]{:S(2)}) %collective-permute-start.4) | collective-permute-done | bytes 131104 | tf_op jit(solution)/shard_map/ppermute | solution.py:320
  29.4 0.7 %change.7 = (f32[1,256,1024]{2,1,0:T(8,128)}, f32[1,256,1024]{2,1,0:T(8,128)}) custom-call(f32[32,1024]{1,0:T(8,128)S(1)} %frame.1.own_ref, f32[32,1024]{1,0:T(8,128)S(1)} %collective-permute-done.4.refs_0_, f32[1,256,1024]{2,1,0:T(8,128)} %get-tuple-element.38.refs_1_, ...), custom_call_target="tpu_custom_call", output_to_operand_aliasing={{0}: (2, {}), {1}: (3, {})} | custom-call | flops 10000000000 | bytes 4096 | tf_op jit(solution)/shard_map/change/pallas_call | solution.py:284
Async XLA Ops:
  0.6 0.7 %copy-start = (s32[1,1,1,2]{3,2,1,0:T(1,128)S(1)}, s32[1,1,1,2]{3,2,1,0:T(1,128)}, u32[]{:S(2)}) copy-start(s32[1,1,1,2]{3,2,1,0:T(1,128)} %off_ref.1) | copy-start | bytes 28
  3.2 14.5 %collective-permute-start.7 = (f32[64,768]{1,0:T(8,128)S(1)}, f32[64,768]{1,0:T(8,128)S(1)}, u32[]{:S(2)}, u32[]{:S(2)}) collective-permute-start(f32[64,768]{1,0:T(8,128)S(1)} %get-tuple-element.33.own_ref), channel_id=1, source_target_pairs={{0,16},{16,0},{1,17},{17,1},{2,18},{18,2},{3,19},{19,3},{4,20},{20... | collective-permute-start | bytes 589832 | tf_op jit(solution)/shard_map/ppermute | solution.py:320
  7.9 14.6 %collective-permute-start.6 = (f32[160,768]{1,0:T(8,128)S(1)}, f32[160,768]{1,0:T(8,128)S(1)}, u32[]{:S(2)}, u32[]{:S(2)}) collective-permute-start(f32[160,768]{1,0:T(8,128)S(1)} %get-tuple-element.32.own_ref), channel_id=1, source_target_pairs={{0,16},{16,0},{1,17},{17,1},{2,18},{18,2},{3,19},{19,3},{4,20},{20... | collective-permute-start | bytes 1474568 | tf_op jit(solution)/shard_map/ppermute | solution.py:320
  8.0 1.2 %collective-permute-start = (f32[16,256]{1,0:T(8,128)S(1)}, f32[16,256]{1,0:T(8,128)S(1)}, u32[]{:S(2)}, u32[]{:S(2)}) collective-permute-start(f32[16,256]{1,0:T(8,128)S(1)} %get-tuple-element.26), channel_id=1, source_target_pairs={{0,1},{1,0},{2,3},{3,2},{4,5},{5,4},{6,7},{7,6},{8,9},{9,8},{10,11... | collective-permute-start | bytes 49160 | tf_op jit(solution)/shard_map/ppermute | solution.py:312
  8.0 1.2 %collective-permute-start.1 = (f32[16,256]{1,0:T(8,128)S(1)}, f32[16,256]{1,0:T(8,128)S(1)}, u32[]{:S(2)}, u32[]{:S(2)}) collective-permute-start(f32[16,256]{1,0:T(8,128)S(1)} %get-tuple-element.27), channel_id=1, source_target_pairs={{0,0},{1,2},{2,1},{3,3},{4,4},{5,6},{6,5},{7,7},{8,8},{9,10},{10,9... | collective-permute-start | bytes 49160 | tf_op jit(solution)/shard_map/ppermute | solution.py:312
  10.3 4.4 %collective-permute-start.2 = (f32[16,1152]{1,0:T(8,128)S(1)}, f32[16,1152]{1,0:T(8,128)S(1)}, u32[]{:S(2)}, u32[]{:S(2)}) collective-permute-start(f32[16,1152]{1,0:T(8,128)S(1)} %get-tuple-element.29), channel_id=1, source_target_pairs={{0,4},{4,0},{8,12},{12,8},{1,5},{5,1},{9,13},{13,9},{2,6},{6,2},{1... | collective-permute-start | bytes 221192 | tf_op jit(solution)/shard_map/ppermute | solution.py:312
  12.4 2.3 %collective-permute-start.3 = (f32[16,1152]{1,0:T(8,128)S(1)}, f32[16,1152]{1,0:T(8,128)S(1)}, u32[]{:S(2)}, u32[]{:S(2)}) collective-permute-start(f32[16,1152]{1,0:T(8,128)S(1)} %get-tuple-element.30), channel_id=1, source_target_pairs={{0,0},{4,8},{8,4},{12,12},{1,1},{5,9},{9,5},{13,13},{2,2},{6,10},{... | collective-permute-start | bytes 221192 | tf_op jit(solution)/shard_map/ppermute | solution.py:312
  13.1 14.4 %collective-permute-start.5 = (f32[224,256]{1,0:T(8,128)S(1)}, f32[224,256]{1,0:T(8,128)S(1)}, u32[]{:S(2)}, u32[]{:S(2)}) collective-permute-start(f32[224,256]{1,0:T(8,128)S(1)} %get-tuple-element.31.own_ref), channel_id=1, source_target_pairs={{0,16},{16,0},{1,17},{17,1},{2,18},{18,2},{3,19},{19,3},{4,20},{20... | collective-permute-start | bytes 688136 | tf_op jit(solution)/shard_map/ppermute | solution.py:320
  15.8 13.6 %collective-permute-start.4 = (f32[32,1024]{1,0:T(8,128)S(1)}, f32[32,1024]{1,0:T(8,128)S(1)}, u32[]{:S(2)}, u32[]{:S(2)}) collective-permute-start(f32[32,1024]{1,0:T(8,128)S(1)} %frame.1.own_ref), channel_id=1, source_target_pairs={{0,16},{16,0},{1,17},{17,1},{2,18},{18,2},{3,19},{19,3},{4,20},{20... | collective-permute-start | bytes 393224 | tf_op jit(solution)/shard_map/ppermute | solution.py:320

commit v6 on v5

--- a/solution.py
+++ b/solution.py
@@ -106,35 +106,27 @@
     return [rolled[:, block * LANE : (block + 2) * LANE] for block in range(1, TW // LANE - 1)]
 
 
-def lead_kernel(off_ref, pick_ref, x_hbm, lead, x, wh, wl, vh, vl, sem):
-    need = LEAD + 2 * FRAME
-    parts = [pl.ds(0, need), pl.ds(need, TH - need)]
-    copies = [
-        pltpu.make_async_copy(x_hbm.at[0, rows], x.at[rows], sem.at[k]) for k, rows in enumerate(parts)
-    ]
-    for copy in copies:
-        copy.start()
+def weights_kernel(off_ref, pick_ref, wh, wl, vh, vl):
     offsets = off_ref[0, 0]
     pick = pick_ref[0, 0, 0]
-    column = column_weights(offsets[:, 1:], pick)
-    row = row_weights(offsets[:, :1], pick)
-    wh[...], wl[...] = column
-    vh[...], vl[...] = row
-    copies[0].wait()
-    sums = column_sums(core_windows(x[:need, :]), column)
-    lead[...] = row_sums([half[:LEAD] for half in row], sums)
-    copies[1].wait()
+    wh[...], wl[...] = column_weights(offsets[:, 1:], pick)
+    vh[...], vl[...] = row_weights(offsets[:, :1], pick)
+
+
+def lead_kernel(x, wh, wl, vh, vl, lead):
+    sums = column_sums(core_windows(x[0, : LEAD + 2 * FRAME, :]), (wh[...], wl[...]))
+    lead[...] = row_sums([half[:LEAD, :] for half in (vh, vl)], sums)
 
 
 def rest_kernel(x, wh, wl, vh, vl, rest, first, second):
     even = lax.axis_index("tx") % 2 == 0
-    start = x[:, :LANE].T[:FRAME]
-    end = x[:, TW - LANE :].T[LANE - FRAME :]
+    start = x[0, :, :LANE].T[:FRAME]
+    end = x[0, :, TW - LANE :].T[LANE - FRAME :]
     first[...] = jnp.where(even, end, start)
     second[...] = jnp.where(even, start, end)
     column = (wh[...], wl[...])
     row = (vh[...], vl[...])
-    sums = column_sums(core_windows(x[LEAD:, :]), column)
+    sums = column_sums(core_windows(x[0, LEAD:, :]), column)
     rest[:SPAN, :] = row_sums(row, sums)
     last = REST - SPAN
     lower = [half[SPAN - last :] for half in row]
@@ -158,7 +150,7 @@
     edge_ref[...] = edge
     windows = [
         pltpu.roll(jnp.concatenate(strip, axis=1), 2 * LANE + HW, 1)[:, : 2 * LANE]
-        for strip in ((edge, x[:, : 2 * LANE]), (x[:, TW - 2 * LANE :], edge))
+        for strip in ((edge, x[0, :, : 2 * LANE]), (x[0, :, TW - 2 * LANE :], edge))
     ]
     sums = column_sums(windows, column)
     side[:SPAN, :] = row_sums(row, sums)
@@ -166,8 +158,8 @@
     last = MID - 2 * SPAN
     lower = [half[SPAN - last :] for half in row]
     side[2 * SPAN :, :] = row_sums(lower, sums, TH - DEPTH)
-    top = jnp.concatenate([x[:FRAME, :], edge[:FRAME]], axis=1)
-    bottom = jnp.concatenate([x[TH - FRAME :, :], edge[TH - FRAME :]], axis=1)
+    top = jnp.concatenate([x[0, :FRAME, :], edge[:FRAME]], axis=1)
+    bottom = jnp.concatenate([x[0, TH - FRAME :, :], edge[TH - FRAME :]], axis=1)
     even = lax.axis_index("ty") % 2 == 0
     send_first[...] = jnp.where(even, bottom, top)
     send_second[...] = jnp.where(even, top, bottom)
@@ -177,7 +169,7 @@
     column = (wh[...], wl[...])
     top, bottom = halos("ty", row_first[...], row_second[...])
     own = [
-        jnp.concatenate([x[rows, :], edge[rows, :]], axis=1)
+        jnp.concatenate([x[0, rows, :], edge[rows, :]], axis=1)
         for rows in (slice(0, STRIP), slice(TH - STRIP, TH))
     ]
     values = jnp.concatenate([top, own[0], own[1], bottom], axis=0)
@@ -207,23 +199,18 @@
     return pl.CostEstimate(flops=flops, bytes_accessed=2**12, transcendentals=0)
 
 
-def keep(array):
-    return pltpu.with_memory_space_constraint(array, pltpu.HBM)
-
-
-def lead_call(offsets, pick, raster):
+def weights_call(offsets, pick):
     column = bf16(2 * LANE, 2 * LANE)
     row = bf16(SPAN, 2 * DEPTH)
     return pl.pallas_call(
-        lead_kernel,
-        out_shape=(f32(LEAD, CORE), f32(TH, TW), column, column, row, row),
-        in_specs=[FAST, pl.BlockSpec(memory_space=pltpu.SMEM), SLOW],
-        out_specs=(FAST,) * 6,
-        scratch_shapes=[pltpu.SemaphoreType.DMA((2,))],
+        weights_kernel,
+        out_shape=(column, column, row, row),
+        in_specs=[FAST, pl.BlockSpec(memory_space=pltpu.SMEM)],
+        out_specs=(FAST,) * 4,
         compiler_params=LIMIT,
-        cost_estimate=cost(10**6),
-        name="lead",
-    )(offsets, pick, keep(raster))
+        cost_estimate=cost(4 * 10**8),
+        name="weights",
+    )(offsets, pick)
 
 
 def fast_call(kernel, name, out_shape, *operands):
@@ -323,20 +310,21 @@
 
 def body(raster, shift_pick, offsets):
     count = lax.axis_size("die")
-    lead, tile, *weights = lead_call(offsets, shift_pick, raster)
+    weights = weights_call(offsets, shift_pick)
+    lead = fast_call(lead_kernel, "lead", f32(LEAD, CORE), raster, *weights)
     lead_others = other_dies(lead)
     strip = f32(FRAME, TH)
-    rest, first, second = fast_call(rest_kernel, "rest", (f32(REST, CORE), strip, strip), tile, *weights)
+    rest, first, second = fast_call(rest_kernel, "rest", (f32(REST, CORE), strip, strip), raster, *weights)
     rest_others = other_dies(rest)
     first, second = swap_rounds("tx", first, second)
     halo = f32(FRAME, TW + LANE)
     side, send_first, send_second, edge = fast_call(
-        side_kernel, "side", (f32(MID, 2 * LANE), halo, halo, f32(TH, LANE)), tile, first, second, *weights
+        side_kernel, "side", (f32(MID, 2 * LANE), halo, halo, f32(TH, LANE)), raster, first, second, *weights
     )
     side_others = other_dies(side)
     row_first, row_second = swap_rounds("ty", send_first, send_second)
     frame = fast_call(
-        frame_kernel, "frame", f32(STRIP, TW), tile, edge, row_first, row_second, *weights
+        frame_kernel, "frame", f32(STRIP, TW), raster, edge, row_first, row_second, *weights
     )
     frame_others = other_dies(frame)
     maps = change_call(count, LEAD_PLACES, COSTS[0], lead, lead_others, ())

time: 30.3 us -> 29.8 us (0.983)
  Pallas kernels: 9.72 us -> 9.12 us
    pallas_call x1, Pallas kernels: 1.92 us -> 0.4 us  [weights_call(): pl.pallas_call(weights_kernel, out_shape=(column, column, row, row), in_s...]
    pallas_call x3 -> x4, Pallas kernels: 3.82 us -> 4.73 us  [fast_call(): pl.pallas_call(kernel, out_shape=out_shape, in_specs=[FAST] * len(operand...]
where the time goes in v6:
time: 29.8 us; the launch traced here: 29.6 us
  starting transfers between devices  10.1 us (34%)
  Pallas kernels  9.12 us (31%)
  waiting for transfers between devices  8.9 us (30%)
  between operations  1.46 us (5%)
    ppermute x4, waiting for transfers between devices, other_dies(): return (lax.ppermute(block, 'die', forward + backward),)  8.29 us
    ppermute x4, starting transfers between devices, other_dies(): return (lax.ppermute(block, 'die', forward + backward),)  6.67 us
    pallas_call x4, Pallas kernels, fast_call(): pl.pallas_call(kernel, out_shape=out_shape, in_specs=[FAST] * len(operand...  4.73 us
    pallas_call x4, Pallas kernels, change_call(): pl.pallas_call(functools.partial(change_kernel, places, count, fill), out...  3.98 us
    ppermute x2, starting transfers between devices, swap_rounds(): lax.ppermute(first, axis, pairs)  2.09 us
    ppermute x2, starting transfers between devices, swap_rounds(): lax.ppermute(second, axis, others)  1.32 us
    ppermute x2, waiting for transfers between devices, swap_rounds(): lax.ppermute(first, axis, pairs)  0.6 us
  transfers between devices with their start and end apart: 8, of which 5 were waited for; matrix products, arithmetic and copies ran while one was open for 0% of the time, Pallas kernels for 24%

profile of v6, /device:TPU:0, one launch (start us, length us, event | category | flops | bytes accessed | tf_op | source)
XLA Modules:
  0.0 29.6 jit_solution(8130382812909177029)
XLA Ops:
  0.6 0.0 copy-start.1
  0.6 0.0 copy-start
  1.4 0.0 copy-done.1
  1.4 0.4 %weights.1 = (bf16[256,256]{1,0:T(8,128)(2,1)S(1)}, bf16[256,256]{1,0:T(8,128)(2,1)S(1)}, bf16[96,256]{1,0:T(8,128)(2,1)S(1)}, bf16[96,256]{1,0:T(8,128)(2,1)S(1)}) custom-call(s32[1,1,1,2]{3,2,1,0:T(1,128)S(1)} %copy-done.1, s32[1,1,1]{2,1,0:T(1,128)S(6)} %copy.17.pick_ref), custom_call_target="tpu_custom_call" | custom-call | flops 400000000 | bytes 4096 | tf_op jit(solution)/shard_map/weights/pallas_call | solution.py:205
  1.8 0.1 copy-done
  1.9 0.9 %lead.1.own_ref = f32[64,768]{1,0:T(8,128)S(1)} custom-call(f32[1,256,1024]{2,1,0:T(8,128)S(1)} %copy-done, bf16[256,256]{1,0:T(8,128)(2,1)S(1)} %get-tuple-element.19.wh, bf16[256,256]{1,0:T(8,128)(2,1)S(1)} %get-tuple-element.20.wl, bf16[96,256]{1,0:T(8,128)(2,1)S(1)} %get-tuple-element.21.vh, bf16[96,256]{1,0:T(8,128)(2,1)S(1)} %get-tuple-element.22.vl), custom_call_target="tpu_custom_call" | custom-call | flops 1000000 | bytes 4096 | tf_op jit(solution)/shard_map/lead/pallas_call | solution.py:218
  2.8 3.0 %collective-permute-start.7 = (f32[64,768]{1,0:T(8,128)S(1)}, f32[64,768]{1,0:T(8,128)S(1)}, u32[]{:S(2)}, u32[]{:S(2)}) collective-permute-start(f32[64,768]{1,0:T(8,128)S(1)} %lead.1.own_ref), channel_id=1, source_target_pairs={{0,16},{16,0},{1,17},{17,1},{2,18},{18,2},{3,19},{19,3},{4,20},{20... | collective-permute-start | bytes 589832 | tf_op jit(solution)/shard_map/ppermute | solution.py:307
  5.8 1.6 %rest.1 = (f32[160,768]{1,0:T(8,128)S(1)}, f32[16,256]{1,0:T(8,128)S(1)}, f32[16,256]{1,0:T(8,128)S(1)}) custom-call(f32[1,256,1024]{2,1,0:T(8,128)S(1)} %copy-done, bf16[256,256]{1,0:T(8,128)(2,1)S(1)} %get-tuple-element.19.wh, bf16[256,256]{1,0:T(8,128)(2,1)S(1)} %get-tuple-element.20.wl, bf16[96,256]{1,0:T(8,128)(2,1)S(1)} %get-tuple-element.21.vh, ...), custom_call_target="tpu_custom_call" | custom-call | flops 1000000 | bytes 4096 | tf_op jit(solution)/shard_map/rest/pallas_call | solution.py:218
  7.5 0.1 collective-permute-start.6
  7.5 0.1 collective-permute-start
  7.6 0.7 %collective-permute-start.1 = (f32[16,256]{1,0:T(8,128)S(1)}, f32[16,256]{1,0:T(8,128)S(1)}, u32[]{:S(2)}, u32[]{:S(2)}) collective-permute-start(f32[16,256]{1,0:T(8,128)S(1)} %get-tuple-element.24), channel_id=1, source_target_pairs={{0,0},{1,2},{2,1},{3,3},{4,4},{5,6},{6,5},{7,7},{8,8},{9,10},{10,9... | collective-permute-start | bytes 49160 | tf_op jit(solution)/shard_map/ppermute | solution.py:299
  8.3 0.5 %collective-permute-done.first = f32[16,256]{1,0:T(8,128)S(1)} collective-permute-done((f32[16,256]{1,0:T(8,128)S(1)}, f32[16,256]{1,0:T(8,128)S(1)}, u32[]{:S(2)}, u32[]{:S(2)}) %collective-permute-start) | collective-permute-done | bytes 16416 | tf_op jit(solution)/shard_map/ppermute | solution.py:299
  8.8 0.0 collective-permute-done.1.second
  8.8 1.1 %side.1 = (f32[224,256]{1,0:T(8,128)S(1)}, f32[16,1152]{1,0:T(8,128)S(1)}, f32[16,1152]{1,0:T(8,128)S(1)}, f32[256,128]{1,0:T(8,128)S(1)}) custom-call(f32[1,256,1024]{2,1,0:T(8,128)S(1)} %copy-done, f32[16,256]{1,0:T(8,128)S(1)} %collective-permute-done.first, f32[16,256]{1,0:T(8,128)S(1)} %collective-permute-done.1.second, ...), custom_call_target="tpu_custom_call" | custom-call | flops 1000000 | bytes 4096 | tf_op jit(solution)/shard_map/side/pallas_call | solution.py:218
  9.9 2.0 %collective-permute-start.2 = (f32[16,1152]{1,0:T(8,128)S(1)}, f32[16,1152]{1,0:T(8,128)S(1)}, u32[]{:S(2)}, u32[]{:S(2)}) collective-permute-start(f32[16,1152]{1,0:T(8,128)S(1)} %get-tuple-element.26), channel_id=1, source_target_pairs={{0,4},{4,0},{8,12},{12,8},{1,5},{5,1},{9,13},{13,9},{2,6},{6,2},{1... | collective-permute-start | bytes 221192 | tf_op jit(solution)/shard_map/ppermute | solution.py:299
  11.9 0.7 %collective-permute-start.3 = (f32[16,1152]{1,0:T(8,128)S(1)}, f32[16,1152]{1,0:T(8,128)S(1)}, u32[]{:S(2)}, u32[]{:S(2)}) collective-permute-start(f32[16,1152]{1,0:T(8,128)S(1)} %get-tuple-element.27), channel_id=1, source_target_pairs={{0,0},{4,8},{8,4},{12,12},{1,1},{5,9},{9,5},{13,13},{2,2},{6,10},{... | collective-permute-start | bytes 221192 | tf_op jit(solution)/shard_map/ppermute | solution.py:299
  12.6 1.6 %collective-permute-start.5 = (f32[224,256]{1,0:T(8,128)S(1)}, f32[224,256]{1,0:T(8,128)S(1)}, u32[]{:S(2)}, u32[]{:S(2)}) collective-permute-start(f32[224,256]{1,0:T(8,128)S(1)} %get-tuple-element.28.own_ref), channel_id=1, source_target_pairs={{0,16},{16,0},{1,17},{17,1},{2,18},{18,2},{3,19},{19,3},{4,20},{20... | collective-permute-start | bytes 688136 | tf_op jit(solution)/shard_map/ppermute | solution.py:307
  14.2 0.1 collective-permute-done.2.row_first
  14.3 0.0 collective-permute-done.3.row_second
  14.3 1.1 %frame.1.own_ref = f32[32,1024]{1,0:T(8,128)S(1)} custom-call(f32[1,256,1024]{2,1,0:T(8,128)S(1)} %copy-done, f32[256,128]{1,0:T(8,128)S(1)} %get-tuple-element.25.edge, f32[16,1152]{1,0:T(8,128)S(1)} %collective-permute-done.2.row_first, f32[16,1152]{1,0:T(8,128)S(1)} %collective-permute-done.3.row_second, bf16[256,256]{1,0:T(8,128)(2,1)S(1)} %get-tuple-element.19.wh, ...), custom_call_target="tpu_custom_call" | custom-call | flops 1000000 | bytes 4096 | tf_op jit(solution)/shard_map/frame/pallas_call | solution.py:218
  15.3 2.0 %collective-permute-start.4 = (f32[32,1024]{1,0:T(8,128)S(1)}, f32[32,1024]{1,0:T(8,128)S(1)}, u32[]{:S(2)}, u32[]{:S(2)}) collective-permute-start(f32[32,1024]{1,0:T(8,128)S(1)} %frame.1.own_ref), channel_id=1, source_target_pairs={{0,16},{16,0},{1,17},{17,1},{2,18},{18,2},{3,19},{19,3},{4,20},{20... | collective-permute-start | bytes 393224 | tf_op jit(solution)/shard_map/ppermute | solution.py:307
  17.3 0.0 collective-permute-done.7.refs_0_
  17.3 1.7 %change.4 = (f32[1,256,1024]{2,1,0:T(8,128)}, f32[1,256,1024]{2,1,0:T(8,128)}) custom-call(f32[64,768]{1,0:T(8,128)S(1)} %lead.1.own_ref, f32[64,768]{1,0:T(8,128)S(1)} %collective-permute-done.7.refs_0_), custom_call_target="tpu_custom_call" | custom-call | flops 4000000000 | bytes 4096 | tf_op jit(solution)/shard_map/change/pallas_call | solution.py:271
  19.1 3.0 %collective-permute-done.6.refs_0_ = f32[160,768]{1,0:T(8,128)S(1)} collective-permute-done((f32[160,768]{1,0:T(8,128)S(1)}, f32[160,768]{1,0:T(8,128)S(1)}, u32[]{:S(2)}, u32[]{:S(2)}) %collective-permute-start.6) | collective-permute-done | bytes 491552 | tf_op jit(solution)/shard_map/ppermute | solution.py:307
  22.1 0.8 %change.5 = (f32[1,256,1024]{2,1,0:T(8,128)}, f32[1,256,1024]{2,1,0:T(8,128)}) custom-call(f32[160,768]{1,0:T(8,128)S(1)} %get-tuple-element.29.own_ref, f32[160,768]{1,0:T(8,128)S(1)} %collective-permute-done.6.refs_0_, f32[1,256,1024]{2,1,0:T(8,128)} %get-tuple-element.30.refs_1_, ...), custom_call_target="tpu_custom_call", output_to_operand_aliasing={{0}: (2, {}), {1}: (3, {})} | custom-call | flops 10000000000 | bytes 4096 | tf_op jit(solution)/shard_map/change/pallas_call | solution.py:271
  22.9 4.1 %collective-permute-done.5.refs_0_ = f32[224,256]{1,0:T(8,128)S(1)} collective-permute-done((f32[224,256]{1,0:T(8,128)S(1)}, f32[224,256]{1,0:T(8,128)S(1)}, u32[]{:S(2)}, u32[]{:S(2)}) %collective-permute-start.5) | collective-permute-done | bytes 229408 | tf_op jit(solution)/shard_map/ppermute | solution.py:307
  27.0 0.7 %change.6 = (f32[1,256,1024]{2,1,0:T(8,128)}, f32[1,256,1024]{2,1,0:T(8,128)}) custom-call(f32[224,256]{1,0:T(8,128)S(1)} %get-tuple-element.28.own_ref, f32[224,256]{1,0:T(8,128)S(1)} %collective-permute-done.5.refs_0_, f32[1,256,1024]{2,1,0:T(8,128)} %get-tuple-element.32.refs_1_, ...), custom_call_target="tpu_custom_call", output_to_operand_aliasing={{0}: (2, {}), {1}: (3, {})} | custom-call | flops 10000000000 | bytes 4096 | tf_op jit(solution)/shard_map/change/pallas_call | solution.py:271
  27.7 1.2 %collective-permute-done.4.refs_0_ = f32[32,1024]{1,0:T(8,128)S(1)} collective-permute-done((f32[32,1024]{1,0:T(8,128)S(1)}, f32[32,1024]{1,0:T(8,128)S(1)}, u32[]{:S(2)}, u32[]{:S(2)}) %collective-permute-start.4) | collective-permute-done | bytes 131104 | tf_op jit(solution)/shard_map/ppermute | solution.py:307
  29.0 0.7 %change.7 = (f32[1,256,1024]{2,1,0:T(8,128)}, f32[1,256,1024]{2,1,0:T(8,128)}) custom-call(f32[32,1024]{1,0:T(8,128)S(1)} %frame.1.own_ref, f32[32,1024]{1,0:T(8,128)S(1)} %collective-permute-done.4.refs_0_, f32[1,256,1024]{2,1,0:T(8,128)} %get-tuple-element.34.refs_1_, ...), custom_call_target="tpu_custom_call", output_to_operand_aliasing={{0}: (2, {}), {1}: (3, {})} | custom-call | flops 10000000000 | bytes 4096 | tf_op jit(solution)/shard_map/change/pallas_call | solution.py:271
Async XLA Ops:
  0.6 0.8 %copy-start.1 = (s32[1,1,1,2]{3,2,1,0:T(1,128)S(1)}, s32[1,1,1,2]{3,2,1,0:T(1,128)}, u32[]{:S(2)}) copy-start(s32[1,1,1,2]{3,2,1,0:T(1,128)} %off_ref.1) | copy-start | bytes 28
  0.6 1.2 %copy-start = (f32[1,256,1024]{2,1,0:T(8,128)S(1)}, f32[1,256,1024]{2,1,0:T(8,128)}, u32[]{:S(2)}) copy-start(f32[1,256,1024]{2,1,0:T(8,128)} %x.7) | copy-start | bytes 3145732
  2.8 14.5 %collective-permute-start.7 = (f32[64,768]{1,0:T(8,128)S(1)}, f32[64,768]{1,0:T(8,128)S(1)}, u32[]{:S(2)}, u32[]{:S(2)}) collective-permute-start(f32[64,768]{1,0:T(8,128)S(1)} %lead.1.own_ref), channel_id=1, source_target_pairs={{0,16},{16,0},{1,17},{17,1},{2,18},{18,2},{3,19},{19,3},{4,20},{20... | collective-permute-start | bytes 589832 | tf_op jit(solution)/shard_map/ppermute | solution.py:307
  7.5 14.6 %collective-permute-start.6 = (f32[160,768]{1,0:T(8,128)S(1)}, f32[160,768]{1,0:T(8,128)S(1)}, u32[]{:S(2)}, u32[]{:S(2)}) collective-permute-start(f32[160,768]{1,0:T(8,128)S(1)} %get-tuple-element.29.own_ref), channel_id=1, source_target_pairs={{0,16},{16,0},{1,17},{17,1},{2,18},{18,2},{3,19},{19,3},{4,20},{20... | collective-permute-start | bytes 1474568 | tf_op jit(solution)/shard_map/ppermute | solution.py:307
  7.5 1.2 %collective-permute-start = (f32[16,256]{1,0:T(8,128)S(1)}, f32[16,256]{1,0:T(8,128)S(1)}, u32[]{:S(2)}, u32[]{:S(2)}) collective-permute-start(f32[16,256]{1,0:T(8,128)S(1)} %get-tuple-element.23), channel_id=1, source_target_pairs={{0,1},{1,0},{2,3},{3,2},{4,5},{5,4},{6,7},{7,6},{8,9},{9,8},{10,11... | collective-permute-start | bytes 49160 | tf_op jit(solution)/shard_map/ppermute | solution.py:299
  7.6 1.2 %collective-permute-start.1 = (f32[16,256]{1,0:T(8,128)S(1)}, f32[16,256]{1,0:T(8,128)S(1)}, u32[]{:S(2)}, u32[]{:S(2)}) collective-permute-start(f32[16,256]{1,0:T(8,128)S(1)} %get-tuple-element.24), channel_id=1, source_target_pairs={{0,0},{1,2},{2,1},{3,3},{4,4},{5,6},{6,5},{7,7},{8,8},{9,10},{10,9... | collective-permute-start | bytes 49160 | tf_op jit(solution)/shard_map/ppermute | solution.py:299
  9.9 4.4 %collective-permute-start.2 = (f32[16,1152]{1,0:T(8,128)S(1)}, f32[16,1152]{1,0:T(8,128)S(1)}, u32[]{:S(2)}, u32[]{:S(2)}) collective-permute-start(f32[16,1152]{1,0:T(8,128)S(1)} %get-tuple-element.26), channel_id=1, source_target_pairs={{0,4},{4,0},{8,12},{12,8},{1,5},{5,1},{9,13},{13,9},{2,6},{6,2},{1... | collective-permute-start | bytes 221192 | tf_op jit(solution)/shard_map/ppermute | solution.py:299
  11.9 2.3 %collective-permute-start.3 = (f32[16,1152]{1,0:T(8,128)S(1)}, f32[16,1152]{1,0:T(8,128)S(1)}, u32[]{:S(2)}, u32[]{:S(2)}) collective-permute-start(f32[16,1152]{1,0:T(8,128)S(1)} %get-tuple-element.27), channel_id=1, source_target_pairs={{0,0},{4,8},{8,4},{12,12},{1,1},{5,9},{9,5},{13,13},{2,2},{6,10},{... | collective-permute-start | bytes 221192 | tf_op jit(solution)/shard_map/ppermute | solution.py:299
  12.6 14.4 %collective-permute-start.5 = (f32[224,256]{1,0:T(8,128)S(1)}, f32[224,256]{1,0:T(8,128)S(1)}, u32[]{:S(2)}, u32[]{:S(2)}) collective-permute-start(f32[224,256]{1,0:T(8,128)S(1)} %get-tuple-element.28.own_ref), channel_id=1, source_target_pairs={{0,16},{16,0},{1,17},{17,1},{2,18},{18,2},{3,19},{19,3},{4,20},{20... | collective-permute-start | bytes 688136 | tf_op jit(solution)/shard_map/ppermute | solution.py:307
  15.3 13.6 %collective-permute-start.4 = (f32[32,1024]{1,0:T(8,128)S(1)}, f32[32,1024]{1,0:T(8,128)S(1)}, u32[]{:S(2)}, u32[]{:S(2)}) collective-permute-start(f32[32,1024]{1,0:T(8,128)S(1)} %frame.1.own_ref), channel_id=1, source_target_pairs={{0,16},{16,0},{1,17},{17,1},{2,18},{18,2},{3,19},{19,3},{4,20},{20... | collective-permute-start | bytes 393224 | tf_op jit(solution)/shard_map/ppermute | solution.py:307

commit v7 on v6

--- a/solution.py
+++ b/solution.py
@@ -19,7 +19,7 @@
 SPAN = 96
 DEPTH = SPAN + 2 * FRAME
 MID = TH - 2 * FRAME
-LEAD = 64
+LEAD = 48
 REST = MID - LEAD
 REACH = LANE + 2 * FRAME
 BF16 = jnp.bfloat16
@@ -101,8 +101,8 @@
     return product(row, stacked)
 
 
-def core_windows(values):
-    rolled = pltpu.roll(values, HW, 1)
+def core_windows(values, level):
+    rolled = pltpu.roll(values - level, HW, 1)
     return [rolled[:, block * LANE : (block + 2) * LANE] for block in range(1, TW // LANE - 1)]
 
 
@@ -113,12 +113,15 @@
     vh[...], vl[...] = row_weights(offsets[:, :1], pick)
 
 
-def lead_kernel(x, wh, wl, vh, vl, lead):
-    sums = column_sums(core_windows(x[0, : LEAD + 2 * FRAME, :]), (wh[...], wl[...]))
+def lead_kernel(x, wh, wl, vh, vl, lead, level_ref):
+    total = jnp.sum(jnp.sum(x[0, :8, :], axis=0, keepdims=True), axis=1, keepdims=True)
+    level = total * (1.0 / (8 * TW))
+    level_ref[...] = jnp.broadcast_to(level, level_ref.shape)
+    sums = column_sums(core_windows(x[0, : LEAD + 2 * FRAME, :], level), (wh[...], wl[...]))
     lead[...] = row_sums([half[:LEAD, :] for half in (vh, vl)], sums)
 
 
-def rest_kernel(x, wh, wl, vh, vl, rest, first, second):
+def rest_kernel(x, level_ref, wh, wl, vh, vl, rest, first, second):
     even = lax.axis_index("tx") % 2 == 0
     start = x[0, :, :LANE].T[:FRAME]
     end = x[0, :, TW - LANE :].T[LANE - FRAME :]
@@ -126,7 +129,7 @@
     second[...] = jnp.where(even, start, end)
     column = (wh[...], wl[...])
     row = (vh[...], vl[...])
-    sums = column_sums(core_windows(x[0, LEAD:, :]), column)
+    sums = column_sums(core_windows(x[0, LEAD:, :], level_ref[:1, :1]), column)
     rest[:SPAN, :] = row_sums(row, sums)
     last = REST - SPAN
     lower = [half[SPAN - last :] for half in row]
@@ -141,7 +144,7 @@
     return jnp.where(even, second, first), jnp.where(even, first, second)
 
 
-def side_kernel(x, first, second, wh, wl, vh, vl, side, send_first, send_second, edge_ref):
+def side_kernel(x, level_ref, first, second, wh, wl, vh, vl, side, send_first, send_second, edge_ref):
     column = (wh[...], wl[...])
     row = (vh[...], vl[...])
     before, after = halos("tx", first[...], second[...])
@@ -149,7 +152,7 @@
     edge = jnp.concatenate([after, filler, before], axis=0).T
     edge_ref[...] = edge
     windows = [
-        pltpu.roll(jnp.concatenate(strip, axis=1), 2 * LANE + HW, 1)[:, : 2 * LANE]
+        pltpu.roll(jnp.concatenate(strip, axis=1) - level_ref[:1, :1], 2 * LANE + HW, 1)[:, : 2 * LANE]
         for strip in ((edge, x[0, :, : 2 * LANE]), (x[0, :, TW - 2 * LANE :], edge))
     ]
     sums = column_sums(windows, column)
@@ -165,7 +168,7 @@
     send_second[...] = jnp.where(even, top, bottom)
 
 
-def frame_kernel(x, edge, row_first, row_second, wh, wl, vh, vl, frame):
+def frame_kernel(x, level_ref, edge, row_first, row_second, wh, wl, vh, vl, frame):
     column = (wh[...], wl[...])
     top, bottom = halos("ty", row_first[...], row_second[...])
     own = [
@@ -173,7 +176,7 @@
         for rows in (slice(0, STRIP), slice(TH - STRIP, TH))
     ]
     values = jnp.concatenate([top, own[0], own[1], bottom], axis=0)
-    rolled = pltpu.roll(values, HW, 1)
+    rolled = pltpu.roll(values - level_ref[:1, :1], HW, 1)
     windows = [rolled[:, block * LANE : (block + 2) * LANE] for block in range(TW // LANE)]
     sums = column_sums(windows, column)
     below = values.shape[0] // 2
@@ -181,7 +184,7 @@
     frame[...] = row_sums(row, sums)
 
 
-COSTS = (4 * 10**9, 10**10, 10**10, 10**10)
+COSTS = (44 * 10**8, 10**10, 10**10, 10**10)
 FAST = pl.BlockSpec(memory_space=pltpu.VMEM)
 SLOW = pl.BlockSpec(memory_space=pltpu.HBM)
 LIMIT = pltpu.CompilerParams(vmem_limit_bytes=16 * 2**20)
@@ -311,20 +314,20 @@
 def body(raster, shift_pick, offsets):
     count = lax.axis_size("die")
     weights = weights_call(offsets, shift_pick)
-    lead = fast_call(lead_kernel, "lead", f32(LEAD, CORE), raster, *weights)
+    lead, level = fast_call(lead_kernel, "lead", (f32(LEAD, CORE), f32(8, LANE)), raster, *weights)
     lead_others = other_dies(lead)
     strip = f32(FRAME, TH)
-    rest, first, second = fast_call(rest_kernel, "rest", (f32(REST, CORE), strip, strip), raster, *weights)
+    rest, first, second = fast_call(rest_kernel, "rest", (f32(REST, CORE), strip, strip), raster, level, *weights)
     rest_others = other_dies(rest)
     first, second = swap_rounds("tx", first, second)
     halo = f32(FRAME, TW + LANE)
     side, send_first, send_second, edge = fast_call(
-        side_kernel, "side", (f32(MID, 2 * LANE), halo, halo, f32(TH, LANE)), raster, first, second, *weights
+        side_kernel, "side", (f32(MID, 2 * LANE), halo, halo, f32(TH, LANE)), raster, level, first, second, *weights
     )
     side_others = other_dies(side)
     row_first, row_second = swap_rounds("ty", send_first, send_second)
     frame = fast_call(
-        frame_kernel, "frame", f32(STRIP, TW), raster, edge, row_first, row_second, *weights
+        frame_kernel, "frame", f32(STRIP, TW), raster, level, edge, row_first, row_second, *weights
     )
     frame_others = other_dies(frame)
     maps = change_call(count, LEAD_PLACES, COSTS[0], lead, lead_others, ())

time: 29.8 us -> 29.9 us (level)
  no operation moved by 1% of the time
where the time goes in v7:
time: 29.9 us; the launch traced here: 29.7 us
  starting transfers between devices  10.1 us (34%)
  Pallas kernels  9.18 us (31%)
  waiting for transfers between devices  8.9 us (30%)
  between operations  1.46 us (5%)
    ppermute x4, waiting for transfers between devices, other_dies(): return (lax.ppermute(block, 'die', forward + backward),)  8.28 us
    ppermute x4, starting transfers between devices, other_dies(): return (lax.ppermute(block, 'die', forward + backward),)  6.64 us
    pallas_call x4, Pallas kernels, fast_call(): pl.pallas_call(kernel, out_shape=out_shape, in_specs=[FAST] * len(operand...  4.79 us
    pallas_call x4, Pallas kernels, change_call(): pl.pallas_call(functools.partial(change_kernel, places, count, fill), out...  3.99 us
    ppermute x2, starting transfers between devices, swap_rounds(): lax.ppermute(first, axis, pairs)  2.11 us
    ppermute x2, starting transfers between devices, swap_rounds(): lax.ppermute(second, axis, others)  1.32 us
    ppermute x2, waiting for transfers between devices, swap_rounds(): lax.ppermute(first, axis, pairs)  0.61 us
  transfers between devices with their start and end apart: 8, of which 5 were waited for; matrix products, arithmetic and copies ran while one was open for 0% of the time, Pallas kernels for 24%

profile of v7, /device:TPU:0, one launch (start us, length us, event | category | flops | bytes accessed | tf_op | source)
XLA Modules:
  0.0 29.7 jit_solution(3736293060565284690)
XLA Ops:
  0.6 0.0 copy-start.1
  0.6 0.0 copy-start
  1.4 0.0 copy-done.1
  1.4 0.4 %weights.1 = (bf16[256,256]{1,0:T(8,128)(2,1)S(1)}, bf16[256,256]{1,0:T(8,128)(2,1)S(1)}, bf16[96,256]{1,0:T(8,128)(2,1)S(1)}, bf16[96,256]{1,0:T(8,128)(2,1)S(1)}) custom-call(s32[1,1,1,2]{3,2,1,0:T(1,128)S(1)} %copy-done.1, s32[1,1,1]{2,1,0:T(1,128)S(6)} %copy.17.pick_ref), custom_call_target="tpu_custom_call" | custom-call | flops 400000000 | bytes 4096 | tf_op jit(solution)/shard_map/weights/pallas_call | solution.py:208
  1.8 0.1 copy-done
  1.9 0.9 %lead.1 = (f32[48,768]{1,0:T(8,128)S(1)}, f32[8,128]{1,0:T(8,128)S(1)}) custom-call(f32[1,256,1024]{2,1,0:T(8,128)S(1)} %copy-done, bf16[256,256]{1,0:T(8,128)(2,1)S(1)} %get-tuple-element.21.wh, bf16[256,256]{1,0:T(8,128)(2,1)S(1)} %get-tuple-element.22.wl, bf16[96,256]{1,0:T(8,128)(2,1)S(1)} %get-tuple-element.23.vh, bf16[96,256]{1,0:T(8,128)(2,1)S(1)} %get-tuple-element.24.vl), custom_call_target="tpu_custom_call" | custom-call | flops 1000000 | bytes 4096 | tf_op jit(solution)/shard_map/lead/pallas_call | solution.py:221
  2.8 3.0 %collective-permute-start.7 = (f32[48,768]{1,0:T(8,128)S(1)}, f32[48,768]{1,0:T(8,128)S(1)}, u32[]{:S(2)}, u32[]{:S(2)}) collective-permute-start(f32[48,768]{1,0:T(8,128)S(1)} %get-tuple-element.33.own_ref), channel_id=1, source_target_pairs={{0,16},{16,0},{1,17},{17,1},{2,18},{18,2},{3,19},{19,3},{4,20},{20... | collective-permute-start | bytes 442376 | tf_op jit(solution)/shard_map/ppermute | solution.py:310
  5.8 1.7 %rest.1 = (f32[176,768]{1,0:T(8,128)S(1)}, f32[16,256]{1,0:T(8,128)S(1)}, f32[16,256]{1,0:T(8,128)S(1)}) custom-call(f32[1,256,1024]{2,1,0:T(8,128)S(1)} %copy-done, f32[8,128]{1,0:T(8,128)S(1)} %get-tuple-element.25.level_ref, bf16[256,256]{1,0:T(8,128)(2,1)S(1)} %get-tuple-element.21.wh, bf16[256,256]{1,0:T(8,128)(2,1)S(1)} %get-tuple-element.22.wl, ...), custom_call_target="tpu_custom_call" | custom-call | flops 1000000 | bytes 4096 | tf_op jit(solution)/shard_map/rest/pallas_call | solution.py:221
  7.5 0.1 collective-permute-start.6
  7.6 0.1 collective-permute-start
  7.7 0.7 %collective-permute-start.1 = (f32[16,256]{1,0:T(8,128)S(1)}, f32[16,256]{1,0:T(8,128)S(1)}, u32[]{:S(2)}, u32[]{:S(2)}) collective-permute-start(f32[16,256]{1,0:T(8,128)S(1)} %get-tuple-element.27), channel_id=1, source_target_pairs={{0,0},{1,2},{2,1},{3,3},{4,4},{5,6},{6,5},{7,7},{8,8},{9,10},{10,9... | collective-permute-start | bytes 49160 | tf_op jit(solution)/shard_map/ppermute | solution.py:302
  8.3 0.5 %collective-permute-done.first = f32[16,256]{1,0:T(8,128)S(1)} collective-permute-done((f32[16,256]{1,0:T(8,128)S(1)}, f32[16,256]{1,0:T(8,128)S(1)}, u32[]{:S(2)}, u32[]{:S(2)}) %collective-permute-start) | collective-permute-done | bytes 16416 | tf_op jit(solution)/shard_map/ppermute | solution.py:302
  8.8 0.0 collective-permute-done.1.second
  8.8 1.1 %side.1 = (f32[224,256]{1,0:T(8,128)S(1)}, f32[16,1152]{1,0:T(8,128)S(1)}, f32[16,1152]{1,0:T(8,128)S(1)}, f32[256,128]{1,0:T(8,128)S(1)}) custom-call(f32[1,256,1024]{2,1,0:T(8,128)S(1)} %copy-done, f32[8,128]{1,0:T(8,128)S(1)} %get-tuple-element.25.level_ref, f32[16,256]{1,0:T(8,128)S(1)} %collective-permute-done.first, ...), custom_call_target="tpu_custom_call" | custom-call | flops 1000000 | bytes 4096 | tf_op jit(solution)/shard_map/side/pallas_call | solution.py:221
  9.9 2.0 %collective-permute-start.2 = (f32[16,1152]{1,0:T(8,128)S(1)}, f32[16,1152]{1,0:T(8,128)S(1)}, u32[]{:S(2)}, u32[]{:S(2)}) collective-permute-start(f32[16,1152]{1,0:T(8,128)S(1)} %get-tuple-element.29), channel_id=1, source_target_pairs={{0,4},{4,0},{8,12},{12,8},{1,5},{5,1},{9,13},{13,9},{2,6},{6,2},{1... | collective-permute-start | bytes 221192 | tf_op jit(solution)/shard_map/ppermute | solution.py:302
  12.0 0.7 %collective-permute-start.3 = (f32[16,1152]{1,0:T(8,128)S(1)}, f32[16,1152]{1,0:T(8,128)S(1)}, u32[]{:S(2)}, u32[]{:S(2)}) collective-permute-start(f32[16,1152]{1,0:T(8,128)S(1)} %get-tuple-element.30), channel_id=1, source_target_pairs={{0,0},{4,8},{8,4},{12,12},{1,1},{5,9},{9,5},{13,13},{2,2},{6,10},{... | collective-permute-start | bytes 221192 | tf_op jit(solution)/shard_map/ppermute | solution.py:302
  12.6 1.6 %collective-permute-start.5 = (f32[224,256]{1,0:T(8,128)S(1)}, f32[224,256]{1,0:T(8,128)S(1)}, u32[]{:S(2)}, u32[]{:S(2)}) collective-permute-start(f32[224,256]{1,0:T(8,128)S(1)} %get-tuple-element.31.own_ref), channel_id=1, source_target_pairs={{0,16},{16,0},{1,17},{17,1},{2,18},{18,2},{3,19},{19,3},{4,20},{20... | collective-permute-start | bytes 688136 | tf_op jit(solution)/shard_map/ppermute | solution.py:310
  14.2 0.1 collective-permute-done.2.row_first
  14.3 0.0 collective-permute-done.3.row_second
  14.3 1.1 %frame.1.own_ref = f32[32,1024]{1,0:T(8,128)S(1)} custom-call(f32[1,256,1024]{2,1,0:T(8,128)S(1)} %copy-done, f32[8,128]{1,0:T(8,128)S(1)} %get-tuple-element.25.level_ref, f32[256,128]{1,0:T(8,128)S(1)} %get-tuple-element.28.edge, f32[16,1152]{1,0:T(8,128)S(1)} %collective-permute-done.2.row_first, f32[16,1152]{1,0:T(8,128)S(1)} %collective-permute-done.3.row_second, ...), custom_call_target="tpu_custom_call" | custom-call | flops 1000000 | bytes 4096 | tf_op jit(solution)/shard_map/frame/pallas_call | solution.py:221
  15.4 2.0 %collective-permute-start.4 = (f32[32,1024]{1,0:T(8,128)S(1)}, f32[32,1024]{1,0:T(8,128)S(1)}, u32[]{:S(2)}, u32[]{:S(2)}) collective-permute-start(f32[32,1024]{1,0:T(8,128)S(1)} %frame.1.own_ref), channel_id=1, source_target_pairs={{0,16},{16,0},{1,17},{17,1},{2,18},{18,2},{3,19},{19,3},{4,20},{20... | collective-permute-start | bytes 393224 | tf_op jit(solution)/shard_map/ppermute | solution.py:310
  17.4 0.0 collective-permute-done.7.refs_0_
  17.4 1.7 %change.4 = (f32[1,256,1024]{2,1,0:T(8,128)}, f32[1,256,1024]{2,1,0:T(8,128)}) custom-call(f32[48,768]{1,0:T(8,128)S(1)} %get-tuple-element.33.own_ref, f32[48,768]{1,0:T(8,128)S(1)} %collective-permute-done.7.refs_0_), custom_call_target="tpu_custom_call" | custom-call | flops 4400000000 | bytes 4096 | tf_op jit(solution)/shard_map/change/pallas_call | solution.py:274
  19.1 3.6 %collective-permute-done.6.refs_0_ = f32[176,768]{1,0:T(8,128)S(1)} collective-permute-done((f32[176,768]{1,0:T(8,128)S(1)}, f32[176,768]{1,0:T(8,128)S(1)}, u32[]{:S(2)}, u32[]{:S(2)}) %collective-permute-start.6) | collective-permute-done | bytes 540704 | tf_op jit(solution)/shard_map/ppermute | solution.py:310
  22.8 0.9 %change.5 = (f32[1,256,1024]{2,1,0:T(8,128)}, f32[1,256,1024]{2,1,0:T(8,128)}) custom-call(f32[176,768]{1,0:T(8,128)S(1)} %get-tuple-element.32.own_ref, f32[176,768]{1,0:T(8,128)S(1)} %collective-permute-done.6.refs_0_, f32[1,256,1024]{2,1,0:T(8,128)} %get-tuple-element.34.refs_1_, ...), custom_call_target="tpu_custom_call", output_to_operand_aliasing={{0}: (2, {}), {1}: (3, {})} | custom-call | flops 10000000000 | bytes 4096 | tf_op jit(solution)/shard_map/change/pallas_call | solution.py:274
  23.6 4.0 %collective-permute-done.5.refs_0_ = f32[224,256]{1,0:T(8,128)S(1)} collective-permute-done((f32[224,256]{1,0:T(8,128)S(1)}, f32[224,256]{1,0:T(8,128)S(1)}, u32[]{:S(2)}, u32[]{:S(2)}) %collective-permute-start.5) | collective-permute-done | bytes 229408 | tf_op jit(solution)/shard_map/ppermute | solution.py:310
  27.6 0.7 %change.6 = (f32[1,256,1024]{2,1,0:T(8,128)}, f32[1,256,1024]{2,1,0:T(8,128)}) custom-call(f32[224,256]{1,0:T(8,128)S(1)} %get-tuple-element.31.own_ref, f32[224,256]{1,0:T(8,128)S(1)} %collective-permute-done.5.refs_0_, f32[1,256,1024]{2,1,0:T(8,128)} %get-tuple-element.36.refs_1_, ...), custom_call_target="tpu_custom_call", output_to_operand_aliasing={{0}: (2, {}), {1}: (3, {})} | custom-call | flops 10000000000 | bytes 4096 | tf_op jit(solution)/shard_map/change/pallas_call | solution.py:274
  28.3 0.7 %collective-permute-done.4.refs_0_ = f32[32,1024]{1,0:T(8,128)S(1)} collective-permute-done((f32[32,1024]{1,0:T(8,128)S(1)}, f32[32,1024]{1,0:T(8,128)S(1)}, u32[]{:S(2)}, u32[]{:S(2)}) %collective-permute-start.4) | collective-permute-done | bytes 131104 | tf_op jit(solution)/shard_map/ppermute | solution.py:310
  29.0 0.7 %change.7 = (f32[1,256,1024]{2,1,0:T(8,128)}, f32[1,256,1024]{2,1,0:T(8,128)}) custom-call(f32[32,1024]{1,0:T(8,128)S(1)} %frame.1.own_ref, f32[32,1024]{1,0:T(8,128)S(1)} %collective-permute-done.4.refs_0_, f32[1,256,1024]{2,1,0:T(8,128)} %get-tuple-element.38.refs_1_, ...), custom_call_target="tpu_custom_call", output_to_operand_aliasing={{0}: (2, {}), {1}: (3, {})} | custom-call | flops 10000000000 | bytes 4096 | tf_op jit(solution)/shard_map/change/pallas_call | solution.py:274
Async XLA Ops:
  0.6 0.8 %copy-start.1 = (s32[1,1,1,2]{3,2,1,0:T(1,128)S(1)}, s32[1,1,1,2]{3,2,1,0:T(1,128)}, u32[]{:S(2)}) copy-start(s32[1,1,1,2]{3,2,1,0:T(1,128)} %off_ref.1) | copy-start | bytes 28
  0.6 1.2 %copy-start = (f32[1,256,1024]{2,1,0:T(8,128)S(1)}, f32[1,256,1024]{2,1,0:T(8,128)}, u32[]{:S(2)}) copy-start(f32[1,256,1024]{2,1,0:T(8,128)} %x.7) | copy-start | bytes 3145732
  2.8 14.6 %collective-permute-start.7 = (f32[48,768]{1,0:T(8,128)S(1)}, f32[48,768]{1,0:T(8,128)S(1)}, u32[]{:S(2)}, u32[]{:S(2)}) collective-permute-start(f32[48,768]{1,0:T(8,128)S(1)} %get-tuple-element.33.own_ref), channel_id=1, source_target_pairs={{0,16},{16,0},{1,17},{17,1},{2,18},{18,2},{3,19},{19,3},{4,20},{20... | collective-permute-start | bytes 442376 | tf_op jit(solution)/shard_map/ppermute | solution.py:310
  7.5 15.3 %collective-permute-start.6 = (f32[176,768]{1,0:T(8,128)S(1)}, f32[176,768]{1,0:T(8,128)S(1)}, u32[]{:S(2)}, u32[]{:S(2)}) collective-permute-start(f32[176,768]{1,0:T(8,128)S(1)} %get-tuple-element.32.own_ref), channel_id=1, source_target_pairs={{0,16},{16,0},{1,17},{17,1},{2,18},{18,2},{3,19},{19,3},{4,20},{20... | collective-permute-start | bytes 1622024 | tf_op jit(solution)/shard_map/ppermute | solution.py:310
  7.6 1.2 %collective-permute-start = (f32[16,256]{1,0:T(8,128)S(1)}, f32[16,256]{1,0:T(8,128)S(1)}, u32[]{:S(2)}, u32[]{:S(2)}) collective-permute-start(f32[16,256]{1,0:T(8,128)S(1)} %get-tuple-element.26), channel_id=1, source_target_pairs={{0,1},{1,0},{2,3},{3,2},{4,5},{5,4},{6,7},{7,6},{8,9},{9,8},{10,11... | collective-permute-start | bytes 49160 | tf_op jit(solution)/shard_map/ppermute | solution.py:302
  7.7 1.2 %collective-permute-start.1 = (f32[16,256]{1,0:T(8,128)S(1)}, f32[16,256]{1,0:T(8,128)S(1)}, u32[]{:S(2)}, u32[]{:S(2)}) collective-permute-start(f32[16,256]{1,0:T(8,128)S(1)} %get-tuple-element.27), channel_id=1, source_target_pairs={{0,0},{1,2},{2,1},{3,3},{4,4},{5,6},{6,5},{7,7},{8,8},{9,10},{10,9... | collective-permute-start | bytes 49160 | tf_op jit(solution)/shard_map/ppermute | solution.py:302
  9.9 4.4 %collective-permute-start.2 = (f32[16,1152]{1,0:T(8,128)S(1)}, f32[16,1152]{1,0:T(8,128)S(1)}, u32[]{:S(2)}, u32[]{:S(2)}) collective-permute-start(f32[16,1152]{1,0:T(8,128)S(1)} %get-tuple-element.29), channel_id=1, source_target_pairs={{0,4},{4,0},{8,12},{12,8},{1,5},{5,1},{9,13},{13,9},{2,6},{6,2},{1... | collective-permute-start | bytes 221192 | tf_op jit(solution)/shard_map/ppermute | solution.py:302
  12.0 2.3 %collective-permute-start.3 = (f32[16,1152]{1,0:T(8,128)S(1)}, f32[16,1152]{1,0:T(8,128)S(1)}, u32[]{:S(2)}, u32[]{:S(2)}) collective-permute-start(f32[16,1152]{1,0:T(8,128)S(1)} %get-tuple-element.30), channel_id=1, source_target_pairs={{0,0},{4,8},{8,4},{12,12},{1,1},{5,9},{9,5},{13,13},{2,2},{6,10},{... | collective-permute-start | bytes 221192 | tf_op jit(solution)/shard_map/ppermute | solution.py:302
  12.6 15.0 %collective-permute-start.5 = (f32[224,256]{1,0:T(8,128)S(1)}, f32[224,256]{1,0:T(8,128)S(1)}, u32[]{:S(2)}, u32[]{:S(2)}) collective-permute-start(f32[224,256]{1,0:T(8,128)S(1)} %get-tuple-element.31.own_ref), channel_id=1, source_target_pairs={{0,16},{16,0},{1,17},{17,1},{2,18},{18,2},{3,19},{19,3},{4,20},{20... | collective-permute-start | bytes 688136 | tf_op jit(solution)/shard_map/ppermute | solution.py:310
  15.4 13.6 %collective-permute-start.4 = (f32[32,1024]{1,0:T(8,128)S(1)}, f32[32,1024]{1,0:T(8,128)S(1)}, u32[]{:S(2)}, u32[]{:S(2)}) collective-permute-start(f32[32,1024]{1,0:T(8,128)S(1)} %frame.1.own_ref), channel_id=1, source_target_pairs={{0,16},{16,0},{1,17},{17,1},{2,18},{18,2},{3,19},{19,3},{4,20},{20... | collective-permute-start | bytes 393224 | tf_op jit(solution)/shard_map/ppermute | solution.py:310

commit v8 on v7

--- a/solution.py
+++ b/solution.py
@@ -19,7 +19,7 @@
 SPAN = 96
 DEPTH = SPAN + 2 * FRAME
 MID = TH - 2 * FRAME
-LEAD = 48
+LEAD = 96
 REST = MID - LEAD
 REACH = LANE + 2 * FRAME
 BF16 = jnp.bfloat16
@@ -184,7 +184,7 @@
     frame[...] = row_sums(row, sums)
 
 
-COSTS = (44 * 10**8, 10**10, 10**10, 10**10)
+COSTS = (25 * 10**8, 10**10, 10**10, 10**10)
 FAST = pl.BlockSpec(memory_space=pltpu.VMEM)
 SLOW = pl.BlockSpec(memory_space=pltpu.HBM)
 LIMIT = pltpu.CompilerParams(vmem_limit_bytes=16 * 2**20)

time: 29.9 us -> 30 us (level)
  no operation moved by 1% of the time
where the time goes in v8:
time: 30 us; the launch traced here: 29.9 us
  starting transfers between devices  10 us (33%)
  Pallas kernels  9.31 us (31%)
  waiting for transfers between devices  8.97 us (30%)
  between operations  1.46 us (5%)
    ppermute x4, waiting for transfers between devices, other_dies(): return (lax.ppermute(block, 'die', forward + backward),)  8.35 us
    ppermute x4, starting transfers between devices, other_dies(): return (lax.ppermute(block, 'die', forward + backward),)  6.62 us
    pallas_call x4, Pallas kernels, fast_call(): pl.pallas_call(kernel, out_shape=out_shape, in_specs=[FAST] * len(operand...  4.89 us
    pallas_call x4, Pallas kernels, change_call(): pl.pallas_call(functools.partial(change_kernel, places, count, fill), out...  4.01 us
    ppermute x2, starting transfers between devices, swap_rounds(): lax.ppermute(first, axis, pairs)  2.11 us
    ppermute x2, starting transfers between devices, swap_rounds(): lax.ppermute(second, axis, others)  1.32 us
    ppermute x2, waiting for transfers between devices, swap_rounds(): lax.ppermute(first, axis, pairs)  0.61 us
  transfers between devices with their start and end apart: 8, of which 5 were waited for; matrix products, arithmetic and copies ran while one was open for 0% of the time, Pallas kernels for 24%

profile of v8, /device:TPU:0, one launch (start us, length us, event | category | flops | bytes accessed | tf_op | source)
XLA Modules:
  0.0 29.9 jit_solution(2689052107170632873)
XLA Ops:
  0.6 0.0 copy-start.1
  0.6 0.0 copy-start
  1.4 0.0 copy-done.1
  1.4 0.4 %weights.1 = (bf16[256,256]{1,0:T(8,128)(2,1)S(1)}, bf16[256,256]{1,0:T(8,128)(2,1)S(1)}, bf16[96,256]{1,0:T(8,128)(2,1)S(1)}, bf16[96,256]{1,0:T(8,128)(2,1)S(1)}) custom-call(s32[1,1,1,2]{3,2,1,0:T(1,128)S(1)} %copy-done.1, s32[1,1,1]{2,1,0:T(1,128)S(6)} %copy.17.pick_ref), custom_call_target="tpu_custom_call" | custom-call | flops 400000000 | bytes 4096 | tf_op jit(solution)/shard_map/weights/pallas_call | solution.py:208
  1.8 0.1 copy-done
  1.9 1.1 %lead.1 = (f32[96,768]{1,0:T(8,128)S(1)}, f32[8,128]{1,0:T(8,128)S(1)}) custom-call(f32[1,256,1024]{2,1,0:T(8,128)S(1)} %copy-done, bf16[256,256]{1,0:T(8,128)(2,1)S(1)} %get-tuple-element.21.wh, bf16[256,256]{1,0:T(8,128)(2,1)S(1)} %get-tuple-element.22.wl, bf16[96,256]{1,0:T(8,128)(2,1)S(1)} %get-tuple-element.23.vh, bf16[96,256]{1,0:T(8,128)(2,1)S(1)} %get-tuple-element.24.vl), custom_call_target="tpu_custom_call" | custom-call | flops 1000000 | bytes 4096 | tf_op jit(solution)/shard_map/lead/pallas_call | solution.py:221
  3.0 3.0 %collective-permute-start.7 = (f32[96,768]{1,0:T(8,128)S(1)}, f32[96,768]{1,0:T(8,128)S(1)}, u32[]{:S(2)}, u32[]{:S(2)}) collective-permute-start(f32[96,768]{1,0:T(8,128)S(1)} %get-tuple-element.33.own_ref), channel_id=1, source_target_pairs={{0,16},{16,0},{1,17},{17,1},{2,18},{18,2},{3,19},{19,3},{4,20},{20... | collective-permute-start | bytes 884744 | tf_op jit(solution)/shard_map/ppermute | solution.py:310
  6.0 1.6 %rest.1 = (f32[128,768]{1,0:T(8,128)S(1)}, f32[16,256]{1,0:T(8,128)S(1)}, f32[16,256]{1,0:T(8,128)S(1)}) custom-call(f32[1,256,1024]{2,1,0:T(8,128)S(1)} %copy-done, f32[8,128]{1,0:T(8,128)S(1)} %get-tuple-element.25.level_ref, bf16[256,256]{1,0:T(8,128)(2,1)S(1)} %get-tuple-element.21.wh, bf16[256,256]{1,0:T(8,128)(2,1)S(1)} %get-tuple-element.22.wl, ...), custom_call_target="tpu_custom_call" | custom-call | flops 1000000 | bytes 4096 | tf_op jit(solution)/shard_map/rest/pallas_call | solution.py:221
  7.6 0.1 collective-permute-start.6
  7.7 0.1 collective-permute-start
  7.7 0.7 %collective-permute-start.1 = (f32[16,256]{1,0:T(8,128)S(1)}, f32[16,256]{1,0:T(8,128)S(1)}, u32[]{:S(2)}, u32[]{:S(2)}) collective-permute-start(f32[16,256]{1,0:T(8,128)S(1)} %get-tuple-element.27), channel_id=1, source_target_pairs={{0,0},{1,2},{2,1},{3,3},{4,4},{5,6},{6,5},{7,7},{8,8},{9,10},{10,9... | collective-permute-start | bytes 49160 | tf_op jit(solution)/shard_map/ppermute | solution.py:302
  8.4 0.5 %collective-permute-done.first = f32[16,256]{1,0:T(8,128)S(1)} collective-permute-done((f32[16,256]{1,0:T(8,128)S(1)}, f32[16,256]{1,0:T(8,128)S(1)}, u32[]{:S(2)}, u32[]{:S(2)}) %collective-permute-start) | collective-permute-done | bytes 16416 | tf_op jit(solution)/shard_map/ppermute | solution.py:302
  8.9 0.0 collective-permute-done.1.second
  8.9 1.1 %side.1 = (f32[224,256]{1,0:T(8,128)S(1)}, f32[16,1152]{1,0:T(8,128)S(1)}, f32[16,1152]{1,0:T(8,128)S(1)}, f32[256,128]{1,0:T(8,128)S(1)}) custom-call(f32[1,256,1024]{2,1,0:T(8,128)S(1)} %copy-done, f32[8,128]{1,0:T(8,128)S(1)} %get-tuple-element.25.level_ref, f32[16,256]{1,0:T(8,128)S(1)} %collective-permute-done.first, ...), custom_call_target="tpu_custom_call" | custom-call | flops 1000000 | bytes 4096 | tf_op jit(solution)/shard_map/side/pallas_call | solution.py:221
  10.0 2.0 %collective-permute-start.2 = (f32[16,1152]{1,0:T(8,128)S(1)}, f32[16,1152]{1,0:T(8,128)S(1)}, u32[]{:S(2)}, u32[]{:S(2)}) collective-permute-start(f32[16,1152]{1,0:T(8,128)S(1)} %get-tuple-element.29), channel_id=1, source_target_pairs={{0,4},{4,0},{8,12},{12,8},{1,5},{5,1},{9,13},{13,9},{2,6},{6,2},{1... | collective-permute-start | bytes 221192 | tf_op jit(solution)/shard_map/ppermute | solution.py:302
  12.1 0.7 %collective-permute-start.3 = (f32[16,1152]{1,0:T(8,128)S(1)}, f32[16,1152]{1,0:T(8,128)S(1)}, u32[]{:S(2)}, u32[]{:S(2)}) collective-permute-start(f32[16,1152]{1,0:T(8,128)S(1)} %get-tuple-element.30), channel_id=1, source_target_pairs={{0,0},{4,8},{8,4},{12,12},{1,1},{5,9},{9,5},{13,13},{2,2},{6,10},{... | collective-permute-start | bytes 221192 | tf_op jit(solution)/shard_map/ppermute | solution.py:302
  12.7 1.6 %collective-permute-start.5 = (f32[224,256]{1,0:T(8,128)S(1)}, f32[224,256]{1,0:T(8,128)S(1)}, u32[]{:S(2)}, u32[]{:S(2)}) collective-permute-start(f32[224,256]{1,0:T(8,128)S(1)} %get-tuple-element.31.own_ref), channel_id=1, source_target_pairs={{0,16},{16,0},{1,17},{17,1},{2,18},{18,2},{3,19},{19,3},{4,20},{20... | collective-permute-start | bytes 688136 | tf_op jit(solution)/shard_map/ppermute | solution.py:310
  14.3 0.1 collective-permute-done.2.row_first
  14.4 0.0 collective-permute-done.3.row_second
  14.4 1.1 %frame.1.own_ref = f32[32,1024]{1,0:T(8,128)S(1)} custom-call(f32[1,256,1024]{2,1,0:T(8,128)S(1)} %copy-done, f32[8,128]{1,0:T(8,128)S(1)} %get-tuple-element.25.level_ref, f32[256,128]{1,0:T(8,128)S(1)} %get-tuple-element.28.edge, f32[16,1152]{1,0:T(8,128)S(1)} %collective-permute-done.2.row_first, f32[16,1152]{1,0:T(8,128)S(1)} %collective-permute-done.3.row_second, ...), custom_call_target="tpu_custom_call" | custom-call | flops 1000000 | bytes 4096 | tf_op jit(solution)/shard_map/frame/pallas_call | solution.py:221
  15.5 2.0 %collective-permute-start.4 = (f32[32,1024]{1,0:T(8,128)S(1)}, f32[32,1024]{1,0:T(8,128)S(1)}, u32[]{:S(2)}, u32[]{:S(2)}) collective-permute-start(f32[32,1024]{1,0:T(8,128)S(1)} %frame.1.own_ref), channel_id=1, source_target_pairs={{0,16},{16,0},{1,17},{17,1},{2,18},{18,2},{3,19},{19,3},{4,20},{20... | collective-permute-start | bytes 393224 | tf_op jit(solution)/shard_map/ppermute | solution.py:310
  17.5 0.0 collective-permute-done.7.refs_0_
  17.5 1.8 %change.4 = (f32[1,256,1024]{2,1,0:T(8,128)}, f32[1,256,1024]{2,1,0:T(8,128)}) custom-call(f32[96,768]{1,0:T(8,128)S(1)} %get-tuple-element.33.own_ref, f32[96,768]{1,0:T(8,128)S(1)} %collective-permute-done.7.refs_0_), custom_call_target="tpu_custom_call" | custom-call | flops 2500000000 | bytes 4096 | tf_op jit(solution)/shard_map/change/pallas_call | solution.py:274
  19.3 3.0 %collective-permute-done.6.refs_0_ = f32[128,768]{1,0:T(8,128)S(1)} collective-permute-done((f32[128,768]{1,0:T(8,128)S(1)}, f32[128,768]{1,0:T(8,128)S(1)}, u32[]{:S(2)}, u32[]{:S(2)}) %collective-permute-start.6) | collective-permute-done | bytes 393248 | tf_op jit(solution)/shard_map/ppermute | solution.py:310
  22.3 0.8 %change.5 = (f32[1,256,1024]{2,1,0:T(8,128)}, f32[1,256,1024]{2,1,0:T(8,128)}) custom-call(f32[128,768]{1,0:T(8,128)S(1)} %get-tuple-element.32.own_ref, f32[128,768]{1,0:T(8,128)S(1)} %collective-permute-done.6.refs_0_, f32[1,256,1024]{2,1,0:T(8,128)} %get-tuple-element.34.refs_1_, ...), custom_call_target="tpu_custom_call", output_to_operand_aliasing={{0}: (2, {}), {1}: (3, {})} | custom-call | flops 10000000000 | bytes 4096 | tf_op jit(solution)/shard_map/change/pallas_call | solution.py:274
  23.1 4.1 %collective-permute-done.5.refs_0_ = f32[224,256]{1,0:T(8,128)S(1)} collective-permute-done((f32[224,256]{1,0:T(8,128)S(1)}, f32[224,256]{1,0:T(8,128)S(1)}, u32[]{:S(2)}, u32[]{:S(2)}) %collective-permute-start.5) | collective-permute-done | bytes 229408 | tf_op jit(solution)/shard_map/ppermute | solution.py:310
  27.2 0.7 %change.6 = (f32[1,256,1024]{2,1,0:T(8,128)}, f32[1,256,1024]{2,1,0:T(8,128)}) custom-call(f32[224,256]{1,0:T(8,128)S(1)} %get-tuple-element.31.own_ref, f32[224,256]{1,0:T(8,128)S(1)} %collective-permute-done.5.refs_0_, f32[1,256,1024]{2,1,0:T(8,128)} %get-tuple-element.36.refs_1_, ...), custom_call_target="tpu_custom_call", output_to_operand_aliasing={{0}: (2, {}), {1}: (3, {})} | custom-call | flops 10000000000 | bytes 4096 | tf_op jit(solution)/shard_map/change/pallas_call | solution.py:274
  28.0 1.2 %collective-permute-done.4.refs_0_ = f32[32,1024]{1,0:T(8,128)S(1)} collective-permute-done((f32[32,1024]{1,0:T(8,128)S(1)}, f32[32,1024]{1,0:T(8,128)S(1)}, u32[]{:S(2)}, u32[]{:S(2)}) %collective-permute-start.4) | collective-permute-done | bytes 131104 | tf_op jit(solution)/shard_map/ppermute | solution.py:310
  29.2 0.7 %change.7 = (f32[1,256,1024]{2,1,0:T(8,128)}, f32[1,256,1024]{2,1,0:T(8,128)}) custom-call(f32[32,1024]{1,0:T(8,128)S(1)} %frame.1.own_ref, f32[32,1024]{1,0:T(8,128)S(1)} %collective-permute-done.4.refs_0_, f32[1,256,1024]{2,1,0:T(8,128)} %get-tuple-element.38.refs_1_, ...), custom_call_target="tpu_custom_call", output_to_operand_aliasing={{0}: (2, {}), {1}: (3, {})} | custom-call | flops 10000000000 | bytes 4096 | tf_op jit(solution)/shard_map/change/pallas_call | solution.py:274
Async XLA Ops:
  0.6 0.8 %copy-start.1 = (s32[1,1,1,2]{3,2,1,0:T(1,128)S(1)}, s32[1,1,1,2]{3,2,1,0:T(1,128)}, u32[]{:S(2)}) copy-start(s32[1,1,1,2]{3,2,1,0:T(1,128)} %off_ref.1) | copy-start | bytes 28
  0.6 1.2 %copy-start = (f32[1,256,1024]{2,1,0:T(8,128)S(1)}, f32[1,256,1024]{2,1,0:T(8,128)}, u32[]{:S(2)}) copy-start(f32[1,256,1024]{2,1,0:T(8,128)} %x.7) | copy-start | bytes 3145732
  3.0 14.5 %collective-permute-start.7 = (f32[96,768]{1,0:T(8,128)S(1)}, f32[96,768]{1,0:T(8,128)S(1)}, u32[]{:S(2)}, u32[]{:S(2)}) collective-permute-start(f32[96,768]{1,0:T(8,128)S(1)} %get-tuple-element.33.own_ref), channel_id=1, source_target_pairs={{0,16},{16,0},{1,17},{17,1},{2,18},{18,2},{3,19},{19,3},{4,20},{20... | collective-permute-start | bytes 884744 | tf_op jit(solution)/shard_map/ppermute | solution.py:310
  7.6 14.7 %collective-permute-start.6 = (f32[128,768]{1,0:T(8,128)S(1)}, f32[128,768]{1,0:T(8,128)S(1)}, u32[]{:S(2)}, u32[]{:S(2)}) collective-permute-start(f32[128,768]{1,0:T(8,128)S(1)} %get-tuple-element.32.own_ref), channel_id=1, source_target_pairs={{0,16},{16,0},{1,17},{17,1},{2,18},{18,2},{3,19},{19,3},{4,20},{20... | collective-permute-start | bytes 1179656 | tf_op jit(solution)/shard_map/ppermute | solution.py:310
  7.7 1.2 %collective-permute-start = (f32[16,256]{1,0:T(8,128)S(1)}, f32[16,256]{1,0:T(8,128)S(1)}, u32[]{:S(2)}, u32[]{:S(2)}) collective-permute-start(f32[16,256]{1,0:T(8,128)S(1)} %get-tuple-element.26), channel_id=1, source_target_pairs={{0,1},{1,0},{2,3},{3,2},{4,5},{5,4},{6,7},{7,6},{8,9},{9,8},{10,11... | collective-permute-start | bytes 49160 | tf_op jit(solution)/shard_map/ppermute | solution.py:302
  7.7 1.2 %collective-permute-start.1 = (f32[16,256]{1,0:T(8,128)S(1)}, f32[16,256]{1,0:T(8,128)S(1)}, u32[]{:S(2)}, u32[]{:S(2)}) collective-permute-start(f32[16,256]{1,0:T(8,128)S(1)} %get-tuple-element.27), channel_id=1, source_target_pairs={{0,0},{1,2},{2,1},{3,3},{4,4},{5,6},{6,5},{7,7},{8,8},{9,10},{10,9... | collective-permute-start | bytes 49160 | tf_op jit(solution)/shard_map/ppermute | solution.py:302
  10.0 4.4 %collective-permute-start.2 = (f32[16,1152]{1,0:T(8,128)S(1)}, f32[16,1152]{1,0:T(8,128)S(1)}, u32[]{:S(2)}, u32[]{:S(2)}) collective-permute-start(f32[16,1152]{1,0:T(8,128)S(1)} %get-tuple-element.29), channel_id=1, source_target_pairs={{0,4},{4,0},{8,12},{12,8},{1,5},{5,1},{9,13},{13,9},{2,6},{6,2},{1... | collective-permute-start | bytes 221192 | tf_op jit(solution)/shard_map/ppermute | solution.py:302
  12.1 2.3 %collective-permute-start.3 = (f32[16,1152]{1,0:T(8,128)S(1)}, f32[16,1152]{1,0:T(8,128)S(1)}, u32[]{:S(2)}, u32[]{:S(2)}) collective-permute-start(f32[16,1152]{1,0:T(8,128)S(1)} %get-tuple-element.30), channel_id=1, source_target_pairs={{0,0},{4,8},{8,4},{12,12},{1,1},{5,9},{9,5},{13,13},{2,2},{6,10},{... | collective-permute-start | bytes 221192 | tf_op jit(solution)/shard_map/ppermute | solution.py:302
  12.7 14.5 %collective-permute-start.5 = (f32[224,256]{1,0:T(8,128)S(1)}, f32[224,256]{1,0:T(8,128)S(1)}, u32[]{:S(2)}, u32[]{:S(2)}) collective-permute-start(f32[224,256]{1,0:T(8,128)S(1)} %get-tuple-element.31.own_ref), channel_id=1, source_target_pairs={{0,16},{16,0},{1,17},{17,1},{2,18},{18,2},{3,19},{19,3},{4,20},{20... | collective-permute-start | bytes 688136 | tf_op jit(solution)/shard_map/ppermute | solution.py:310
  15.5 13.7 %collective-permute-start.4 = (f32[32,1024]{1,0:T(8,128)S(1)}, f32[32,1024]{1,0:T(8,128)S(1)}, u32[]{:S(2)}, u32[]{:S(2)}) collective-permute-start(f32[32,1024]{1,0:T(8,128)S(1)} %frame.1.own_ref), channel_id=1, source_target_pairs={{0,16},{16,0},{1,17},{17,1},{2,18},{18,2},{3,19},{19,3},{4,20},{20... | collective-permute-start | bytes 393224 | tf_op jit(solution)/shard_map/ppermute | solution.py:310

commit v9 on v7

--- a/solution.py
+++ b/solution.py
@@ -117,8 +117,12 @@
     total = jnp.sum(jnp.sum(x[0, :8, :], axis=0, keepdims=True), axis=1, keepdims=True)
     level = total * (1.0 / (8 * TW))
     level_ref[...] = jnp.broadcast_to(level, level_ref.shape)
-    sums = column_sums(core_windows(x[0, : LEAD + 2 * FRAME, :], level), (wh[...], wl[...]))
-    lead[...] = row_sums([half[:LEAD, :] for half in (vh, vl)], sums)
+    windows = core_windows(x[0, : LEAD + 2 * FRAME, :], level)
+    column = (wh[...], wl[...])
+    row = [half[:LEAD, :] for half in (vh, vl)]
+    for group in range(0, len(windows), 2):
+        spot = pl.ds(group * LANE, 2 * LANE)
+        lead[:, spot] = row_sums(row, column_sums(windows[group : group + 2], column))
 
 
 def rest_kernel(x, level_ref, wh, wl, vh, vl, rest, first, second):

time: 29.9 us -> 30 us (level)
  no operation moved by 1% of the time
where the time goes in v9:
time: 30 us; the launch traced here: 29.8 us
  starting transfers between devices  10 us (33%)
  Pallas kernels  9.35 us (31%)
  waiting for transfers between devices  8.9 us (30%)
  between operations  1.46 us (5%)
    ppermute x4, waiting for transfers between devices, other_dies(): return (lax.ppermute(block, 'die', forward + backward),)  8.28 us
    ppermute x4, starting transfers between devices, other_dies(): return (lax.ppermute(block, 'die', forward + backward),)  6.58 us
    pallas_call x4, Pallas kernels, fast_call(): pl.pallas_call(kernel, out_shape=out_shape, in_specs=[FAST] * len(operand...  4.96 us
    pallas_call x4, Pallas kernels, change_call(): pl.pallas_call(functools.partial(change_kernel, places, count, fill), out...  3.99 us
    ppermute x2, starting transfers between devices, swap_rounds(): lax.ppermute(first, axis, pairs)  2.11 us
    ppermute x2, starting transfers between devices, swap_rounds(): lax.ppermute(second, axis, others)  1.32 us
    ppermute x2, waiting for transfers between devices, swap_rounds(): lax.ppermute(first, axis, pairs)  0.61 us
  transfers between devices with their start and end apart: 8, of which 5 were waited for; matrix products, arithmetic and copies ran while one was open for 0% of the time, Pallas kernels for 24%

profile of v9, /device:TPU:0, one launch (start us, length us, event | category | flops | bytes accessed | tf_op | source)
XLA Modules:
  0.0 29.8 jit_solution(4045571224274324188)
XLA Ops:
  0.6 0.0 copy-start.1
  0.6 0.0 copy-start
  1.4 0.0 copy-done.1
  1.4 0.4 %weights.1 = (bf16[256,256]{1,0:T(8,128)(2,1)S(1)}, bf16[256,256]{1,0:T(8,128)(2,1)S(1)}, bf16[96,256]{1,0:T(8,128)(2,1)S(1)}, bf16[96,256]{1,0:T(8,128)(2,1)S(1)}) custom-call(s32[1,1,1,2]{3,2,1,0:T(1,128)S(1)} %copy-done.1, s32[1,1,1]{2,1,0:T(1,128)S(6)} %copy.17.pick_ref), custom_call_target="tpu_custom_call" | custom-call | flops 400000000 | bytes 4096 | tf_op jit(solution)/shard_map/weights/pallas_call | solution.py:212
  1.8 0.1 copy-done
  1.9 1.1 %lead.1 = (f32[48,768]{1,0:T(8,128)S(1)}, f32[8,128]{1,0:T(8,128)S(1)}) custom-call(f32[1,256,1024]{2,1,0:T(8,128)S(1)} %copy-done, bf16[256,256]{1,0:T(8,128)(2,1)S(1)} %get-tuple-element.21.wh, bf16[256,256]{1,0:T(8,128)(2,1)S(1)} %get-tuple-element.22.wl, bf16[96,256]{1,0:T(8,128)(2,1)S(1)} %get-tuple-element.23.vh, bf16[96,256]{1,0:T(8,128)(2,1)S(1)} %get-tuple-element.24.vl), custom_call_target="tpu_custom_call" | custom-call | flops 1000000 | bytes 4096 | tf_op jit(solution)/shard_map/lead/pallas_call | solution.py:225
  3.0 3.0 %collective-permute-start.7 = (f32[48,768]{1,0:T(8,128)S(1)}, f32[48,768]{1,0:T(8,128)S(1)}, u32[]{:S(2)}, u32[]{:S(2)}) collective-permute-start(f32[48,768]{1,0:T(8,128)S(1)} %get-tuple-element.33.own_ref), channel_id=1, source_target_pairs={{0,16},{16,0},{1,17},{17,1},{2,18},{18,2},{3,19},{19,3},{4,20},{20... | collective-permute-start | bytes 442376 | tf_op jit(solution)/shard_map/ppermute | solution.py:314
  5.9 1.7 %rest.1 = (f32[176,768]{1,0:T(8,128)S(1)}, f32[16,256]{1,0:T(8,128)S(1)}, f32[16,256]{1,0:T(8,128)S(1)}) custom-call(f32[1,256,1024]{2,1,0:T(8,128)S(1)} %copy-done, f32[8,128]{1,0:T(8,128)S(1)} %get-tuple-element.25.level_ref, bf16[256,256]{1,0:T(8,128)(2,1)S(1)} %get-tuple-element.21.wh, bf16[256,256]{1,0:T(8,128)(2,1)S(1)} %get-tuple-element.22.wl, ...), custom_call_target="tpu_custom_call" | custom-call | flops 1000000 | bytes 4096 | tf_op jit(solution)/shard_map/rest/pallas_call | solution.py:225
  7.6 0.1 collective-permute-start.6
  7.7 0.1 collective-permute-start
  7.8 0.7 %collective-permute-start.1 = (f32[16,256]{1,0:T(8,128)S(1)}, f32[16,256]{1,0:T(8,128)S(1)}, u32[]{:S(2)}, u32[]{:S(2)}) collective-permute-start(f32[16,256]{1,0:T(8,128)S(1)} %get-tuple-element.27), channel_id=1, source_target_pairs={{0,0},{1,2},{2,1},{3,3},{4,4},{5,6},{6,5},{7,7},{8,8},{9,10},{10,9... | collective-permute-start | bytes 49160 | tf_op jit(solution)/shard_map/ppermute | solution.py:306
  8.4 0.5 %collective-permute-done.first = f32[16,256]{1,0:T(8,128)S(1)} collective-permute-done((f32[16,256]{1,0:T(8,128)S(1)}, f32[16,256]{1,0:T(8,128)S(1)}, u32[]{:S(2)}, u32[]{:S(2)}) %collective-permute-start) | collective-permute-done | bytes 16416 | tf_op jit(solution)/shard_map/ppermute | solution.py:306
  8.9 0.0 collective-permute-done.1.second
  8.9 1.1 %side.1 = (f32[224,256]{1,0:T(8,128)S(1)}, f32[16,1152]{1,0:T(8,128)S(1)}, f32[16,1152]{1,0:T(8,128)S(1)}, f32[256,128]{1,0:T(8,128)S(1)}) custom-call(f32[1,256,1024]{2,1,0:T(8,128)S(1)} %copy-done, f32[8,128]{1,0:T(8,128)S(1)} %get-tuple-element.25.level_ref, f32[16,256]{1,0:T(8,128)S(1)} %collective-permute-done.first, ...), custom_call_target="tpu_custom_call" | custom-call | flops 1000000 | bytes 4096 | tf_op jit(solution)/shard_map/side/pallas_call | solution.py:225
  10.1 2.0 %collective-permute-start.2 = (f32[16,1152]{1,0:T(8,128)S(1)}, f32[16,1152]{1,0:T(8,128)S(1)}, u32[]{:S(2)}, u32[]{:S(2)}) collective-permute-start(f32[16,1152]{1,0:T(8,128)S(1)} %get-tuple-element.29), channel_id=1, source_target_pairs={{0,4},{4,0},{8,12},{12,8},{1,5},{5,1},{9,13},{13,9},{2,6},{6,2},{1... | collective-permute-start | bytes 221192 | tf_op jit(solution)/shard_map/ppermute | solution.py:306
  12.1 0.7 %collective-permute-start.3 = (f32[16,1152]{1,0:T(8,128)S(1)}, f32[16,1152]{1,0:T(8,128)S(1)}, u32[]{:S(2)}, u32[]{:S(2)}) collective-permute-start(f32[16,1152]{1,0:T(8,128)S(1)} %get-tuple-element.30), channel_id=1, source_target_pairs={{0,0},{4,8},{8,4},{12,12},{1,1},{5,9},{9,5},{13,13},{2,2},{6,10},{... | collective-permute-start | bytes 221192 | tf_op jit(solution)/shard_map/ppermute | solution.py:306
  12.8 1.6 %collective-permute-start.5 = (f32[224,256]{1,0:T(8,128)S(1)}, f32[224,256]{1,0:T(8,128)S(1)}, u32[]{:S(2)}, u32[]{:S(2)}) collective-permute-start(f32[224,256]{1,0:T(8,128)S(1)} %get-tuple-element.31.own_ref), channel_id=1, source_target_pairs={{0,16},{16,0},{1,17},{17,1},{2,18},{18,2},{3,19},{19,3},{4,20},{20... | collective-permute-start | bytes 688136 | tf_op jit(solution)/shard_map/ppermute | solution.py:314
  14.3 0.1 collective-permute-done.2.row_first
  14.4 0.0 collective-permute-done.3.row_second
  14.4 1.1 %frame.1.own_ref = f32[32,1024]{1,0:T(8,128)S(1)} custom-call(f32[1,256,1024]{2,1,0:T(8,128)S(1)} %copy-done, f32[8,128]{1,0:T(8,128)S(1)} %get-tuple-element.25.level_ref, f32[256,128]{1,0:T(8,128)S(1)} %get-tuple-element.28.edge, f32[16,1152]{1,0:T(8,128)S(1)} %collective-permute-done.2.row_first, f32[16,1152]{1,0:T(8,128)S(1)} %collective-permute-done.3.row_second, ...), custom_call_target="tpu_custom_call" | custom-call | flops 1000000 | bytes 4096 | tf_op jit(solution)/shard_map/frame/pallas_call | solution.py:225
  15.5 2.0 %collective-permute-start.4 = (f32[32,1024]{1,0:T(8,128)S(1)}, f32[32,1024]{1,0:T(8,128)S(1)}, u32[]{:S(2)}, u32[]{:S(2)}) collective-permute-start(f32[32,1024]{1,0:T(8,128)S(1)} %frame.1.own_ref), channel_id=1, source_target_pairs={{0,16},{16,0},{1,17},{17,1},{2,18},{18,2},{3,19},{19,3},{4,20},{20... | collective-permute-start | bytes 393224 | tf_op jit(solution)/shard_map/ppermute | solution.py:314
  17.5 0.0 collective-permute-done.7.refs_0_
  17.5 1.7 %change.4 = (f32[1,256,1024]{2,1,0:T(8,128)}, f32[1,256,1024]{2,1,0:T(8,128)}) custom-call(f32[48,768]{1,0:T(8,128)S(1)} %get-tuple-element.33.own_ref, f32[48,768]{1,0:T(8,128)S(1)} %collective-permute-done.7.refs_0_), custom_call_target="tpu_custom_call" | custom-call | flops 4400000000 | bytes 4096 | tf_op jit(solution)/shard_map/change/pallas_call | solution.py:278
  19.2 3.6 %collective-permute-done.6.refs_0_ = f32[176,768]{1,0:T(8,128)S(1)} collective-permute-done((f32[176,768]{1,0:T(8,128)S(1)}, f32[176,768]{1,0:T(8,128)S(1)}, u32[]{:S(2)}, u32[]{:S(2)}) %collective-permute-start.6) | collective-permute-done | bytes 540704 | tf_op jit(solution)/shard_map/ppermute | solution.py:314
  22.9 0.9 %change.5 = (f32[1,256,1024]{2,1,0:T(8,128)}, f32[1,256,1024]{2,1,0:T(8,128)}) custom-call(f32[176,768]{1,0:T(8,128)S(1)} %get-tuple-element.32.own_ref, f32[176,768]{1,0:T(8,128)S(1)} %collective-permute-done.6.refs_0_, f32[1,256,1024]{2,1,0:T(8,128)} %get-tuple-element.34.refs_1_, ...), custom_call_target="tpu_custom_call", output_to_operand_aliasing={{0}: (2, {}), {1}: (3, {})} | custom-call | flops 10000000000 | bytes 4096 | tf_op jit(solution)/shard_map/change/pallas_call | solution.py:278
  23.7 4.0 %collective-permute-done.5.refs_0_ = f32[224,256]{1,0:T(8,128)S(1)} collective-permute-done((f32[224,256]{1,0:T(8,128)S(1)}, f32[224,256]{1,0:T(8,128)S(1)}, u32[]{:S(2)}, u32[]{:S(2)}) %collective-permute-start.5) | collective-permute-done | bytes 229408 | tf_op jit(solution)/shard_map/ppermute | solution.py:314
  27.7 0.7 %change.6 = (f32[1,256,1024]{2,1,0:T(8,128)}, f32[1,256,1024]{2,1,0:T(8,128)}) custom-call(f32[224,256]{1,0:T(8,128)S(1)} %get-tuple-element.31.own_ref, f32[224,256]{1,0:T(8,128)S(1)} %collective-permute-done.5.refs_0_, f32[1,256,1024]{2,1,0:T(8,128)} %get-tuple-element.36.refs_1_, ...), custom_call_target="tpu_custom_call", output_to_operand_aliasing={{0}: (2, {}), {1}: (3, {})} | custom-call | flops 10000000000 | bytes 4096 | tf_op jit(solution)/shard_map/change/pallas_call | solution.py:278
  28.5 0.7 %collective-permute-done.4.refs_0_ = f32[32,1024]{1,0:T(8,128)S(1)} collective-permute-done((f32[32,1024]{1,0:T(8,128)S(1)}, f32[32,1024]{1,0:T(8,128)S(1)}, u32[]{:S(2)}, u32[]{:S(2)}) %collective-permute-start.4) | collective-permute-done | bytes 131104 | tf_op jit(solution)/shard_map/ppermute | solution.py:314
  29.1 0.7 %change.7 = (f32[1,256,1024]{2,1,0:T(8,128)}, f32[1,256,1024]{2,1,0:T(8,128)}) custom-call(f32[32,1024]{1,0:T(8,128)S(1)} %frame.1.own_ref, f32[32,1024]{1,0:T(8,128)S(1)} %collective-permute-done.4.refs_0_, f32[1,256,1024]{2,1,0:T(8,128)} %get-tuple-element.38.refs_1_, ...), custom_call_target="tpu_custom_call", output_to_operand_aliasing={{0}: (2, {}), {1}: (3, {})} | custom-call | flops 10000000000 | bytes 4096 | tf_op jit(solution)/shard_map/change/pallas_call | solution.py:278
Async XLA Ops:
  0.6 0.8 %copy-start.1 = (s32[1,1,1,2]{3,2,1,0:T(1,128)S(1)}, s32[1,1,1,2]{3,2,1,0:T(1,128)}, u32[]{:S(2)}) copy-start(s32[1,1,1,2]{3,2,1,0:T(1,128)} %off_ref.1) | copy-start | bytes 28
  0.6 1.2 %copy-start = (f32[1,256,1024]{2,1,0:T(8,128)S(1)}, f32[1,256,1024]{2,1,0:T(8,128)}, u32[]{:S(2)}) copy-start(f32[1,256,1024]{2,1,0:T(8,128)} %x.7) | copy-start | bytes 3145732
  3.0 14.6 %collective-permute-start.7 = (f32[48,768]{1,0:T(8,128)S(1)}, f32[48,768]{1,0:T(8,128)S(1)}, u32[]{:S(2)}, u32[]{:S(2)}) collective-permute-start(f32[48,768]{1,0:T(8,128)S(1)} %get-tuple-element.33.own_ref), channel_id=1, source_target_pairs={{0,16},{16,0},{1,17},{17,1},{2,18},{18,2},{3,19},{19,3},{4,20},{20... | collective-permute-start | bytes 442376 | tf_op jit(solution)/shard_map/ppermute | solution.py:314
  7.6 15.3 %collective-permute-start.6 = (f32[176,768]{1,0:T(8,128)S(1)}, f32[176,768]{1,0:T(8,128)S(1)}, u32[]{:S(2)}, u32[]{:S(2)}) collective-permute-start(f32[176,768]{1,0:T(8,128)S(1)} %get-tuple-element.32.own_ref), channel_id=1, source_target_pairs={{0,16},{16,0},{1,17},{17,1},{2,18},{18,2},{3,19},{19,3},{4,20},{20... | collective-permute-start | bytes 1622024 | tf_op jit(solution)/shard_map/ppermute | solution.py:314
  7.7 1.2 %collective-permute-start = (f32[16,256]{1,0:T(8,128)S(1)}, f32[16,256]{1,0:T(8,128)S(1)}, u32[]{:S(2)}, u32[]{:S(2)}) collective-permute-start(f32[16,256]{1,0:T(8,128)S(1)} %get-tuple-element.26), channel_id=1, source_target_pairs={{0,1},{1,0},{2,3},{3,2},{4,5},{5,4},{6,7},{7,6},{8,9},{9,8},{10,11... | collective-permute-start | bytes 49160 | tf_op jit(solution)/shard_map/ppermute | solution.py:306
  7.8 1.2 %collective-permute-start.1 = (f32[16,256]{1,0:T(8,128)S(1)}, f32[16,256]{1,0:T(8,128)S(1)}, u32[]{:S(2)}, u32[]{:S(2)}) collective-permute-start(f32[16,256]{1,0:T(8,128)S(1)} %get-tuple-element.27), channel_id=1, source_target_pairs={{0,0},{1,2},{2,1},{3,3},{4,4},{5,6},{6,5},{7,7},{8,8},{9,10},{10,9... | collective-permute-start | bytes 49160 | tf_op jit(solution)/shard_map/ppermute | solution.py:306
  10.1 4.4 %collective-permute-start.2 = (f32[16,1152]{1,0:T(8,128)S(1)}, f32[16,1152]{1,0:T(8,128)S(1)}, u32[]{:S(2)}, u32[]{:S(2)}) collective-permute-start(f32[16,1152]{1,0:T(8,128)S(1)} %get-tuple-element.29), channel_id=1, source_target_pairs={{0,4},{4,0},{8,12},{12,8},{1,5},{5,1},{9,13},{13,9},{2,6},{6,2},{1... | collective-permute-start | bytes 221192 | tf_op jit(solution)/shard_map/ppermute | solution.py:306
  12.1 2.3 %collective-permute-start.3 = (f32[16,1152]{1,0:T(8,128)S(1)}, f32[16,1152]{1,0:T(8,128)S(1)}, u32[]{:S(2)}, u32[]{:S(2)}) collective-permute-start(f32[16,1152]{1,0:T(8,128)S(1)} %get-tuple-element.30), channel_id=1, source_target_pairs={{0,0},{4,8},{8,4},{12,12},{1,1},{5,9},{9,5},{13,13},{2,2},{6,10},{... | collective-permute-start | bytes 221192 | tf_op jit(solution)/shard_map/ppermute | solution.py:306
  12.8 15.0 %collective-permute-start.5 = (f32[224,256]{1,0:T(8,128)S(1)}, f32[224,256]{1,0:T(8,128)S(1)}, u32[]{:S(2)}, u32[]{:S(2)}) collective-permute-start(f32[224,256]{1,0:T(8,128)S(1)} %get-tuple-element.31.own_ref), channel_id=1, source_target_pairs={{0,16},{16,0},{1,17},{17,1},{2,18},{18,2},{3,19},{19,3},{4,20},{20... | collective-permute-start | bytes 688136 | tf_op jit(solution)/shard_map/ppermute | solution.py:314
  15.5 13.6 %collective-permute-start.4 = (f32[32,1024]{1,0:T(8,128)S(1)}, f32[32,1024]{1,0:T(8,128)S(1)}, u32[]{:S(2)}, u32[]{:S(2)}) collective-permute-start(f32[32,1024]{1,0:T(8,128)S(1)} %frame.1.own_ref), channel_id=1, source_target_pairs={{0,16},{16,0},{1,17},{17,1},{2,18},{18,2},{3,19},{19,3},{4,20},{20... | collective-permute-start | bytes 393224 | tf_op jit(solution)/shard_map/ppermute | solution.py:314

commit v10 on v8

--- a/solution.py
+++ b/solution.py
@@ -19,7 +19,7 @@
 SPAN = 96
 DEPTH = SPAN + 2 * FRAME
 MID = TH - 2 * FRAME
-LEAD = 96
+LEAD = 64
 REST = MID - LEAD
 REACH = LANE + 2 * FRAME
 BF16 = jnp.bfloat16
@@ -114,7 +114,8 @@
 
 
 def lead_kernel(x, wh, wl, vh, vl, lead, level_ref):
-    total = jnp.sum(jnp.sum(x[0, :8, :], axis=0, keepdims=True), axis=1, keepdims=True)
+    blocks = [x[0, :8, k * LANE : (k + 1) * LANE] for k in range(TW // LANE)]
+    total = jnp.sum(jnp.sum(sum(blocks[1:], blocks[0]), axis=0, keepdims=True), axis=1, keepdims=True)
     level = total * (1.0 / (8 * TW))
     level_ref[...] = jnp.broadcast_to(level, level_ref.shape)
     sums = column_sums(core_windows(x[0, : LEAD + 2 * FRAME, :], level), (wh[...], wl[...]))
@@ -184,7 +185,7 @@
     frame[...] = row_sums(row, sums)
 
 
-COSTS = (25 * 10**8, 10**10, 10**10, 10**10)
+COSTS = (39 * 10**8, 10**10, 10**10, 10**10)
 FAST = pl.BlockSpec(memory_space=pltpu.VMEM)
 SLOW = pl.BlockSpec(memory_space=pltpu.HBM)
 LIMIT = pltpu.CompilerParams(vmem_limit_bytes=16 * 2**20)
@@ -241,18 +242,20 @@
 
         @pl.when(there)
         def _():
-            own = own_ref[...]
-            value[...] = others[0][...] - own if forward else own - others[-1][...]
-            copies = [
-                pltpu.make_async_copy(
-                    value.at[pl.ds(row, tall), pl.ds(column, wide)],
-                    out.at[0, pl.ds(out_row, tall), pl.ds(out_column, wide)],
-                    sem.at[k],
+            copies = []
+            for k, ((row, column), (out_row, out_column), (tall, wide)) in enumerate(places):
+                rows, columns = pl.ds(row, tall), pl.ds(column, wide)
+                own = own_ref[rows, columns]
+                other = others[0 if forward else -1][rows, columns]
+                value[rows, columns] = other - own if forward else own - other
+                copies.append(
+                    pltpu.make_async_copy(
+                        value.at[rows, columns],
+                        out.at[0, pl.ds(out_row, tall), pl.ds(out_column, wide)],
+                        sem.at[k],
+                    )
                 )
-                for k, ((row, column), (out_row, out_column), (tall, wide)) in enumerate(places)
-            ]
-            for copy in copies:
-                copy.start()
+                copies[-1].start()
             for copy in copies:
                 copy.wait()
 

time: 30 us -> 29.9 us (level)
  no operation moved by 1% of the time
where the time goes in v10:
time: 29.9 us; the launch traced here: 29.7 us
  starting transfers between devices  10 us (33%)
  Pallas kernels  9.25 us (31%)
  waiting for transfers between devices  8.89 us (30%)
  between operations  1.46 us (5%)
    ppermute x4, waiting for transfers between devices, other_dies(): return (lax.ppermute(block, 'die', forward + backward),)  8.28 us
    ppermute x4, starting transfers between devices, other_dies(): return (lax.ppermute(block, 'die', forward + backward),)  6.6 us
    pallas_call x4, Pallas kernels, fast_call(): pl.pallas_call(kernel, out_shape=out_shape, in_specs=[FAST] * len(operand...  4.87 us
    pallas_call x4, Pallas kernels, change_call(): pl.pallas_call(functools.partial(change_kernel, places, count, fill), out...  3.97 us
    ppermute x2, starting transfers between devices, swap_rounds(): lax.ppermute(first, axis, pairs)  2.13 us
    ppermute x2, starting transfers between devices, swap_rounds(): lax.ppermute(second, axis, others)  1.32 us
    ppermute x2, waiting for transfers between devices, swap_rounds(): lax.ppermute(first, axis, pairs)  0.61 us
  transfers between devices with their start and end apart: 8, of which 5 were waited for; matrix products, arithmetic and copies ran while one was open for 0% of the time, Pallas kernels for 24%

profile of v10, /device:TPU:0, one launch (start us, length us, event | category | flops | bytes accessed | tf_op | source)
XLA Modules:
  0.0 29.7 jit_solution(1388861438745306062)
XLA Ops:
  0.6 0.0 copy-start.1
  0.6 0.0 copy-start
  1.4 0.0 copy-done.1
  1.4 0.4 %weights.1 = (bf16[256,256]{1,0:T(8,128)(2,1)S(1)}, bf16[256,256]{1,0:T(8,128)(2,1)S(1)}, bf16[96,256]{1,0:T(8,128)(2,1)S(1)}, bf16[96,256]{1,0:T(8,128)(2,1)S(1)}) custom-call(s32[1,1,1,2]{3,2,1,0:T(1,128)S(1)} %copy-done.1, s32[1,1,1]{2,1,0:T(1,128)S(6)} %copy.17.pick_ref), custom_call_target="tpu_custom_call" | custom-call | flops 400000000 | bytes 4096 | tf_op jit(solution)/shard_map/weights/pallas_call | solution.py:209
  1.8 0.1 copy-done
  1.9 1.0 %lead.1 = (f32[64,768]{1,0:T(8,128)S(1)}, f32[8,128]{1,0:T(8,128)S(1)}) custom-call(f32[1,256,1024]{2,1,0:T(8,128)S(1)} %copy-done, bf16[256,256]{1,0:T(8,128)(2,1)S(1)} %get-tuple-element.21.wh, bf16[256,256]{1,0:T(8,128)(2,1)S(1)} %get-tuple-element.22.wl, bf16[96,256]{1,0:T(8,128)(2,1)S(1)} %get-tuple-element.23.vh, bf16[96,256]{1,0:T(8,128)(2,1)S(1)} %get-tuple-element.24.vl), custom_call_target="tpu_custom_call" | custom-call | flops 1000000 | bytes 4096 | tf_op jit(solution)/shard_map/lead/pallas_call | solution.py:222
  2.9 3.0 %collective-permute-start.7 = (f32[64,768]{1,0:T(8,128)S(1)}, f32[64,768]{1,0:T(8,128)S(1)}, u32[]{:S(2)}, u32[]{:S(2)}) collective-permute-start(f32[64,768]{1,0:T(8,128)S(1)} %get-tuple-element.33.own_ref), channel_id=1, source_target_pairs={{0,16},{16,0},{1,17},{17,1},{2,18},{18,2},{3,19},{19,3},{4,20},{20... | collective-permute-start | bytes 589832 | tf_op jit(solution)/shard_map/ppermute | solution.py:313
  5.9 1.7 %rest.1 = (f32[160,768]{1,0:T(8,128)S(1)}, f32[16,256]{1,0:T(8,128)S(1)}, f32[16,256]{1,0:T(8,128)S(1)}) custom-call(f32[1,256,1024]{2,1,0:T(8,128)S(1)} %copy-done, f32[8,128]{1,0:T(8,128)S(1)} %get-tuple-element.25.level_ref, bf16[256,256]{1,0:T(8,128)(2,1)S(1)} %get-tuple-element.21.wh, bf16[256,256]{1,0:T(8,128)(2,1)S(1)} %get-tuple-element.22.wl, ...), custom_call_target="tpu_custom_call" | custom-call | flops 1000000 | bytes 4096 | tf_op jit(solution)/shard_map/rest/pallas_call | solution.py:222
  7.6 0.1 collective-permute-start.6
  7.6 0.1 collective-permute-start
  7.7 0.7 %collective-permute-start.1 = (f32[16,256]{1,0:T(8,128)S(1)}, f32[16,256]{1,0:T(8,128)S(1)}, u32[]{:S(2)}, u32[]{:S(2)}) collective-permute-start(f32[16,256]{1,0:T(8,128)S(1)} %get-tuple-element.27), channel_id=1, source_target_pairs={{0,0},{1,2},{2,1},{3,3},{4,4},{5,6},{6,5},{7,7},{8,8},{9,10},{10,9... | collective-permute-start | bytes 49160 | tf_op jit(solution)/shard_map/ppermute | solution.py:305
  8.4 0.5 %collective-permute-done.first = f32[16,256]{1,0:T(8,128)S(1)} collective-permute-done((f32[16,256]{1,0:T(8,128)S(1)}, f32[16,256]{1,0:T(8,128)S(1)}, u32[]{:S(2)}, u32[]{:S(2)}) %collective-permute-start) | collective-permute-done | bytes 16416 | tf_op jit(solution)/shard_map/ppermute | solution.py:305
  8.9 0.0 collective-permute-done.1.second
  8.9 1.1 %side.1 = (f32[224,256]{1,0:T(8,128)S(1)}, f32[16,1152]{1,0:T(8,128)S(1)}, f32[16,1152]{1,0:T(8,128)S(1)}, f32[256,128]{1,0:T(8,128)S(1)}) custom-call(f32[1,256,1024]{2,1,0:T(8,128)S(1)} %copy-done, f32[8,128]{1,0:T(8,128)S(1)} %get-tuple-element.25.level_ref, f32[16,256]{1,0:T(8,128)S(1)} %collective-permute-done.first, ...), custom_call_target="tpu_custom_call" | custom-call | flops 1000000 | bytes 4096 | tf_op jit(solution)/shard_map/side/pallas_call | solution.py:222
  10.0 2.1 %collective-permute-start.2 = (f32[16,1152]{1,0:T(8,128)S(1)}, f32[16,1152]{1,0:T(8,128)S(1)}, u32[]{:S(2)}, u32[]{:S(2)}) collective-permute-start(f32[16,1152]{1,0:T(8,128)S(1)} %get-tuple-element.29), channel_id=1, source_target_pairs={{0,4},{4,0},{8,12},{12,8},{1,5},{5,1},{9,13},{13,9},{2,6},{6,2},{1... | collective-permute-start | bytes 221192 | tf_op jit(solution)/shard_map/ppermute | solution.py:305
  12.1 0.7 %collective-permute-start.3 = (f32[16,1152]{1,0:T(8,128)S(1)}, f32[16,1152]{1,0:T(8,128)S(1)}, u32[]{:S(2)}, u32[]{:S(2)}) collective-permute-start(f32[16,1152]{1,0:T(8,128)S(1)} %get-tuple-element.30), channel_id=1, source_target_pairs={{0,0},{4,8},{8,4},{12,12},{1,1},{5,9},{9,5},{13,13},{2,2},{6,10},{... | collective-permute-start | bytes 221192 | tf_op jit(solution)/shard_map/ppermute | solution.py:305
  12.7 1.6 %collective-permute-start.5 = (f32[224,256]{1,0:T(8,128)S(1)}, f32[224,256]{1,0:T(8,128)S(1)}, u32[]{:S(2)}, u32[]{:S(2)}) collective-permute-start(f32[224,256]{1,0:T(8,128)S(1)} %get-tuple-element.31.own_ref), channel_id=1, source_target_pairs={{0,16},{16,0},{1,17},{17,1},{2,18},{18,2},{3,19},{19,3},{4,20},{20... | collective-permute-start | bytes 688136 | tf_op jit(solution)/shard_map/ppermute | solution.py:313
  14.3 0.1 collective-permute-done.2.row_first
  14.4 0.0 collective-permute-done.3.row_second
  14.4 1.1 %frame.1.own_ref = f32[32,1024]{1,0:T(8,128)S(1)} custom-call(f32[1,256,1024]{2,1,0:T(8,128)S(1)} %copy-done, f32[8,128]{1,0:T(8,128)S(1)} %get-tuple-element.25.level_ref, f32[256,128]{1,0:T(8,128)S(1)} %get-tuple-element.28.edge, f32[16,1152]{1,0:T(8,128)S(1)} %collective-permute-done.2.row_first, f32[16,1152]{1,0:T(8,128)S(1)} %collective-permute-done.3.row_second, ...), custom_call_target="tpu_custom_call" | custom-call | flops 1000000 | bytes 4096 | tf_op jit(solution)/shard_map/frame/pallas_call | solution.py:222
  15.5 2.0 %collective-permute-start.4 = (f32[32,1024]{1,0:T(8,128)S(1)}, f32[32,1024]{1,0:T(8,128)S(1)}, u32[]{:S(2)}, u32[]{:S(2)}) collective-permute-start(f32[32,1024]{1,0:T(8,128)S(1)} %frame.1.own_ref), channel_id=1, source_target_pairs={{0,16},{16,0},{1,17},{17,1},{2,18},{18,2},{3,19},{19,3},{4,20},{20... | collective-permute-start | bytes 393224 | tf_op jit(solution)/shard_map/ppermute | solution.py:313
  17.5 0.0 collective-permute-done.7.refs_0_
  17.5 1.7 %change.4 = (f32[1,256,1024]{2,1,0:T(8,128)}, f32[1,256,1024]{2,1,0:T(8,128)}) custom-call(f32[64,768]{1,0:T(8,128)S(1)} %get-tuple-element.33.own_ref, f32[64,768]{1,0:T(8,128)S(1)} %collective-permute-done.7.refs_0_), custom_call_target="tpu_custom_call" | custom-call | flops 3900000000 | bytes 4096 | tf_op jit(solution)/shard_map/change/pallas_call | solution.py:277
  19.2 2.9 %collective-permute-done.6.refs_0_ = f32[160,768]{1,0:T(8,128)S(1)} collective-permute-done((f32[160,768]{1,0:T(8,128)S(1)}, f32[160,768]{1,0:T(8,128)S(1)}, u32[]{:S(2)}, u32[]{:S(2)}) %collective-permute-start.6) | collective-permute-done | bytes 491552 | tf_op jit(solution)/shard_map/ppermute | solution.py:313
  22.1 0.8 %change.5 = (f32[1,256,1024]{2,1,0:T(8,128)}, f32[1,256,1024]{2,1,0:T(8,128)}) custom-call(f32[160,768]{1,0:T(8,128)S(1)} %get-tuple-element.32.own_ref, f32[160,768]{1,0:T(8,128)S(1)} %collective-permute-done.6.refs_0_, f32[1,256,1024]{2,1,0:T(8,128)} %get-tuple-element.34.refs_1_, ...), custom_call_target="tpu_custom_call", output_to_operand_aliasing={{0}: (2, {}), {1}: (3, {})} | custom-call | flops 10000000000 | bytes 4096 | tf_op jit(solution)/shard_map/change/pallas_call | solution.py:277
  23.0 4.1 %collective-permute-done.5.refs_0_ = f32[224,256]{1,0:T(8,128)S(1)} collective-permute-done((f32[224,256]{1,0:T(8,128)S(1)}, f32[224,256]{1,0:T(8,128)S(1)}, u32[]{:S(2)}, u32[]{:S(2)}) %collective-permute-start.5) | collective-permute-done | bytes 229408 | tf_op jit(solution)/shard_map/ppermute | solution.py:313
  27.1 0.7 %change.6 = (f32[1,256,1024]{2,1,0:T(8,128)}, f32[1,256,1024]{2,1,0:T(8,128)}) custom-call(f32[224,256]{1,0:T(8,128)S(1)} %get-tuple-element.31.own_ref, f32[224,256]{1,0:T(8,128)S(1)} %collective-permute-done.5.refs_0_, f32[1,256,1024]{2,1,0:T(8,128)} %get-tuple-element.36.refs_1_, ...), custom_call_target="tpu_custom_call", output_to_operand_aliasing={{0}: (2, {}), {1}: (3, {})} | custom-call | flops 10000000000 | bytes 4096 | tf_op jit(solution)/shard_map/change/pallas_call | solution.py:277
  27.8 1.3 %collective-permute-done.4.refs_0_ = f32[32,1024]{1,0:T(8,128)S(1)} collective-permute-done((f32[32,1024]{1,0:T(8,128)S(1)}, f32[32,1024]{1,0:T(8,128)S(1)}, u32[]{:S(2)}, u32[]{:S(2)}) %collective-permute-start.4) | collective-permute-done | bytes 131104 | tf_op jit(solution)/shard_map/ppermute | solution.py:313
  29.1 0.7 %change.7 = (f32[1,256,1024]{2,1,0:T(8,128)}, f32[1,256,1024]{2,1,0:T(8,128)}) custom-call(f32[32,1024]{1,0:T(8,128)S(1)} %frame.1.own_ref, f32[32,1024]{1,0:T(8,128)S(1)} %collective-permute-done.4.refs_0_, f32[1,256,1024]{2,1,0:T(8,128)} %get-tuple-element.38.refs_1_, ...), custom_call_target="tpu_custom_call", output_to_operand_aliasing={{0}: (2, {}), {1}: (3, {})} | custom-call | flops 10000000000 | bytes 4096 | tf_op jit(solution)/shard_map/change/pallas_call | solution.py:277
Async XLA Ops:
  0.6 0.8 %copy-start.1 = (s32[1,1,1,2]{3,2,1,0:T(1,128)S(1)}, s32[1,1,1,2]{3,2,1,0:T(1,128)}, u32[]{:S(2)}) copy-start(s32[1,1,1,2]{3,2,1,0:T(1,128)} %off_ref.1) | copy-start | bytes 28
  0.6 1.2 %copy-start = (f32[1,256,1024]{2,1,0:T(8,128)S(1)}, f32[1,256,1024]{2,1,0:T(8,128)}, u32[]{:S(2)}) copy-start(f32[1,256,1024]{2,1,0:T(8,128)} %x.7) | copy-start | bytes 3145732
  2.9 14.6 %collective-permute-start.7 = (f32[64,768]{1,0:T(8,128)S(1)}, f32[64,768]{1,0:T(8,128)S(1)}, u32[]{:S(2)}, u32[]{:S(2)}) collective-permute-start(f32[64,768]{1,0:T(8,128)S(1)} %get-tuple-element.33.own_ref), channel_id=1, source_target_pairs={{0,16},{16,0},{1,17},{17,1},{2,18},{18,2},{3,19},{19,3},{4,20},{20... | collective-permute-start | bytes 589832 | tf_op jit(solution)/shard_map/ppermute | solution.py:313
  7.6 14.6 %collective-permute-start.6 = (f32[160,768]{1,0:T(8,128)S(1)}, f32[160,768]{1,0:T(8,128)S(1)}, u32[]{:S(2)}, u32[]{:S(2)}) collective-permute-start(f32[160,768]{1,0:T(8,128)S(1)} %get-tuple-element.32.own_ref), channel_id=1, source_target_pairs={{0,16},{16,0},{1,17},{17,1},{2,18},{18,2},{3,19},{19,3},{4,20},{20... | collective-permute-start | bytes 1474568 | tf_op jit(solution)/shard_map/ppermute | solution.py:313
  7.6 1.2 %collective-permute-start = (f32[16,256]{1,0:T(8,128)S(1)}, f32[16,256]{1,0:T(8,128)S(1)}, u32[]{:S(2)}, u32[]{:S(2)}) collective-permute-start(f32[16,256]{1,0:T(8,128)S(1)} %get-tuple-element.26), channel_id=1, source_target_pairs={{0,1},{1,0},{2,3},{3,2},{4,5},{5,4},{6,7},{7,6},{8,9},{9,8},{10,11... | collective-permute-start | bytes 49160 | tf_op jit(solution)/shard_map/ppermute | solution.py:305
  7.7 1.2 %collective-permute-start.1 = (f32[16,256]{1,0:T(8,128)S(1)}, f32[16,256]{1,0:T(8,128)S(1)}, u32[]{:S(2)}, u32[]{:S(2)}) collective-permute-start(f32[16,256]{1,0:T(8,128)S(1)} %get-tuple-element.27), channel_id=1, source_target_pairs={{0,0},{1,2},{2,1},{3,3},{4,4},{5,6},{6,5},{7,7},{8,8},{9,10},{10,9... | collective-permute-start | bytes 49160 | tf_op jit(solution)/shard_map/ppermute | solution.py:305
  10.0 4.4 %collective-permute-start.2 = (f32[16,1152]{1,0:T(8,128)S(1)}, f32[16,1152]{1,0:T(8,128)S(1)}, u32[]{:S(2)}, u32[]{:S(2)}) collective-permute-start(f32[16,1152]{1,0:T(8,128)S(1)} %get-tuple-element.29), channel_id=1, source_target_pairs={{0,4},{4,0},{8,12},{12,8},{1,5},{5,1},{9,13},{13,9},{2,6},{6,2},{1... | collective-permute-start | bytes 221192 | tf_op jit(solution)/shard_map/ppermute | solution.py:305
  12.1 2.3 %collective-permute-start.3 = (f32[16,1152]{1,0:T(8,128)S(1)}, f32[16,1152]{1,0:T(8,128)S(1)}, u32[]{:S(2)}, u32[]{:S(2)}) collective-permute-start(f32[16,1152]{1,0:T(8,128)S(1)} %get-tuple-element.30), channel_id=1, source_target_pairs={{0,0},{4,8},{8,4},{12,12},{1,1},{5,9},{9,5},{13,13},{2,2},{6,10},{... | collective-permute-start | bytes 221192 | tf_op jit(solution)/shard_map/ppermute | solution.py:305
  12.7 14.3 %collective-permute-start.5 = (f32[224,256]{1,0:T(8,128)S(1)}, f32[224,256]{1,0:T(8,128)S(1)}, u32[]{:S(2)}, u32[]{:S(2)}) collective-permute-start(f32[224,256]{1,0:T(8,128)S(1)} %get-tuple-element.31.own_ref), channel_id=1, source_target_pairs={{0,16},{16,0},{1,17},{17,1},{2,18},{18,2},{3,19},{19,3},{4,20},{20... | collective-permute-start | bytes 688136 | tf_op jit(solution)/shard_map/ppermute | solution.py:313
  15.5 13.6 %collective-permute-start.4 = (f32[32,1024]{1,0:T(8,128)S(1)}, f32[32,1024]{1,0:T(8,128)S(1)}, u32[]{:S(2)}, u32[]{:S(2)}) collective-permute-start(f32[32,1024]{1,0:T(8,128)S(1)} %frame.1.own_ref), channel_id=1, source_target_pairs={{0,16},{16,0},{1,17},{17,1},{2,18},{18,2},{3,19},{19,3},{4,20},{20... | collective-permute-start | bytes 393224 | tf_op jit(solution)/shard_map/ppermute | solution.py:313

commit v11 on v10

--- a/solution.py
+++ b/solution.py
@@ -19,7 +19,7 @@
 SPAN = 96
 DEPTH = SPAN + 2 * FRAME
 MID = TH - 2 * FRAME
-LEAD = 64
+LEAD = 48
 REST = MID - LEAD
 REACH = LANE + 2 * FRAME
 BF16 = jnp.bfloat16
@@ -185,7 +185,7 @@
     frame[...] = row_sums(row, sums)
 
 
-COSTS = (39 * 10**8, 10**10, 10**10, 10**10)
+COSTS = (44 * 10**8, 10**10, 10**10, 10**10)
 FAST = pl.BlockSpec(memory_space=pltpu.VMEM)
 SLOW = pl.BlockSpec(memory_space=pltpu.HBM)
 LIMIT = pltpu.CompilerParams(vmem_limit_bytes=16 * 2**20)

time: 29.9 us -> 29.9 us (level)
  no operation moved by 1% of the time
where the time goes in v11:
time: 29.9 us; the launch traced here: 29.7 us
  starting transfers between devices  10.1 us (34%)
  Pallas kernels  9.17 us (31%)
  waiting for transfers between devices  8.91 us (30%)
  between operations  1.46 us (5%)
    ppermute x4, waiting for transfers between devices, other_dies(): return (lax.ppermute(block, 'die', forward + backward),)  8.29 us
    ppermute x4, starting transfers between devices, other_dies(): return (lax.ppermute(block, 'die', forward + backward),)  6.64 us
    pallas_call x4, Pallas kernels, fast_call(): pl.pallas_call(kernel, out_shape=out_shape, in_specs=[FAST] * len(operand...  4.79 us
    pallas_call x4, Pallas kernels, change_call(): pl.pallas_call(functools.partial(change_kernel, places, count, fill), out...  3.97 us
    ppermute x2, starting transfers between devices, swap_rounds(): lax.ppermute(first, axis, pairs)  2.11 us
    ppermute x2, starting transfers between devices, swap_rounds(): lax.ppermute(second, axis, others)  1.32 us
    ppermute x2, waiting for transfers between devices, swap_rounds(): lax.ppermute(first, axis, pairs)  0.61 us
  transfers between devices with their start and end apart: 8, of which 5 were waited for; matrix products, arithmetic and copies ran while one was open for 0% of the time, Pallas kernels for 24%

profile of v11, /device:TPU:0, one launch (start us, length us, event | category | flops | bytes accessed | tf_op | source)
XLA Modules:
  0.0 29.7 jit_solution(17705710969260494889)
XLA Ops:
  0.6 0.0 copy-start.1
  0.6 0.0 copy-start
  1.4 0.0 copy-done.1
  1.4 0.4 %weights.1 = (bf16[256,256]{1,0:T(8,128)(2,1)S(1)}, bf16[256,256]{1,0:T(8,128)(2,1)S(1)}, bf16[96,256]{1,0:T(8,128)(2,1)S(1)}, bf16[96,256]{1,0:T(8,128)(2,1)S(1)}) custom-call(s32[1,1,1,2]{3,2,1,0:T(1,128)S(1)} %copy-done.1, s32[1,1,1]{2,1,0:T(1,128)S(6)} %copy.17.pick_ref), custom_call_target="tpu_custom_call" | custom-call | flops 400000000 | bytes 4096 | tf_op jit(solution)/shard_map/weights/pallas_call | solution.py:209
  1.8 0.1 copy-done
  1.9 0.9 %lead.1 = (f32[48,768]{1,0:T(8,128)S(1)}, f32[8,128]{1,0:T(8,128)S(1)}) custom-call(f32[1,256,1024]{2,1,0:T(8,128)S(1)} %copy-done, bf16[256,256]{1,0:T(8,128)(2,1)S(1)} %get-tuple-element.21.wh, bf16[256,256]{1,0:T(8,128)(2,1)S(1)} %get-tuple-element.22.wl, bf16[96,256]{1,0:T(8,128)(2,1)S(1)} %get-tuple-element.23.vh, bf16[96,256]{1,0:T(8,128)(2,1)S(1)} %get-tuple-element.24.vl), custom_call_target="tpu_custom_call" | custom-call | flops 1000000 | bytes 4096 | tf_op jit(solution)/shard_map/lead/pallas_call | solution.py:222
  2.8 3.0 %collective-permute-start.7 = (f32[48,768]{1,0:T(8,128)S(1)}, f32[48,768]{1,0:T(8,128)S(1)}, u32[]{:S(2)}, u32[]{:S(2)}) collective-permute-start(f32[48,768]{1,0:T(8,128)S(1)} %get-tuple-element.33.own_ref), channel_id=1, source_target_pairs={{0,16},{16,0},{1,17},{17,1},{2,18},{18,2},{3,19},{19,3},{4,20},{20... | collective-permute-start | bytes 442376 | tf_op jit(solution)/shard_map/ppermute | solution.py:313
  5.8 1.7 %rest.1 = (f32[176,768]{1,0:T(8,128)S(1)}, f32[16,256]{1,0:T(8,128)S(1)}, f32[16,256]{1,0:T(8,128)S(1)}) custom-call(f32[1,256,1024]{2,1,0:T(8,128)S(1)} %copy-done, f32[8,128]{1,0:T(8,128)S(1)} %get-tuple-element.25.level_ref, bf16[256,256]{1,0:T(8,128)(2,1)S(1)} %get-tuple-element.21.wh, bf16[256,256]{1,0:T(8,128)(2,1)S(1)} %get-tuple-element.22.wl, ...), custom_call_target="tpu_custom_call" | custom-call | flops 1000000 | bytes 4096 | tf_op jit(solution)/shard_map/rest/pallas_call | solution.py:222
  7.5 0.1 collective-permute-start.6
  7.6 0.1 collective-permute-start
  7.7 0.7 %collective-permute-start.1 = (f32[16,256]{1,0:T(8,128)S(1)}, f32[16,256]{1,0:T(8,128)S(1)}, u32[]{:S(2)}, u32[]{:S(2)}) collective-permute-start(f32[16,256]{1,0:T(8,128)S(1)} %get-tuple-element.27), channel_id=1, source_target_pairs={{0,0},{1,2},{2,1},{3,3},{4,4},{5,6},{6,5},{7,7},{8,8},{9,10},{10,9... | collective-permute-start | bytes 49160 | tf_op jit(solution)/shard_map/ppermute | solution.py:305
  8.3 0.5 %collective-permute-done.first = f32[16,256]{1,0:T(8,128)S(1)} collective-permute-done((f32[16,256]{1,0:T(8,128)S(1)}, f32[16,256]{1,0:T(8,128)S(1)}, u32[]{:S(2)}, u32[]{:S(2)}) %collective-permute-start) | collective-permute-done | bytes 16416 | tf_op jit(solution)/shard_map/ppermute | solution.py:305
  8.8 0.0 collective-permute-done.1.second
  8.8 1.1 %side.1 = (f32[224,256]{1,0:T(8,128)S(1)}, f32[16,1152]{1,0:T(8,128)S(1)}, f32[16,1152]{1,0:T(8,128)S(1)}, f32[256,128]{1,0:T(8,128)S(1)}) custom-call(f32[1,256,1024]{2,1,0:T(8,128)S(1)} %copy-done, f32[8,128]{1,0:T(8,128)S(1)} %get-tuple-element.25.level_ref, f32[16,256]{1,0:T(8,128)S(1)} %collective-permute-done.first, ...), custom_call_target="tpu_custom_call" | custom-call | flops 1000000 | bytes 4096 | tf_op jit(solution)/shard_map/side/pallas_call | solution.py:222
  9.9 2.0 %collective-permute-start.2 = (f32[16,1152]{1,0:T(8,128)S(1)}, f32[16,1152]{1,0:T(8,128)S(1)}, u32[]{:S(2)}, u32[]{:S(2)}) collective-permute-start(f32[16,1152]{1,0:T(8,128)S(1)} %get-tuple-element.29), channel_id=1, source_target_pairs={{0,4},{4,0},{8,12},{12,8},{1,5},{5,1},{9,13},{13,9},{2,6},{6,2},{1... | collective-permute-start | bytes 221192 | tf_op jit(solution)/shard_map/ppermute | solution.py:305
  12.0 0.7 %collective-permute-start.3 = (f32[16,1152]{1,0:T(8,128)S(1)}, f32[16,1152]{1,0:T(8,128)S(1)}, u32[]{:S(2)}, u32[]{:S(2)}) collective-permute-start(f32[16,1152]{1,0:T(8,128)S(1)} %get-tuple-element.30), channel_id=1, source_target_pairs={{0,0},{4,8},{8,4},{12,12},{1,1},{5,9},{9,5},{13,13},{2,2},{6,10},{... | collective-permute-start | bytes 221192 | tf_op jit(solution)/shard_map/ppermute | solution.py:305
  12.6 1.6 %collective-permute-start.5 = (f32[224,256]{1,0:T(8,128)S(1)}, f32[224,256]{1,0:T(8,128)S(1)}, u32[]{:S(2)}, u32[]{:S(2)}) collective-permute-start(f32[224,256]{1,0:T(8,128)S(1)} %get-tuple-element.31.own_ref), channel_id=1, source_target_pairs={{0,16},{16,0},{1,17},{17,1},{2,18},{18,2},{3,19},{19,3},{4,20},{20... | collective-permute-start | bytes 688136 | tf_op jit(solution)/shard_map/ppermute | solution.py:313
  14.2 0.1 collective-permute-done.2.row_first
  14.3 0.0 collective-permute-done.3.row_second
  14.3 1.1 %frame.1.own_ref = f32[32,1024]{1,0:T(8,128)S(1)} custom-call(f32[1,256,1024]{2,1,0:T(8,128)S(1)} %copy-done, f32[8,128]{1,0:T(8,128)S(1)} %get-tuple-element.25.level_ref, f32[256,128]{1,0:T(8,128)S(1)} %get-tuple-element.28.edge, f32[16,1152]{1,0:T(8,128)S(1)} %collective-permute-done.2.row_first, f32[16,1152]{1,0:T(8,128)S(1)} %collective-permute-done.3.row_second, ...), custom_call_target="tpu_custom_call" | custom-call | flops 1000000 | bytes 4096 | tf_op jit(solution)/shard_map/frame/pallas_call | solution.py:222
  15.4 2.0 %collective-permute-start.4 = (f32[32,1024]{1,0:T(8,128)S(1)}, f32[32,1024]{1,0:T(8,128)S(1)}, u32[]{:S(2)}, u32[]{:S(2)}) collective-permute-start(f32[32,1024]{1,0:T(8,128)S(1)} %frame.1.own_ref), channel_id=1, source_target_pairs={{0,16},{16,0},{1,17},{17,1},{2,18},{18,2},{3,19},{19,3},{4,20},{20... | collective-permute-start | bytes 393224 | tf_op jit(solution)/shard_map/ppermute | solution.py:313
  17.4 0.0 collective-permute-done.7.refs_0_
  17.4 1.7 %change.4 = (f32[1,256,1024]{2,1,0:T(8,128)}, f32[1,256,1024]{2,1,0:T(8,128)}) custom-call(f32[48,768]{1,0:T(8,128)S(1)} %get-tuple-element.33.own_ref, f32[48,768]{1,0:T(8,128)S(1)} %collective-permute-done.7.refs_0_), custom_call_target="tpu_custom_call" | custom-call | flops 4400000000 | bytes 4096 | tf_op jit(solution)/shard_map/change/pallas_call | solution.py:277
  19.1 3.6 %collective-permute-done.6.refs_0_ = f32[176,768]{1,0:T(8,128)S(1)} collective-permute-done((f32[176,768]{1,0:T(8,128)S(1)}, f32[176,768]{1,0:T(8,128)S(1)}, u32[]{:S(2)}, u32[]{:S(2)}) %collective-permute-start.6) | collective-permute-done | bytes 540704 | tf_op jit(solution)/shard_map/ppermute | solution.py:313
  22.8 0.9 %change.5 = (f32[1,256,1024]{2,1,0:T(8,128)}, f32[1,256,1024]{2,1,0:T(8,128)}) custom-call(f32[176,768]{1,0:T(8,128)S(1)} %get-tuple-element.32.own_ref, f32[176,768]{1,0:T(8,128)S(1)} %collective-permute-done.6.refs_0_, f32[1,256,1024]{2,1,0:T(8,128)} %get-tuple-element.34.refs_1_, ...), custom_call_target="tpu_custom_call", output_to_operand_aliasing={{0}: (2, {}), {1}: (3, {})} | custom-call | flops 10000000000 | bytes 4096 | tf_op jit(solution)/shard_map/change/pallas_call | solution.py:277
  23.6 4.0 %collective-permute-done.5.refs_0_ = f32[224,256]{1,0:T(8,128)S(1)} collective-permute-done((f32[224,256]{1,0:T(8,128)S(1)}, f32[224,256]{1,0:T(8,128)S(1)}, u32[]{:S(2)}, u32[]{:S(2)}) %collective-permute-start.5) | collective-permute-done | bytes 229408 | tf_op jit(solution)/shard_map/ppermute | solution.py:313
  27.6 0.7 %change.6 = (f32[1,256,1024]{2,1,0:T(8,128)}, f32[1,256,1024]{2,1,0:T(8,128)}) custom-call(f32[224,256]{1,0:T(8,128)S(1)} %get-tuple-element.31.own_ref, f32[224,256]{1,0:T(8,128)S(1)} %collective-permute-done.5.refs_0_, f32[1,256,1024]{2,1,0:T(8,128)} %get-tuple-element.36.refs_1_, ...), custom_call_target="tpu_custom_call", output_to_operand_aliasing={{0}: (2, {}), {1}: (3, {})} | custom-call | flops 10000000000 | bytes 4096 | tf_op jit(solution)/shard_map/change/pallas_call | solution.py:277
  28.3 0.7 %collective-permute-done.4.refs_0_ = f32[32,1024]{1,0:T(8,128)S(1)} collective-permute-done((f32[32,1024]{1,0:T(8,128)S(1)}, f32[32,1024]{1,0:T(8,128)S(1)}, u32[]{:S(2)}, u32[]{:S(2)}) %collective-permute-start.4) | collective-permute-done | bytes 131104 | tf_op jit(solution)/shard_map/ppermute | solution.py:313
  29.0 0.7 %change.7 = (f32[1,256,1024]{2,1,0:T(8,128)}, f32[1,256,1024]{2,1,0:T(8,128)}) custom-call(f32[32,1024]{1,0:T(8,128)S(1)} %frame.1.own_ref, f32[32,1024]{1,0:T(8,128)S(1)} %collective-permute-done.4.refs_0_, f32[1,256,1024]{2,1,0:T(8,128)} %get-tuple-element.38.refs_1_, ...), custom_call_target="tpu_custom_call", output_to_operand_aliasing={{0}: (2, {}), {1}: (3, {})} | custom-call | flops 10000000000 | bytes 4096 | tf_op jit(solution)/shard_map/change/pallas_call | solution.py:277
Async XLA Ops:
  0.6 0.8 %copy-start.1 = (s32[1,1,1,2]{3,2,1,0:T(1,128)S(1)}, s32[1,1,1,2]{3,2,1,0:T(1,128)}, u32[]{:S(2)}) copy-start(s32[1,1,1,2]{3,2,1,0:T(1,128)} %off_ref.1) | copy-start | bytes 28
  0.6 1.2 %copy-start = (f32[1,256,1024]{2,1,0:T(8,128)S(1)}, f32[1,256,1024]{2,1,0:T(8,128)}, u32[]{:S(2)}) copy-start(f32[1,256,1024]{2,1,0:T(8,128)} %x.7) | copy-start | bytes 3145732
  2.8 14.6 %collective-permute-start.7 = (f32[48,768]{1,0:T(8,128)S(1)}, f32[48,768]{1,0:T(8,128)S(1)}, u32[]{:S(2)}, u32[]{:S(2)}) collective-permute-start(f32[48,768]{1,0:T(8,128)S(1)} %get-tuple-element.33.own_ref), channel_id=1, source_target_pairs={{0,16},{16,0},{1,17},{17,1},{2,18},{18,2},{3,19},{19,3},{4,20},{20... | collective-permute-start | bytes 442376 | tf_op jit(solution)/shard_map/ppermute | solution.py:313
  7.5 15.3 %collective-permute-start.6 = (f32[176,768]{1,0:T(8,128)S(1)}, f32[176,768]{1,0:T(8,128)S(1)}, u32[]{:S(2)}, u32[]{:S(2)}) collective-permute-start(f32[176,768]{1,0:T(8,128)S(1)} %get-tuple-element.32.own_ref), channel_id=1, source_target_pairs={{0,16},{16,0},{1,17},{17,1},{2,18},{18,2},{3,19},{19,3},{4,20},{20... | collective-permute-start | bytes 1622024 | tf_op jit(solution)/shard_map/ppermute | solution.py:313
  7.6 1.2 %collective-permute-start = (f32[16,256]{1,0:T(8,128)S(1)}, f32[16,256]{1,0:T(8,128)S(1)}, u32[]{:S(2)}, u32[]{:S(2)}) collective-permute-start(f32[16,256]{1,0:T(8,128)S(1)} %get-tuple-element.26), channel_id=1, source_target_pairs={{0,1},{1,0},{2,3},{3,2},{4,5},{5,4},{6,7},{7,6},{8,9},{9,8},{10,11... | collective-permute-start | bytes 49160 | tf_op jit(solution)/shard_map/ppermute | solution.py:305
  7.7 1.2 %collective-permute-start.1 = (f32[16,256]{1,0:T(8,128)S(1)}, f32[16,256]{1,0:T(8,128)S(1)}, u32[]{:S(2)}, u32[]{:S(2)}) collective-permute-start(f32[16,256]{1,0:T(8,128)S(1)} %get-tuple-element.27), channel_id=1, source_target_pairs={{0,0},{1,2},{2,1},{3,3},{4,4},{5,6},{6,5},{7,7},{8,8},{9,10},{10,9... | collective-permute-start | bytes 49160 | tf_op jit(solution)/shard_map/ppermute | solution.py:305
  9.9 4.4 %collective-permute-start.2 = (f32[16,1152]{1,0:T(8,128)S(1)}, f32[16,1152]{1,0:T(8,128)S(1)}, u32[]{:S(2)}, u32[]{:S(2)}) collective-permute-start(f32[16,1152]{1,0:T(8,128)S(1)} %get-tuple-element.29), channel_id=1, source_target_pairs={{0,4},{4,0},{8,12},{12,8},{1,5},{5,1},{9,13},{13,9},{2,6},{6,2},{1... | collective-permute-start | bytes 221192 | tf_op jit(solution)/shard_map/ppermute | solution.py:305
  12.0 2.3 %collective-permute-start.3 = (f32[16,1152]{1,0:T(8,128)S(1)}, f32[16,1152]{1,0:T(8,128)S(1)}, u32[]{:S(2)}, u32[]{:S(2)}) collective-permute-start(f32[16,1152]{1,0:T(8,128)S(1)} %get-tuple-element.30), channel_id=1, source_target_pairs={{0,0},{4,8},{8,4},{12,12},{1,1},{5,9},{9,5},{13,13},{2,2},{6,10},{... | collective-permute-start | bytes 221192 | tf_op jit(solution)/shard_map/ppermute | solution.py:305
  12.6 15.0 %collective-permute-start.5 = (f32[224,256]{1,0:T(8,128)S(1)}, f32[224,256]{1,0:T(8,128)S(1)}, u32[]{:S(2)}, u32[]{:S(2)}) collective-permute-start(f32[224,256]{1,0:T(8,128)S(1)} %get-tuple-element.31.own_ref), channel_id=1, source_target_pairs={{0,16},{16,0},{1,17},{17,1},{2,18},{18,2},{3,19},{19,3},{4,20},{20... | collective-permute-start | bytes 688136 | tf_op jit(solution)/shard_map/ppermute | solution.py:313
  15.4 13.6 %collective-permute-start.4 = (f32[32,1024]{1,0:T(8,128)S(1)}, f32[32,1024]{1,0:T(8,128)S(1)}, u32[]{:S(2)}, u32[]{:S(2)}) collective-permute-start(f32[32,1024]{1,0:T(8,128)S(1)} %frame.1.own_ref), channel_id=1, source_target_pairs={{0,16},{16,0},{1,17},{17,1},{2,18},{18,2},{3,19},{19,3},{4,20},{20... | collective-permute-start | bytes 393224 | tf_op jit(solution)/shard_map/ppermute | solution.py:313

commit v12 on v11

--- a/solution.py
+++ b/solution.py
@@ -114,8 +114,7 @@
 
 
 def lead_kernel(x, wh, wl, vh, vl, lead, level_ref):
-    blocks = [x[0, :8, k * LANE : (k + 1) * LANE] for k in range(TW // LANE)]
-    total = jnp.sum(jnp.sum(sum(blocks[1:], blocks[0]), axis=0, keepdims=True), axis=1, keepdims=True)
+    total = jnp.sum(jnp.sum(x[0, :8, :], axis=0, keepdims=True), axis=1, keepdims=True)
     level = total * (1.0 / (8 * TW))
     level_ref[...] = jnp.broadcast_to(level, level_ref.shape)
     sums = column_sums(core_windows(x[0, : LEAD + 2 * FRAME, :], level), (wh[...], wl[...]))

time: 29.9 us -> 29.9 us (level)
  no operation moved by 1% of the time
where the time goes in v12:
time: 29.9 us; the launch traced here: 29.7 us
  starting transfers between devices  10.1 us (34%)
  Pallas kernels  9.17 us (31%)
  waiting for transfers between devices  8.91 us (30%)
  between operations  1.46 us (5%)
    ppermute x4, waiting for transfers between devices, other_dies(): return (lax.ppermute(block, 'die', forward + backward),)  8.29 us
    ppermute x4, starting transfers between devices, other_dies(): return (lax.ppermute(block, 'die', forward + backward),)  6.64 us
    pallas_call x4, Pallas kernels, fast_call(): pl.pallas_call(kernel, out_shape=out_shape, in_specs=[FAST] * len(operand...  4.79 us
    pallas_call x4, Pallas kernels, change_call(): pl.pallas_call(functools.partial(change_kernel, places, count, fill), out...  3.97 us
    ppermute x2, starting transfers between devices, swap_rounds(): lax.ppermute(first, axis, pairs)  2.11 us
    ppermute x2, starting transfers between devices, swap_rounds(): lax.ppermute(second, axis, others)  1.32 us
    ppermute x2, waiting for transfers between devices, swap_rounds(): lax.ppermute(first, axis, pairs)  0.61 us
  transfers between devices with their start and end apart: 8, of which 5 were waited for; matrix products, arithmetic and copies ran while one was open for 0% of the time, Pallas kernels for 24%

profile of v12, /device:TPU:0, one launch (start us, length us, event | category | flops | bytes accessed | tf_op | source)
XLA Modules:
  0.0 29.7 jit_solution(4202568195647442869)
XLA Ops:
  0.6 0.0 copy-start.1
  0.6 0.0 copy-start
  1.4 0.0 copy-done.1
  1.4 0.4 %weights.1 = (bf16[256,256]{1,0:T(8,128)(2,1)S(1)}, bf16[256,256]{1,0:T(8,128)(2,1)S(1)}, bf16[96,256]{1,0:T(8,128)(2,1)S(1)}, bf16[96,256]{1,0:T(8,128)(2,1)S(1)}) custom-call(s32[1,1,1,2]{3,2,1,0:T(1,128)S(1)} %copy-done.1, s32[1,1,1]{2,1,0:T(1,128)S(6)} %copy.17.pick_ref), custom_call_target="tpu_custom_call" | custom-call | flops 400000000 | bytes 4096 | tf_op jit(solution)/shard_map/weights/pallas_call | solution.py:208
  1.8 0.1 copy-done
  1.9 0.9 %lead.1 = (f32[48,768]{1,0:T(8,128)S(1)}, f32[8,128]{1,0:T(8,128)S(1)}) custom-call(f32[1,256,1024]{2,1,0:T(8,128)S(1)} %copy-done, bf16[256,256]{1,0:T(8,128)(2,1)S(1)} %get-tuple-element.21.wh, bf16[256,256]{1,0:T(8,128)(2,1)S(1)} %get-tuple-element.22.wl, bf16[96,256]{1,0:T(8,128)(2,1)S(1)} %get-tuple-element.23.vh, bf16[96,256]{1,0:T(8,128)(2,1)S(1)} %get-tuple-element.24.vl), custom_call_target="tpu_custom_call" | custom-call | flops 1000000 | bytes 4096 | tf_op jit(solution)/shard_map/lead/pallas_call | solution.py:221
  2.8 3.0 %collective-permute-start.7 = (f32[48,768]{1,0:T(8,128)S(1)}, f32[48,768]{1,0:T(8,128)S(1)}, u32[]{:S(2)}, u32[]{:S(2)}) collective-permute-start(f32[48,768]{1,0:T(8,128)S(1)} %get-tuple-element.33.own_ref), channel_id=1, source_target_pairs={{0,16},{16,0},{1,17},{17,1},{2,18},{18,2},{3,19},{19,3},{4,20},{20... | collective-permute-start | bytes 442376 | tf_op jit(solution)/shard_map/ppermute | solution.py:312
  5.8 1.7 %rest.1 = (f32[176,768]{1,0:T(8,128)S(1)}, f32[16,256]{1,0:T(8,128)S(1)}, f32[16,256]{1,0:T(8,128)S(1)}) custom-call(f32[1,256,1024]{2,1,0:T(8,128)S(1)} %copy-done, f32[8,128]{1,0:T(8,128)S(1)} %get-tuple-element.25.level_ref, bf16[256,256]{1,0:T(8,128)(2,1)S(1)} %get-tuple-element.21.wh, bf16[256,256]{1,0:T(8,128)(2,1)S(1)} %get-tuple-element.22.wl, ...), custom_call_target="tpu_custom_call" | custom-call | flops 1000000 | bytes 4096 | tf_op jit(solution)/shard_map/rest/pallas_call | solution.py:221
  7.5 0.1 collective-permute-start.6
  7.6 0.1 collective-permute-start
  7.7 0.7 %collective-permute-start.1 = (f32[16,256]{1,0:T(8,128)S(1)}, f32[16,256]{1,0:T(8,128)S(1)}, u32[]{:S(2)}, u32[]{:S(2)}) collective-permute-start(f32[16,256]{1,0:T(8,128)S(1)} %get-tuple-element.27), channel_id=1, source_target_pairs={{0,0},{1,2},{2,1},{3,3},{4,4},{5,6},{6,5},{7,7},{8,8},{9,10},{10,9... | collective-permute-start | bytes 49160 | tf_op jit(solution)/shard_map/ppermute | solution.py:304
  8.3 0.5 %collective-permute-done.first = f32[16,256]{1,0:T(8,128)S(1)} collective-permute-done((f32[16,256]{1,0:T(8,128)S(1)}, f32[16,256]{1,0:T(8,128)S(1)}, u32[]{:S(2)}, u32[]{:S(2)}) %collective-permute-start) | collective-permute-done | bytes 16416 | tf_op jit(solution)/shard_map/ppermute | solution.py:304
  8.8 0.0 collective-permute-done.1.second
  8.8 1.1 %side.1 = (f32[224,256]{1,0:T(8,128)S(1)}, f32[16,1152]{1,0:T(8,128)S(1)}, f32[16,1152]{1,0:T(8,128)S(1)}, f32[256,128]{1,0:T(8,128)S(1)}) custom-call(f32[1,256,1024]{2,1,0:T(8,128)S(1)} %copy-done, f32[8,128]{1,0:T(8,128)S(1)} %get-tuple-element.25.level_ref, f32[16,256]{1,0:T(8,128)S(1)} %collective-permute-done.first, ...), custom_call_target="tpu_custom_call" | custom-call | flops 1000000 | bytes 4096 | tf_op jit(solution)/shard_map/side/pallas_call | solution.py:221
  9.9 2.0 %collective-permute-start.2 = (f32[16,1152]{1,0:T(8,128)S(1)}, f32[16,1152]{1,0:T(8,128)S(1)}, u32[]{:S(2)}, u32[]{:S(2)}) collective-permute-start(f32[16,1152]{1,0:T(8,128)S(1)} %get-tuple-element.29), channel_id=1, source_target_pairs={{0,4},{4,0},{8,12},{12,8},{1,5},{5,1},{9,13},{13,9},{2,6},{6,2},{1... | collective-permute-start | bytes 221192 | tf_op jit(solution)/shard_map/ppermute | solution.py:304
  12.0 0.7 %collective-permute-start.3 = (f32[16,1152]{1,0:T(8,128)S(1)}, f32[16,1152]{1,0:T(8,128)S(1)}, u32[]{:S(2)}, u32[]{:S(2)}) collective-permute-start(f32[16,1152]{1,0:T(8,128)S(1)} %get-tuple-element.30), channel_id=1, source_target_pairs={{0,0},{4,8},{8,4},{12,12},{1,1},{5,9},{9,5},{13,13},{2,2},{6,10},{... | collective-permute-start | bytes 221192 | tf_op jit(solution)/shard_map/ppermute | solution.py:304
  12.6 1.6 %collective-permute-start.5 = (f32[224,256]{1,0:T(8,128)S(1)}, f32[224,256]{1,0:T(8,128)S(1)}, u32[]{:S(2)}, u32[]{:S(2)}) collective-permute-start(f32[224,256]{1,0:T(8,128)S(1)} %get-tuple-element.31.own_ref), channel_id=1, source_target_pairs={{0,16},{16,0},{1,17},{17,1},{2,18},{18,2},{3,19},{19,3},{4,20},{20... | collective-permute-start | bytes 688136 | tf_op jit(solution)/shard_map/ppermute | solution.py:312
  14.2 0.1 collective-permute-done.2.row_first
  14.3 0.0 collective-permute-done.3.row_second
  14.3 1.1 %frame.1.own_ref = f32[32,1024]{1,0:T(8,128)S(1)} custom-call(f32[1,256,1024]{2,1,0:T(8,128)S(1)} %copy-done, f32[8,128]{1,0:T(8,128)S(1)} %get-tuple-element.25.level_ref, f32[256,128]{1,0:T(8,128)S(1)} %get-tuple-element.28.edge, f32[16,1152]{1,0:T(8,128)S(1)} %collective-permute-done.2.row_first, f32[16,1152]{1,0:T(8,128)S(1)} %collective-permute-done.3.row_second, ...), custom_call_target="tpu_custom_call" | custom-call | flops 1000000 | bytes 4096 | tf_op jit(solution)/shard_map/frame/pallas_call | solution.py:221
  15.4 2.0 %collective-permute-start.4 = (f32[32,1024]{1,0:T(8,128)S(1)}, f32[32,1024]{1,0:T(8,128)S(1)}, u32[]{:S(2)}, u32[]{:S(2)}) collective-permute-start(f32[32,1024]{1,0:T(8,128)S(1)} %frame.1.own_ref), channel_id=1, source_target_pairs={{0,16},{16,0},{1,17},{17,1},{2,18},{18,2},{3,19},{19,3},{4,20},{20... | collective-permute-start | bytes 393224 | tf_op jit(solution)/shard_map/ppermute | solution.py:312
  17.4 0.0 collective-permute-done.7.refs_0_
  17.4 1.7 %change.4 = (f32[1,256,1024]{2,1,0:T(8,128)}, f32[1,256,1024]{2,1,0:T(8,128)}) custom-call(f32[48,768]{1,0:T(8,128)S(1)} %get-tuple-element.33.own_ref, f32[48,768]{1,0:T(8,128)S(1)} %collective-permute-done.7.refs_0_), custom_call_target="tpu_custom_call" | custom-call | flops 4400000000 | bytes 4096 | tf_op jit(solution)/shard_map/change/pallas_call | solution.py:276
  19.1 3.6 %collective-permute-done.6.refs_0_ = f32[176,768]{1,0:T(8,128)S(1)} collective-permute-done((f32[176,768]{1,0:T(8,128)S(1)}, f32[176,768]{1,0:T(8,128)S(1)}, u32[]{:S(2)}, u32[]{:S(2)}) %collective-permute-start.6) | collective-permute-done | bytes 540704 | tf_op jit(solution)/shard_map/ppermute | solution.py:312
  22.8 0.9 %change.5 = (f32[1,256,1024]{2,1,0:T(8,128)}, f32[1,256,1024]{2,1,0:T(8,128)}) custom-call(f32[176,768]{1,0:T(8,128)S(1)} %get-tuple-element.32.own_ref, f32[176,768]{1,0:T(8,128)S(1)} %collective-permute-done.6.refs_0_, f32[1,256,1024]{2,1,0:T(8,128)} %get-tuple-element.34.refs_1_, ...), custom_call_target="tpu_custom_call", output_to_operand_aliasing={{0}: (2, {}), {1}: (3, {})} | custom-call | flops 10000000000 | bytes 4096 | tf_op jit(solution)/shard_map/change/pallas_call | solution.py:276
  23.6 4.0 %collective-permute-done.5.refs_0_ = f32[224,256]{1,0:T(8,128)S(1)} collective-permute-done((f32[224,256]{1,0:T(8,128)S(1)}, f32[224,256]{1,0:T(8,128)S(1)}, u32[]{:S(2)}, u32[]{:S(2)}) %collective-permute-start.5) | collective-permute-done | bytes 229408 | tf_op jit(solution)/shard_map/ppermute | solution.py:312
  27.6 0.7 %change.6 = (f32[1,256,1024]{2,1,0:T(8,128)}, f32[1,256,1024]{2,1,0:T(8,128)}) custom-call(f32[224,256]{1,0:T(8,128)S(1)} %get-tuple-element.31.own_ref, f32[224,256]{1,0:T(8,128)S(1)} %collective-permute-done.5.refs_0_, f32[1,256,1024]{2,1,0:T(8,128)} %get-tuple-element.36.refs_1_, ...), custom_call_target="tpu_custom_call", output_to_operand_aliasing={{0}: (2, {}), {1}: (3, {})} | custom-call | flops 10000000000 | bytes 4096 | tf_op jit(solution)/shard_map/change/pallas_call | solution.py:276
  28.3 0.7 %collective-permute-done.4.refs_0_ = f32[32,1024]{1,0:T(8,128)S(1)} collective-permute-done((f32[32,1024]{1,0:T(8,128)S(1)}, f32[32,1024]{1,0:T(8,128)S(1)}, u32[]{:S(2)}, u32[]{:S(2)}) %collective-permute-start.4) | collective-permute-done | bytes 131104 | tf_op jit(solution)/shard_map/ppermute | solution.py:312
  29.0 0.7 %change.7 = (f32[1,256,1024]{2,1,0:T(8,128)}, f32[1,256,1024]{2,1,0:T(8,128)}) custom-call(f32[32,1024]{1,0:T(8,128)S(1)} %frame.1.own_ref, f32[32,1024]{1,0:T(8,128)S(1)} %collective-permute-done.4.refs_0_, f32[1,256,1024]{2,1,0:T(8,128)} %get-tuple-element.38.refs_1_, ...), custom_call_target="tpu_custom_call", output_to_operand_aliasing={{0}: (2, {}), {1}: (3, {})} | custom-call | flops 10000000000 | bytes 4096 | tf_op jit(solution)/shard_map/change/pallas_call | solution.py:276
Async XLA Ops:
  0.6 0.8 %copy-start.1 = (s32[1,1,1,2]{3,2,1,0:T(1,128)S(1)}, s32[1,1,1,2]{3,2,1,0:T(1,128)}, u32[]{:S(2)}) copy-start(s32[1,1,1,2]{3,2,1,0:T(1,128)} %off_ref.1) | copy-start | bytes 28
  0.6 1.2 %copy-start = (f32[1,256,1024]{2,1,0:T(8,128)S(1)}, f32[1,256,1024]{2,1,0:T(8,128)}, u32[]{:S(2)}) copy-start(f32[1,256,1024]{2,1,0:T(8,128)} %x.7) | copy-start | bytes 3145732
  2.8 14.6 %collective-permute-start.7 = (f32[48,768]{1,0:T(8,128)S(1)}, f32[48,768]{1,0:T(8,128)S(1)}, u32[]{:S(2)}, u32[]{:S(2)}) collective-permute-start(f32[48,768]{1,0:T(8,128)S(1)} %get-tuple-element.33.own_ref), channel_id=1, source_target_pairs={{0,16},{16,0},{1,17},{17,1},{2,18},{18,2},{3,19},{19,3},{4,20},{20... | collective-permute-start | bytes 442376 | tf_op jit(solution)/shard_map/ppermute | solution.py:312
  7.5 15.3 %collective-permute-start.6 = (f32[176,768]{1,0:T(8,128)S(1)}, f32[176,768]{1,0:T(8,128)S(1)}, u32[]{:S(2)}, u32[]{:S(2)}) collective-permute-start(f32[176,768]{1,0:T(8,128)S(1)} %get-tuple-element.32.own_ref), channel_id=1, source_target_pairs={{0,16},{16,0},{1,17},{17,1},{2,18},{18,2},{3,19},{19,3},{4,20},{20... | collective-permute-start | bytes 1622024 | tf_op jit(solution)/shard_map/ppermute | solution.py:312
  7.6 1.2 %collective-permute-start = (f32[16,256]{1,0:T(8,128)S(1)}, f32[16,256]{1,0:T(8,128)S(1)}, u32[]{:S(2)}, u32[]{:S(2)}) collective-permute-start(f32[16,256]{1,0:T(8,128)S(1)} %get-tuple-element.26), channel_id=1, source_target_pairs={{0,1},{1,0},{2,3},{3,2},{4,5},{5,4},{6,7},{7,6},{8,9},{9,8},{10,11... | collective-permute-start | bytes 49160 | tf_op jit(solution)/shard_map/ppermute | solution.py:304
  7.7 1.2 %collective-permute-start.1 = (f32[16,256]{1,0:T(8,128)S(1)}, f32[16,256]{1,0:T(8,128)S(1)}, u32[]{:S(2)}, u32[]{:S(2)}) collective-permute-start(f32[16,256]{1,0:T(8,128)S(1)} %get-tuple-element.27), channel_id=1, source_target_pairs={{0,0},{1,2},{2,1},{3,3},{4,4},{5,6},{6,5},{7,7},{8,8},{9,10},{10,9... | collective-permute-start | bytes 49160 | tf_op jit(solution)/shard_map/ppermute | solution.py:304
  9.9 4.4 %collective-permute-start.2 = (f32[16,1152]{1,0:T(8,128)S(1)}, f32[16,1152]{1,0:T(8,128)S(1)}, u32[]{:S(2)}, u32[]{:S(2)}) collective-permute-start(f32[16,1152]{1,0:T(8,128)S(1)} %get-tuple-element.29), channel_id=1, source_target_pairs={{0,4},{4,0},{8,12},{12,8},{1,5},{5,1},{9,13},{13,9},{2,6},{6,2},{1... | collective-permute-start | bytes 221192 | tf_op jit(solution)/shard_map/ppermute | solution.py:304
  12.0 2.3 %collective-permute-start.3 = (f32[16,1152]{1,0:T(8,128)S(1)}, f32[16,1152]{1,0:T(8,128)S(1)}, u32[]{:S(2)}, u32[]{:S(2)}) collective-permute-start(f32[16,1152]{1,0:T(8,128)S(1)} %get-tuple-element.30), channel_id=1, source_target_pairs={{0,0},{4,8},{8,4},{12,12},{1,1},{5,9},{9,5},{13,13},{2,2},{6,10},{... | collective-permute-start | bytes 221192 | tf_op jit(solution)/shard_map/ppermute | solution.py:304
  12.6 15.0 %collective-permute-start.5 = (f32[224,256]{1,0:T(8,128)S(1)}, f32[224,256]{1,0:T(8,128)S(1)}, u32[]{:S(2)}, u32[]{:S(2)}) collective-permute-start(f32[224,256]{1,0:T(8,128)S(1)} %get-tuple-element.31.own_ref), channel_id=1, source_target_pairs={{0,16},{16,0},{1,17},{17,1},{2,18},{18,2},{3,19},{19,3},{4,20},{20... | collective-permute-start | bytes 688136 | tf_op jit(solution)/shard_map/ppermute | solution.py:312
  15.4 13.6 %collective-permute-start.4 = (f32[32,1024]{1,0:T(8,128)S(1)}, f32[32,1024]{1,0:T(8,128)S(1)}, u32[]{:S(2)}, u32[]{:S(2)}) collective-permute-start(f32[32,1024]{1,0:T(8,128)S(1)} %frame.1.own_ref), channel_id=1, source_target_pairs={{0,16},{16,0},{1,17},{17,1},{2,18},{18,2},{3,19},{19,3},{4,20},{20... | collective-permute-start | bytes 393224 | tf_op jit(solution)/shard_map/ppermute | solution.py:312
